TPU v7x, 32 devices: a whole 2x2x4 slice. The times are simulated.
32 devices in a mesh: dp: 4 (over x, core), seq: 8 (over z, y).
Axes of the slice: x: 2, y: 2, z: 4, core: 2. Of those that a mesh axis runs over, the one named last changes fastest.
Arguments:
- byte_embed: bfloat16 [16384, 1024], P(('dp', 'seq')), parts along dimension 0, may hold values from -6 to 6
- conv_taps: float32 [4, 1024], replicated, may hold values from -3 to 3
- norm_gain: float32 [4096], replicated, may hold values from 0.25 to 1.75
- w_qdown: bfloat16 [4096, 128], replicated
- w_qup: bfloat16 [128, 4096], replicated
- w_key: bfloat16 [4096, 256], replicated
- w_value: bfloat16 [4096, 256], replicated, may hold values from -0.09375 to 0.09375
- doc_lengths: int32 [64], P('dp'), parts along dimension 0, may hold values from 1 to 256, 1024 in all
- panel_dest: int32 [1024], P(('dp', 'seq')), parts along dimension 0, may hold values from 0 to 7, as said below
Outputs:
- rebalanced: bfloat16 [4096, 4096], P(('dp', 'seq')), parts along dimension 0
There are 4 independent parts, one for each index of `dp`. A program takes and returns all parts, laid end to end along the dimension named above; an argument that names none is the same for every part. Nothing has to cross between parts.
Inputs may be any that keep to these rules, and one draw needn't show every extreme that they name: `doc_lengths`: the documents sum to 1024 shortened tokens and the longest has exactly 256. `panel_dest`: every index of seq receives exactly 32 panels; no index of seq sends more than 8 panels to one index of seq, and some pair reaches 8.
All inputs are finite; a program needn't handle non-finite values.
Results may differ from a plain program's by a relative error of at most 0.015.
Values may be sent and summed in bfloat16 or wider, within the bound.
No kernel may reach another device: no remote copies, remote signals or barrier semaphores. Data moves between devices by JAX's collectives and lax.ppermute only.
A program may use at most 64 MiB of HBM per device.

v0:
```python
import math

import jax
import jax.numpy as jnp
from jax import lax
from jax.sharding import PartitionSpec as P

H = 32
SHORTEN = 4
KCONV = 4
PANEL = 4


def from_behind(array, axis, by):
    size = lax.axis_size(axis)
    pairs = [(i, i + by) for i in range(size) if 0 <= i + by < size]
    return lax.ppermute(array, axis, pairs)


def doc_index(positions, doc_ends):
    return jnp.sum((positions[:, None] >= doc_ends[None, :]).astype(jnp.int32), axis=1)


def project(rows, weights):
    return jnp.einsum("td,sdf->stf", rows, weights, preferred_element_type=jnp.float32).astype(
        jnp.bfloat16
    )


def per_device(
    byte_embed, conv_taps, norm_gain, w_qdown, w_qup, w_key, w_value, doc_lengths, panel_dest
):
    n_seq = lax.axis_size("seq")
    my_index = lax.axis_index("seq")
    n_bytes, byte_dim = byte_embed.shape
    tok_rows = n_bytes // SHORTEN
    width = SHORTEN * byte_dim
    head_dim = width // H
    kv_heads = w_key.shape[1] // head_dim
    groups = H // kv_heads
    doc_ends = jnp.cumsum(doc_lengths)
    query_pos = my_index * tok_rows + jnp.arange(tok_rows, dtype=jnp.int32)
    query_doc = doc_index(query_pos, doc_ends)
    rim_rows = from_behind(byte_embed[n_bytes - (KCONV - 1) :], "seq", 1)
    extended = jnp.concatenate([rim_rows, byte_embed], axis=0)
    byte_doc = jnp.repeat(query_doc, SHORTEN, total_repeat_length=n_bytes)
    before_doc = doc_index(jnp.reshape(my_index * tok_rows - 1, (1,)), doc_ends)
    ext_doc = jnp.concatenate([jnp.broadcast_to(before_doc, (KCONV - 1,)), byte_doc])
    conv_sum = jnp.zeros((n_bytes, byte_dim), jnp.float32)
    for tap_index in range(KCONV):
        begin_at = KCONV - 1 - tap_index
        window = extended[begin_at : begin_at + n_bytes]
        same_doc = ext_doc[begin_at : begin_at + n_bytes] == byte_doc
        conv_sum = conv_sum + jnp.where(
            same_doc[:, None], window.astype(jnp.float32) * conv_taps[tap_index][None, :], 0.0
        )
    shortened = conv_sum.reshape(tok_rows, width).astype(jnp.bfloat16)
    short_wide = shortened.astype(jnp.float32)
    mean_sq = jnp.mean(short_wide * short_wide, axis=1, keepdims=True)
    normed = (short_wide * lax.rsqrt(mean_sq + 1e-06) * norm_gain[None, :]).astype(jnp.bfloat16)
    latent = jnp.dot(normed, w_qdown, preferred_element_type=jnp.float32).astype(jnp.bfloat16)
    query = jnp.dot(latent, w_qup, preferred_element_type=jnp.float32).astype(jnp.bfloat16)
    query = query.reshape(tok_rows, kv_heads, groups, head_dim)
    kv_weights = jnp.stack([w_key, w_value])
    own_kv = project(normed, kv_weights)
    current = own_kv
    received = []
    for cycle_step in range(2):
        current = from_behind(current, "seq", 1)
        received.append(current)
    keys_values = jnp.concatenate([received[1], received[0], own_kv], axis=1)
    keys_values = keys_values.reshape(2, 3 * tok_rows, kv_heads, head_dim)
    key_pos = (my_index - 2) * tok_rows + jnp.arange(3 * tok_rows, dtype=jnp.int32)
    key_doc = doc_index(key_pos, doc_ends)
    allowed = (
        (key_pos[None, :] <= query_pos[:, None])
        & (key_pos[None, :] >= 0)
        & (key_doc[None, :] == query_doc[:, None])
    )
    score_scale = 1.0 / math.sqrt(head_dim)

    def attend(kv_index):
        query_grp = lax.dynamic_index_in_dim(query, kv_index, 1, keepdims=False)
        key_grp = lax.dynamic_index_in_dim(keys_values[0], kv_index, 1, keepdims=False)
        value_grp = lax.dynamic_index_in_dim(keys_values[1], kv_index, 1, keepdims=False)
        scores = (
            jnp.einsum("qge,ke->gqk", query_grp, key_grp, preferred_element_type=jnp.float32)
            * score_scale
        )
        scores = jnp.where(allowed[None], scores, -1e30)
        row_max = jnp.max(scores, axis=2, keepdims=True)
        exp_scores = jnp.exp(scores - row_max)
        attn_probs = (exp_scores / jnp.sum(exp_scores, axis=2, keepdims=True)).astype(jnp.bfloat16)
        return jnp.einsum("gqk,ke->qge", attn_probs, value_grp, preferred_element_type=jnp.float32)

    grouped = lax.map(attend, jnp.arange(kv_heads, dtype=jnp.int32))
    attended = jnp.moveaxis(grouped, 0, 1).reshape(tok_rows, width)
    layer_out = (short_wide + attended).astype(jnp.bfloat16)
    pan_count = tok_rows // PANEL
    most_slots = (2 * pan_count + n_seq - 1) // n_seq
    panel_ids = jnp.arange(pan_count, dtype=jnp.int32)
    same_dest = (panel_dest[:, None] == panel_dest[None, :]) & (
        panel_ids[:, None] < panel_ids[None, :]
    )
    slot_rank = jnp.sum(same_dest.astype(jnp.int32), axis=0)
    send_slot = panel_dest * most_slots + slot_rank
    slot_ids = jnp.arange(n_seq * most_slots, dtype=jnp.int32)
    select = (slot_ids[:, None] == send_slot[None, :]).astype(jnp.bfloat16)
    panels = layer_out.reshape(pan_count, PANEL * width)
    send_buffer = jnp.dot(select, panels, preferred_element_type=jnp.float32).astype(jnp.bfloat16)
    send_buffer = send_buffer.reshape(n_seq, most_slots * PANEL, width)
    dest_ids = jnp.arange(n_seq, dtype=jnp.int32)
    send_counts = jnp.sum(
        (panel_dest[None, :] == dest_ids[:, None]).astype(jnp.int32), axis=1, keepdims=True
    )
    recv_buffer, recv_counts = (
        lax.all_to_all(send_buffer, "seq", split_axis=0, concat_axis=0, tiled=True),
        lax.all_to_all(send_counts, "seq", split_axis=0, concat_axis=0, tiled=True),
    )
    from_counts = recv_counts[:, 0]
    from_offset = jnp.cumsum(from_counts) - from_counts
    slot_index = jnp.arange(most_slots, dtype=jnp.int32)
    target_row = jnp.where(
        slot_index[None, :] < from_counts[:, None], from_offset[:, None] + slot_index[None, :], -1
    )
    gather_pick = (panel_ids[:, None] == target_row.reshape(1, n_seq * most_slots)).astype(
        jnp.bfloat16
    )
    placed = jnp.dot(
        gather_pick,
        recv_buffer.reshape(n_seq * most_slots, PANEL * width),
        preferred_element_type=jnp.float32,
    )
    return placed.astype(jnp.bfloat16).reshape(tok_rows, width)


def solution(mesh):
    in_specs = (P(("dp", "seq"), None), P(), P(), P(), P(), P(), P(), P("dp"), P(("dp", "seq")))
    out_specs = P(("dp", "seq"), None)
    return jax.shard_map(
        per_device, mesh=mesh, in_specs=in_specs, out_specs=out_specs, check_vma=False
    )
```

profile of v0, /device:TPU:0, one launch (start us, length us, event | category | flops | bytes accessed | tf_op | source)
XLA Modules:
  0.0 132.9 jit_solution(17280850036278746915)
XLA Ops:
  0.0 0.8 slice.57
  0.8 4.9 %collective-permute-start = (bf16[3,1024]{1,0:T(4,128)(2,1)S(1)}, bf16[3,1024]{1,0:T(4,128)(2,1)S(1)}, u32[]{:S(2)}, u32[]{:S(2)}) collective-permute-start(bf16[3,1024]{1,0:T(4,128)(2,1)S(1)} %slice.57), channel_id=1, source_target_pairs={{0,1},{1,2},{2,3},{3,4},{4,5},{5,6},{6,7},{8,9},{9,10},{10,11},{11... | collective-permute-start | bytes 18440 | tf_op jit(solution)/shard_map/ppermute | solution.py:17
  5.7 0.8 convert_reduce_fusion.4
  6.5 0.7 copy.37
  7.2 4.9 %all-to-all-start = ((s32[8,1,1]{2,1,0:T(1,128)}), s32[8,1,1]{2,1,0:T(1,128)S(1)}, u32[]{:S(2)}, u32[]{:S(2)}) async-start(s32[8,1,1]{2,1,0:T(1,128)} %copy.37), calls=%async_computation | async-start | bytes 8192 | tf_op jit(solution)/shard_map/all_to_all | solution.py:118
  12.0 0.8 convert_reduce_fusion.1
  12.9 0.7 copy.38
  13.6 0.8 add_add_fusion.1
  14.4 0.6 convert_reduce_fusion.2
  15.1 3.3 %gather_fusion = s32[512]{0:T(512)S(1)} fusion(s32[128]{0:T(128)S(1)} %convert_reduce_fusion.3, s32[1024]{0:T(1024)S(1)} %pad_clamp_fusion), kind=kCustom, calls=%fused_computation | custom fusion | bytes 6144 | tf_op jit(solution)/shard_map/jit(_take)/gather | solution.py:46
  18.6 0.5 multiply_add_fusion
  19.2 0.7 fusion.37
  19.9 4.8 %multiply_reduce_fusion = (f32[512]{0:T(512)S(1)}, f32[512,1024]{1,0:T(8,128)S(1)}) fusion(f32[1024]{0:T(1024)S(1)} %bitcast.89, bf16[512,1024]{1,0:T(8,128)(2,1)} %param.13, bf16[3,1024]{1,0:T(4,128)(2,1)S(1)} %collective-permute-done, pred[512]{0:T(512)(128)(4,1)S(1)} %get-tuple-element.163, f32[1024]{0:T(1024)S(1)} %bitcast.90, ...), kind=kLoop, calls=%fused_computation.34 | loop fusion | flops 14155264 | bytes 3171840 | tf_op jit(solution)/shard_map/reduce_sum | solution.py:59
  24.7 2.0 %reshape.253 = f32[128,4096]{1,0:T(8,128)} reshape(f32[512,1024]{1,0:T(8,128)S(1)} %get-tuple-element.150) | data formatting | bytes 4194304 | tf_op jit(solution)/shard_map/convert_element_type | solution.py:58
  26.7 0.1 reduce_sum.75
  26.8 0.1 reduce_sum.76
  27.0 0.5 copy-done.9
  27.5 3.6 %fusion.27 = bf16[2,128,256]{2,1,0:T(8,128)(2,1)S(1)} fusion(bf16[1,4096,256]{2,1,0:T(8,128)(2,1)} %bitcast.97, bf16[1,4096,256]{2,1,0:T(8,128)(2,1)} %bitcast.98, f32[128,4096]{1,0:T(8,128)} %reshape.253, f32[4096]{0:T(1024)S(1)} %copy-done.2, f32[128]{0:T(128)S(1)} %add_rsqrt_fusion), kind=kOutput, calls=%fused_computation.40 | convolution fusion | flops 546897920 | bytes 6439424 | tf_op jit(solution)/shard_map/td,sdf->stf/dot_general | solution.py:25
  31.1 3.9 %collective-permute-start.1 = (bf16[2,128,256]{2,1,0:T(8,128)(2,1)S(1)}, bf16[2,128,256]{2,1,0:T(8,128)(2,1)S(1)}, u32[]{:S(2)}, u32[]{:S(2)}) collective-permute-start(bf16[2,128,256]{2,1,0:T(8,128)(2,1)S(1)} %fusion.27), channel_id=1, source_target_pairs={{0,1},{1,2},{2,3},{3,4},{4,5},{5,6},{6,7},{8,9},{9,10},{10,11},{11... | collective-permute-start | bytes 393224 | tf_op jit(solution)/shard_map/ppermute | solution.py:17
  35.1 0.6 broadcast_compare_fusion
  35.7 0.1 convert_reduce_fusion
  35.7 1.8 %collective-permute-done.1 = bf16[2,128,256]{2,1,0:T(8,128)(2,1)S(1)} collective-permute-done((bf16[2,128,256]{2,1,0:T(8,128)(2,1)S(1)}, bf16[2,128,256]{2,1,0:T(8,128)(2,1)S(1)}, u32[]{:S(2)}, u32[]{:S(2)}) %collective-permute-start.1) | collective-permute-done | bytes 131104 | tf_op jit(solution)/shard_map/ppermute | solution.py:17
  37.5 4.3 %collective-permute-start.2 = (bf16[2,128,256]{2,1,0:T(8,128)(2,1)S(1)}, bf16[2,128,256]{2,1,0:T(8,128)(2,1)S(1)}, u32[]{:S(2)}, u32[]{:S(2)}) collective-permute-start(bf16[2,128,256]{2,1,0:T(8,128)(2,1)S(1)} %collective-permute-done.1), channel_id=1, source_target_pairs={{0,1},{1,2},{2,3},{3,4},{4,5},{5,6},{6,7},{8,9},{9,10},{10,11},{11... | collective-permute-start | bytes 393224 | tf_op jit(solution)/shard_map/ppermute | solution.py:17
  41.9 3.7 %fusion.23 = bf16[16,8,32,128]{3,1,2,0:T(8,128)(2,1)} fusion(bf16[128,4096]{1,0:T(8,128)(2,1)S(1)} %copy-done, bf16[4096,128]{1,0:T(8,128)(2,1)} %param.16, f32[128,4096]{1,0:T(8,128)} %reshape.253, f32[4096]{0:T(1024)} %param.15, f32[128]{0:T(128)} %copy-done.9), kind=kOutput, calls=%fused_computation.38 | convolution fusion | flops 270548992 | bytes 5259776 | tf_op jit(solution)/shard_map/dot_general | solution.py:62
  45.6 1.6 %reshape.252 = f32[32,16384]{1,0:T(8,128)} reshape(f32[512,1024]{1,0:T(8,128)S(1)} %get-tuple-element.150) | data formatting | bytes 4194304 | tf_op jit(solution)/shard_map/convert_element_type | solution.py:58
  47.2 1.5 %copy.45 = bf16[16,8,32,128]{3,2,1,0:T(8,128)(2,1)S(1)} copy(bf16[16,8,32,128]{3,1,2,0:T(8,128)(2,1)} %fusion.23) | data formatting | bytes 2097152
  48.8 11.7 %while.12 = (s32[]{:T(128)}, f32[2,128,16,128]{1,3,2,0:T(8,128)}, bf16[2,384,2,128]{3,1,2,0:T(8,128)(2,1)S(1)}, s32[2]{0:T(128)S(1)}, bf16[128,2,16,128]{3,2,1,0...) while((s32[]{:T(128)}, f32[2,128,16,128]{1,3,2,0:T(8,128)}, ...), condition=%wide.region_12.13_spmd.clone, body=%wide.region_9.12_spmd.clone.sunk | while | flops 409141632 | bytes 16307255 | solution.py:96
  48.8 0.6 dynamic_slice.35
  51.4 0.6 fusion.57
  52.0 0.2 compare_and_fusion.2
  52.2 1.0 fusion.58
  53.2 1.5 %fusion.59 = f32[2,128,16,128]{1,3,2,0:T(8,128)} fusion(f32[2,128,16,128]{1,3,2,0:T(8,128)} %get-tuple-element.247, s32[]{:T(128)} %get-tuple-element.246, f32[16,128,384]{1,2,0:T(8,128)S(1)} %get-tuple-element.230, f32[16,128]{1,0:T(8,128)S(1)} %get-tuple-element.231, bf16[1,384,2,128]{3,1,2,0:T(8,128)(2,1)S(1)} %get-tuple-element.232, ...), kind=kOutput, calls=%fused_computation.12.clone.1 | convolution fusion | flops 202899456 | bytes 4301316 | tf_op jit(solution)/shard_map/while/body/eval_jaxpr/gqk,ke->qge/dot_general | solution.py:94
  54.6 0.6 dynamic_slice.35
  57.3 0.6 fusion.57
  57.8 0.2 compare_and_fusion.2
  58.1 1.0 fusion.58
  59.0 1.5 %fusion.59 = f32[2,128,16,128]{1,3,2,0:T(8,128)} fusion(f32[2,128,16,128]{1,3,2,0:T(8,128)} %get-tuple-element.247, s32[]{:T(128)} %get-tuple-element.246, f32[16,128,384]{1,2,0:T(8,128)S(1)} %get-tuple-element.230, f32[16,128]{1,0:T(8,128)S(1)} %get-tuple-element.231, bf16[1,384,2,128]{3,1,2,0:T(8,128)(2,1)S(1)} %get-tuple-element.232, ...), kind=kOutput, calls=%fused_computation.12.clone.1 | convolution fusion | flops 202899456 | bytes 4301316 | tf_op jit(solution)/shard_map/while/body/eval_jaxpr/gqk,ke->qge/dot_general | solution.py:94
  60.5 3.1 %copy.41 = f32[128,2,16,128]{3,2,1,0:T(8,128)} copy(f32[128,2,16,128]{0,3,2,1:T(8,128)} %bitcast.16) | data formatting | bytes 4194304 | tf_op jit(solution)/shard_map/transpose | solution.py:97
  63.6 2.9 %reshape.248 = f32[32,16384]{1,0:T(8,128)} reshape(f32[128,2,16,128]{3,2,1,0:T(8,128)} %copy.41) | data formatting | bytes 4194304 | tf_op jit(solution)/shard_map/reshape | solution.py:97
  66.5 3.6 %convolution_convert_fusion = bf16[64,16384]{1,0:T(8,128)(2,1)} fusion(f32[32,16384]{1,0:T(8,128)S(1)} %copy-done.1, f32[32,16384]{1,0:T(8,128)} %reshape.248, s32[32]{0:T(128)S(1)} %copy-done.8), kind=kOutput, calls=%fused_computation.25 | convolution fusion | flops 69208064 | bytes 6291584 | tf_op jit(solution)/shard_map/dot_general | solution.py:110
  70.1 4.6 %reshape.249 = bf16[8,32,4096]{2,1,0:T(8,128)(2,1)} reshape(bf16[64,16384]{1,0:T(8,128)(2,1)} %convolution_convert_fusion) | data formatting | bytes 4194304 | tf_op jit(solution)/shard_map/reshape | solution.py:111
  74.7 5.4 %all-to-all-start.1 = ((bf16[8,32,4096]{2,1,0:T(8,128)(2,1)}), bf16[8,32,4096]{2,1,0:T(8,128)(2,1)S(1)}, u32[]{:S(2)}, u32[]{:S(2)}) async-start(bf16[8,32,4096]{2,1,0:T(8,128)(2,1)} %reshape.249), calls=%async_computation.1 | async-start | bytes 4194304 | tf_op jit(solution)/shard_map/all_to_all | solution.py:117
  80.1 0.2 reduce.6
  80.4 0.2 reduce-window.17
  80.7 45.6 %all-to-all-done.1 = bf16[8,32,4096]{2,1,0:T(8,128)(2,1)S(1)} async-done(((bf16[8,32,4096]{2,1,0:T(8,128)(2,1)}), bf16[8,32,4096]{2,1,0:T(8,128)(2,1)S(1)}, u32[]{:S(2)}, u32[]{:S(2)}) %all-to-all-start.1) | async-done | bytes 2097184 | tf_op jit(solution)/shard_map/all_to_all | solution.py:117
  126.3 2.9 %reshape.250 = bf16[64,16384]{1,0:T(8,128)(2,1)} reshape(bf16[8,32,4096]{2,1,0:T(8,128)(2,1)S(1)} %all-to-all-done.1) | data formatting | bytes 4194304 | tf_op jit(solution)/shard_map/reshape | solution.py:131
  129.2 2.0 %convolution_convert_fusion.1 = bf16[32,16384]{1,0:T(8,128)(2,1)S(1)} fusion(bf16[64,16384]{1,0:T(8,128)(2,1)} %reshape.250, s32[64]{0:T(128)S(1)} %select_n.56), kind=kOutput, calls=%fused_computation.26 | convolution fusion | flops 67635200 | bytes 3145984 | tf_op jit(solution)/shard_map/dot_general | solution.py:129
  131.2 1.7 %reshape.251 = bf16[128,4096]{1,0:T(8,128)(2,1)} reshape(bf16[32,16384]{1,0:T(8,128)(2,1)S(1)} %convolution_convert_fusion.1) | data formatting | bytes 2097152 | tf_op jit(solution)/shard_map/reshape | solution.py:134
  (44 shorter events, 0.7 us)
Async XLA Ops:
  0.0 41.9 %copy-start = (bf16[128,4096]{1,0:T(8,128)(2,1)S(1)}, bf16[128,4096]{1,0:T(8,128)(2,1)}, u32[]{:S(2)}) copy-start(bf16[128,4096]{1,0:T(8,128)(2,1)} %param.17) | copy-start | bytes 3145732
  0.0 18.5 %copy-start.7 = (s32[4,128]{1,0:T(4,128)S(1)}, s32[4,128]{1,0:T(4,128)}, u32[]{:S(2)}) copy-start(s32[4,128]{1,0:T(4,128)} %constant.136.clone.1) | copy-start | bytes 6148
  0.0 18.6 %copy-start.10 = (s32[32]{0:T(128)S(1)}, s32[32]{0:T(128)}, u32[]{:S(2)}) copy-start(s32[32]{0:T(128)} %param.21) | copy-start | bytes 388
  0.0 18.6 %copy-start.3 = (f32[4,1024]{1,0:T(4,128)S(1)}, f32[4,1024]{1,0:T(4,128)}, u32[]{:S(2)}) copy-start(f32[4,1024]{1,0:T(4,128)} %param.14) | copy-start | bytes 49156
  0.8 19.1 %collective-permute-start = (bf16[3,1024]{1,0:T(4,128)(2,1)S(1)}, bf16[3,1024]{1,0:T(4,128)(2,1)S(1)}, u32[]{:S(2)}, u32[]{:S(2)}) collective-permute-start(bf16[3,1024]{1,0:T(4,128)(2,1)S(1)} %slice.57), channel_id=1, source_target_pairs={{0,1},{1,2},{2,3},{3,4},{4,5},{5,6},{6,7},{8,9},{9,10},{10,11},{11... | collective-permute-start | bytes 18440 | tf_op jit(solution)/shard_map/ppermute | solution.py:17
  7.2 67.6 %all-to-all-start = ((s32[8,1,1]{2,1,0:T(1,128)}), s32[8,1,1]{2,1,0:T(1,128)S(1)}, u32[]{:S(2)}, u32[]{:S(2)}) async-start(s32[8,1,1]{2,1,0:T(1,128)} %copy.37), calls=%async_computation | async-start | bytes 8192 | tf_op jit(solution)/shard_map/all_to_all | solution.py:118
  12.9 11.8 %copy-start.4 = (s32[128]{0:T(128)}, s32[128]{0:T(128)S(1)}, u32[]{:S(2)}) copy-start(s32[128]{0:T(128)S(1)} %iota_add_fusion.1) | copy-start | bytes 1540
  24.7 2.8 %copy-start.2 = (f32[4096]{0:T(1024)S(1)}, f32[4096]{0:T(1024)}, u32[]{:S(2)}) copy-start(f32[4096]{0:T(1024)} %param.15) | copy-start | bytes 49156
  27.0 0.5 copy-start.9
  31.1 6.4 %collective-permute-start.1 = (bf16[2,128,256]{2,1,0:T(8,128)(2,1)S(1)}, bf16[2,128,256]{2,1,0:T(8,128)(2,1)S(1)}, u32[]{:S(2)}, u32[]{:S(2)}) collective-permute-start(bf16[2,128,256]{2,1,0:T(8,128)(2,1)S(1)} %fusion.27), channel_id=1, source_target_pairs={{0,1},{1,2},{2,3},{3,4},{4,5},{5,6},{6,7},{8,9},{9,10},{10,11},{11... | collective-permute-start | bytes 393224 | tf_op jit(solution)/shard_map/ppermute | solution.py:17
  37.5 11.1 %collective-permute-start.2 = (bf16[2,128,256]{2,1,0:T(8,128)(2,1)S(1)}, bf16[2,128,256]{2,1,0:T(8,128)(2,1)S(1)}, u32[]{:S(2)}, u32[]{:S(2)}) collective-permute-start(bf16[2,128,256]{2,1,0:T(8,128)(2,1)S(1)} %collective-permute-done.1), channel_id=1, source_target_pairs={{0,1},{1,2},{2,3},{3,4},{4,5},{5,6},{6,7},{8,9},{9,10},{10,11},{11... | collective-permute-start | bytes 393224 | tf_op jit(solution)/shard_map/ppermute | solution.py:17
  47.2 1.6 %copy-start.5 = (s32[128]{0:T(128)S(1)}, s32[128]{0:T(128)}, u32[]{:S(2)}) copy-start(s32[128]{0:T(128)} %copy-done.4) | copy-start | bytes 1540
  47.2 1.6 %copy-start.6 = (pred[384]{0:T(512)(128)(4,1)S(1)}, pred[384]{0:T(512)(128)(4,1)}, u32[]{:S(2)}) copy-start(pred[384]{0:T(512)(128)(4,1)} %broadcast_compare_fusion) | copy-start | bytes 1156
  63.6 2.9 %copy-start.1 = (f32[32,16384]{1,0:T(8,128)S(1)}, f32[32,16384]{1,0:T(8,128)}, u32[]{:S(2)}) copy-start(f32[32,16384]{1,0:T(8,128)} %reshape.252) | copy-start | bytes 6291460
  63.6 2.9 %copy-start.8 = (s32[32]{0:T(128)S(1)}, s32[32]{0:T(128)}, u32[]{:S(2)}) copy-start(s32[32]{0:T(128)} %multiply_add_fusion) | copy-start | bytes 388
  74.7 51.6 %all-to-all-start.1 = ((bf16[8,32,4096]{2,1,0:T(8,128)(2,1)}), bf16[8,32,4096]{2,1,0:T(8,128)(2,1)S(1)}, u32[]{:S(2)}, u32[]{:S(2)}) async-start(bf16[8,32,4096]{2,1,0:T(8,128)(2,1)} %reshape.249), calls=%async_computation.1 | async-start | bytes 4194304 | tf_op jit(solution)/shard_map/all_to_all | solution.py:117
where the time goes:
time: 133 us
  waiting for transfers between devices  47.4 us (36%)
  local copies, waits for them, and re-layouts  27.8 us (21%)
  starting transfers between devices  23.5 us (18%)
  matrix products  17.1 us (13%)
  other arithmetic  13 us (10%)
  loops' own time  3.96 us (3%)
    all_to_all x1, waiting for transfers between devices, per_device(): lax.all_to_all(send_buffer, 'seq', split_axis=0, concat_axis=0, tiled=True)  45.6 us
    ppermute x3, starting transfers between devices, from_behind(): return lax.ppermute(array, axis, pairs)  13.1 us
    all_to_all x1, starting transfers between devices, per_device(): lax.all_to_all(send_buffer, 'seq', split_axis=0, concat_axis=0, tiled=True)  5.42 us
    reduce_sum x2, other arithmetic, per_device(): mean_sq = jnp.mean(short_wide * short_wide, axis=1, keepdims=True)  4.91 us
    all_to_all x1, starting transfers between devices, per_device(): lax.all_to_all(send_counts, 'seq', split_axis=0, concat_axis=0, tiled=True)  4.88 us
    reshape x1, local copies, waits for them, and re-layouts, per_device(): send_buffer = send_buffer.reshape(n_seq, most_slots * PANEL, width)  4.56 us
    another operation x1, loops' own time, per_device(): grouped = lax.map(attend, jnp.arange(kv_heads, dtype=jnp.int32))  3.96 us
    dot_general x1, matrix products, per_device(): jnp.dot(latent, w_qup, preferred_element_type=jnp.float32)  3.72 us
  transfers between devices with their start and end apart: 5, of which 2 were waited for; matrix products, arithmetic and copies ran while one was open for 38% of the time, Pallas kernels for 0%

commit v1 on v0

v1 whole, which is shorter than its diff:
```python
import functools
import math

import jax
import jax.numpy as jnp
from jax import lax
from jax.experimental import pallas as pl
from jax.experimental.pallas import tpu as pltpu
from jax.sharding import PartitionSpec as P

H = 32
SHORTEN = 4
KCONV = 4
PANEL = 4
PAD = 8
EDGE = 16
VMEM_BYTES = 48 * 1024 * 1024
F32 = jnp.float32
BF16 = jnp.bfloat16


def iota(shape, dim):
    return lax.broadcasted_iota(jnp.int32, shape, dim)


def reverse_bits(value, bits):
    out = value * 0
    for b in range(bits):
        out = out + (((value >> b) & 1) << (bits - 1 - b))
    return out


def conv_kernel(n_seq, rows, merged, me_ref, lens_ref, dest_ref, x_ref, taps_ref, *refs):
    n_out = 1 if merged else n_seq
    block_refs = refs[:n_out]
    short_ref, corr_ref, wide_ref, keep_ref, pick_ref = refs[n_out:]
    n_bytes, byte_dim = x_ref.shape
    toks = n_bytes // SHORTEN
    slot = pl.program_id(0)
    me = me_ref[0]

    @pl.when(slot == 0)
    def _():
        for c in range(byte_dim // 128):
            wide_ref[c, 0:PAD, :] = jnp.zeros((PAD, 128), F32)
            wide_ref[c, PAD + n_bytes :, :] = jnp.zeros((PAD, 128), F32)
            wide_ref[c, PAD : PAD + n_bytes, :] = x_ref[:, c * 128 : (c + 1) * 128].astype(F32)
        token = me * toks + iota((toks + 8, 128), 0)

        def doc(d, carry):
            first, keep = carry
            return first + lens_ref[d], jnp.where(token == first, 0.0, keep)

        _, keep = lax.fori_loop(
            0, lens_ref.shape[0], doc, (jnp.int32(0), jnp.ones((toks + 8, 128), F32))
        )
        keep_ref[...] = keep
        lane = iota((8, toks), 1)
        panel = lane // PANEL
        dest = jnp.full((8, toks), -1, jnp.int32)
        for p in range(toks // PANEL):
            dest = jnp.where(panel == p, dest_ref[p], dest)
        rank = jnp.zeros((8, toks), jnp.int32)
        for p in range(toks // PANEL):
            rank = rank + jnp.where((panel > p) & (dest == dest_ref[p]), 1, 0)
        place = (dest ^ me) * rows + rank * PANEL + lane % PANEL
        row = iota((n_seq * rows, toks), 0)
        pick_ref[...] = jnp.where(row == place[0:1], 1.0, 0.0).astype(BF16)

    for c in range(byte_dim // 128):
        cols = slice(c * 128, (c + 1) * 128)
        total = jnp.zeros((toks, 128), F32)
        corr = jnp.zeros((1, 128), F32)
        for tap in range(KCONV):
            weight = taps_ref[tap : tap + 1, cols]
            part = wide_ref[c, pl.ds(PAD + slot - tap, toks, stride=SHORTEN), :] * weight
            if tap > 0:
                part = part * jnp.where(slot < tap, keep_ref[0:toks, :], 1.0)
                corr = corr + wide_ref[c, pl.ds(PAD + n_bytes + slot - tap, 1), :] * weight
            total = total + part
        corr_ref[:, cols] = jnp.broadcast_to(corr * keep_ref[toks : toks + 1, :], (8, 128))
        short_ref[:, cols] = total.astype(BF16)
    step = min(256, byte_dim)
    for at in range(0, byte_dim, step):
        cols = slice(at, at + step)
        placed = jnp.dot(pick_ref[...], short_ref[:, cols], preferred_element_type=F32).astype(BF16)
        if merged:
            block_refs[0][:, cols] = placed
        else:
            for k in range(n_seq):
                block_refs[k][:, cols] = placed[k * rows : (k + 1) * rows]


def project_kernel(
    dest_ref, short_ref, corr_ref, gain_ref, wk_ref, wv_ref, wd_ref, out_ref, rs_ref, acc_ref, edge_ref
):
    toks, width = short_ref.shape
    depth = wk_ref.shape[0]
    at = pl.program_id(0)
    kv = wk_ref.shape[1]

    @pl.when(at == 0)
    def _():
        total = jnp.zeros((toks, 128), F32)
        for c in range(0, width, 128):
            piece = short_ref[:, c : c + 128].astype(F32)
            total = total + piece * piece
        mean = jnp.sum(total, axis=1, keepdims=True) * (1.0 / width)
        rs_ref[...] = jnp.broadcast_to(lax.rsqrt(mean + 1e-06), (toks, 128))
        acc_ref[...] = jnp.zeros_like(acc_ref)

    cols = pl.ds(pl.multiple_of(at * depth, depth), depth)
    piece = short_ref[:, cols].astype(F32)
    gain = gain_ref[:, cols]
    normed = (piece * rs_ref[:, 0:1] * gain).astype(BF16)
    row = iota((EDGE, depth), 0)
    edge = jnp.where(row == 0, piece[0:1], jnp.where(row == 1, corr_ref[0:1, cols], 0.0)) * gain
    left = jnp.concatenate([normed, edge.astype(BF16)], axis=0)
    acc_ref[:, 0:kv] += jnp.dot(left, wk_ref[...], preferred_element_type=F32)
    acc_ref[:, kv : 2 * kv] += jnp.dot(left, wv_ref[...], preferred_element_type=F32)
    acc_ref[:, 2 * kv :] += jnp.dot(left, wd_ref[...], preferred_element_type=F32)

    @pl.when(at == pl.num_programs(0) - 1)
    def _():
        out_ref[0 : toks + EDGE, :] = acc_ref[...].astype(BF16)
        row = iota((EDGE, 128), 0)
        lane = iota((EDGE, 128), 1)
        dest = jnp.zeros((EDGE, 128), F32)
        for p in range(dest_ref.shape[0]):
            dest = jnp.where(lane == p, dest_ref[p].astype(F32), dest)
        low = acc_ref[toks : toks + EDGE, 0:128]
        out_ref[toks : toks + EDGE, 0:128] = jnp.where(row == 2, dest, low).astype(BF16)
        part = width // 8
        for c in range(8):
            edge_ref[c : c + 1, :] = short_ref[0:EDGE, c * part : (c + 1) * part].astype(F32)[0:1]
            edge_ref[8 + c : 9 + c, :] = corr_ref[0:1, c * part : (c + 1) * part]
        out_ref[toks + EDGE : toks + 2 * EDGE, 0:part] = edge_ref[...].astype(BF16)


def attend_kernel(
    n_seq, rows, pans, stack, me_ref, lens_ref, all_ref, wq_ref, add_ref, sel_ref,
    k_ref, v_ref, lat_ref, bias_ref, pick_ref, corr_ref, mine_ref,
):
    bits = n_seq.bit_length() - 1
    toks = lat_ref.shape[0]
    hd = lat_ref.shape[1]
    kvh = k_ref.shape[0]
    kv = kvh * hd
    width = corr_ref.shape[1]
    part = width // 8
    heads = wq_ref.shape[1] // hd
    keys = n_seq * toks
    me = me_ref[0]
    step = pl.program_id(0)

    @pl.when(step == 0)
    def _():
        perm = [int(reverse_bits(q, bits)) for q in range(n_seq)]
        shards = [me ^ perm[q] for q in range(n_seq)]
        mine_ref[...] = jnp.zeros_like(mine_ref)
        corr_ref[...] = jnp.zeros_like(corr_ref)
        lane128 = iota((1, 128), 1)
        me_f = me.astype(F32)
        latents = []
        top_row = iota((EDGE, 2 * kv + hd), 0)
        for q in range(n_seq):
            shard = shards[q]
            live = shard > 0
            before = reverse_bits(me ^ jnp.where(live, shard - 1, shard), bits)
            live = jnp.where(live, 1.0, 0.0)
            corr = all_ref[before, toks + EDGE : toks + 2 * EDGE, 0:part].astype(F32)[8:16] * live
            own = all_ref[q, toks + EDGE : toks + 2 * EDGE, 0:part].astype(F32)[0:8]
            first = (own + corr).astype(BF16).astype(F32)
            mean = jnp.sum(jnp.sum(first * first, axis=1, keepdims=True), axis=0, keepdims=True) * (1.0 / width)
            info = all_ref[q, toks : toks + EDGE, :].astype(F32)
            past = all_ref[before, toks : toks + EDGE, :].astype(F32)
            fixed = lax.rsqrt(mean + 1e-06) * (info[0:1] + past[1:2] * live)
            top = jnp.where(top_row == 0, fixed, all_ref[q, 0:EDGE, :].astype(F32)).astype(BF16)
            for g in range(kvh):
                at = slice(g * hd, (g + 1) * hd)
                k_ref[g, q * toks : q * toks + EDGE, :] = top[:, at]
                k_ref[g, q * toks + EDGE : (q + 1) * toks, :] = all_ref[q, EDGE:toks, at]
                at = slice(kv + g * hd, kv + (g + 1) * hd)
                v_ref[g, q * toks : q * toks + EDGE, 0:hd] = top[:, at]
                v_ref[g, q * toks + EDGE : (q + 1) * toks, 0:hd] = all_ref[q, EDGE:toks, at]
                v_ref[g, q * toks : (q + 1) * toks, hd:] = jnp.ones((toks, hd), BF16)
            latents.append(jnp.concatenate([top[:, 2 * kv :], all_ref[q, EDGE:toks, 2 * kv :]], axis=0))
            for c in range(8):
                corr_ref[q : q + 1, c * part : (c + 1) * part] = corr[c : c + 1]
            mine_ref[q : q + 1, :] = jnp.where((info[2:3, 0:128] == me_f) & (lane128 < pans), 1.0, 0.0)
        mine = mine_ref[...]
        n_pad = mine.shape[0]
        count = jnp.sum(mine, axis=1, keepdims=True)
        shard_col = me ^ reverse_bits(iota((n_pad, 1), 0), bits)
        offset = jnp.zeros((n_pad, 1), F32)
        for q in range(n_seq):
            offset = offset + jnp.where(shard_col > shards[q], count[q : q + 1], 0.0)
        pan_row, tok_lane = iota((128, toks), 0), iota((128, toks), 1)
        below = jnp.where(pan_row < tok_lane // PANEL, 1.0, 0.0).astype(BF16)
        equal = jnp.where(pan_row == tok_lane // PANEL, 1.0, 0.0).astype(BF16)
        mine16 = mine.astype(BF16)
        rank = jnp.dot(mine16, below, preferred_element_type=F32)
        chosen = jnp.dot(mine16, equal, preferred_element_type=F32)
        lane = iota((n_pad, toks), 1)
        place = jnp.where(chosen > 0.5, PANEL * (offset + rank) + (lane % PANEL).astype(F32), -1.0)
        out_row = iota((toks, toks), 0).astype(F32)
        tok = iota((toks, toks), 1)
        latent = jnp.zeros((toks, hd), F32)
        where_at = jnp.zeros((toks, toks), F32)
        pick = jnp.zeros(pick_ref.shape, F32)
        pick_lane = iota(pick_ref.shape, 1)
        for q in range(n_seq):
            hit = jnp.where(out_row == place[q : q + 1], 1.0, 0.0)
            latent = latent + jnp.dot(hit.astype(BF16), latents[q], preferred_element_type=F32)
            where_at = where_at + hit * (shards[q] * toks + tok).astype(F32)
            pick = jnp.where(pick_lane == q, hit[:, 0:1], pick)
        lat_ref[...] = latent.astype(BF16)
        pick_ref[...] = pick.astype(BF16)
        pos = jnp.broadcast_to(jnp.sum(where_at, axis=1, keepdims=True), (toks, 128)).astype(jnp.int32)

        def doc(d, carry):
            first, begin = carry
            return first + lens_ref[d], jnp.where(pos >= first, first, begin)

        _, begin = lax.fori_loop(
            0, lens_ref.shape[0], doc, (jnp.int32(0), jnp.zeros((toks, 128), jnp.int32))
        )
        for q in range(n_seq):
            key = shards[q] * toks + tok
            bias_ref[:, q * toks : (q + 1) * toks] = jnp.where(
                (key >= begin[:, 0:1]) & (key <= pos[:, 0:1]), 0.0, -1e30
            )
        slot_lane = iota((1, n_seq * rows), 1)
        within = slot_lane % rows
        target = jnp.full((1, n_seq * rows), -1.0, F32)
        for q in range(n_seq):
            valid = (slot_lane // rows == perm[q]) & ((within // PANEL).astype(F32) < count[q : q + 1])
            target = jnp.where(valid, PANEL * offset[q : q + 1] + within.astype(F32), target)
        sel_row = iota((toks, n_seq * rows), 0).astype(F32)
        sel_ref[...] = jnp.where(sel_row == target, 1.0, 0.0).astype(BF16)

    scale = math.log2(math.e) / math.sqrt(hd)
    group = step // (pl.num_programs(0) // kvh)
    query = (jnp.dot(lat_ref[...], wq_ref[...], preferred_element_type=F32) * scale).astype(BF16)
    key_all, value_all = k_ref[group], v_ref[group]
    outs = []
    for h in range(0, heads, stack):
        rows_q = jnp.concatenate([query[:, (h + i) * hd : (h + i + 1) * hd] for i in range(stack)], axis=0)
        scores = lax.dot_general(rows_q, key_all, (((1,), (1,)), ((), ())), preferred_element_type=F32)
        scores = scores.reshape(stack, toks, keys) + bias_ref[...][None]
        top = jnp.max(scores, axis=2, keepdims=True)
        probs = jnp.exp2(scores - top).astype(BF16).reshape(stack * toks, keys)
        mixed = jnp.dot(probs, value_all, preferred_element_type=F32)
        mixed = mixed[:, 0:hd] / mixed[:, hd:]
        outs += [mixed[i * toks : (i + 1) * toks] for i in range(stack)]
    wide = heads * hd
    cols = pl.ds(pl.multiple_of(step * wide, wide), wide)
    extra = jnp.dot(pick_ref[...], corr_ref[:, cols].astype(BF16), preferred_element_type=F32)
    add_ref[...] = jnp.concatenate(outs, axis=1) + extra


def place_kernel(sel_ref, add_ref, *refs):
    out_ref = refs[-1]
    blocks = [r[...] for r in refs[:-1]]
    rows = blocks[0] if len(blocks) == 1 else jnp.concatenate(blocks, axis=0)
    out_ref[...] = (jnp.dot(sel_ref[...], rows, preferred_element_type=F32) + add_ref[...]).astype(BF16)


def swap(array, by, size):
    return lax.ppermute(array, "seq", [(i, i ^ by) for i in range(size)])


def smem():
    return pl.BlockSpec(memory_space=pltpu.SMEM)


def whole_block(shape):
    return pl.BlockSpec(shape, lambda i: (0,) * len(shape))


def column_block(rows, cols):
    return pl.BlockSpec((rows, cols), lambda i: (0, i))


def params():
    return pltpu.CompilerParams(vmem_limit_bytes=VMEM_BYTES, dimension_semantics=("arbitrary",))


def per_device(
    byte_embed, conv_taps, norm_gain, w_qdown, w_qup, w_key, w_value, doc_lengths, panel_dest
):
    n_seq = lax.axis_size("seq")
    bits = n_seq.bit_length() - 1
    me = lax.axis_index("seq").astype(jnp.int32).reshape(1)
    n_bytes, byte_dim = byte_embed.shape
    toks = n_bytes // SHORTEN
    width = SHORTEN * byte_dim
    hd = width // H
    kv = w_key.shape[1]
    kvh = kv // hd
    rank = w_qdown.shape[1]
    pans = toks // PANEL
    slots = (2 * pans + n_seq - 1) // n_seq
    rows = slots * PANEL
    merged = rows % 16 != 0
    wide = 2 * kv + rank

    block_rows = n_seq * rows if merged else rows
    n_out = 1 if merged else n_seq
    *blocks, short, corr = pl.pallas_call(
        functools.partial(conv_kernel, n_seq, rows, merged),
        grid=(SHORTEN,),
        out_shape=[jax.ShapeDtypeStruct((block_rows, width), BF16)] * n_out
        + [jax.ShapeDtypeStruct((toks, width), BF16), jax.ShapeDtypeStruct((8, width), F32)],
        in_specs=[smem(), smem(), smem(), whole_block(byte_embed.shape), whole_block(conv_taps.shape)],
        out_specs=[column_block(block_rows, byte_dim)] * n_out
        + [column_block(toks, byte_dim), column_block(8, byte_dim)],
        scratch_shapes=[
            pltpu.VMEM((byte_dim // 128, n_bytes + 2 * PAD, 128), F32),
            pltpu.VMEM((toks + 8, 128), F32),
            pltpu.VMEM((n_seq * rows, toks), BF16),
        ],
        compiler_params=params(),
        name="conv_panels",
    )(me, doc_lengths, panel_dest, byte_embed, conv_taps)
    if merged:
        blocks = [blocks[0][k * rows : (k + 1) * rows] for k in range(n_seq)]

    depth = width // 4
    held = pl.pallas_call(
        project_kernel,
        grid=(width // depth,),
        out_shape=jax.ShapeDtypeStruct((toks + 2 * EDGE, wide), BF16),
        in_specs=[
            smem(),
            whole_block((toks, width)),
            whole_block((8, width)),
            whole_block((1, width)),
            pl.BlockSpec((depth, kv), lambda i: (i, 0)),
            pl.BlockSpec((depth, kv), lambda i: (i, 0)),
            pl.BlockSpec((depth, rank), lambda i: (i, 0)),
        ],
        out_specs=whole_block((toks + 2 * EDGE, wide)),
        scratch_shapes=[
            pltpu.VMEM((toks, 128), F32),
            pltpu.VMEM((toks + EDGE, wide), F32),
            pltpu.VMEM((16, width // 8), F32),
        ],
        compiler_params=params(),
        name="project",
    )(panel_dest, short, corr, norm_gain.reshape(1, width), w_key, w_value, w_qdown)

    held = held[None]
    for b in range(bits - 1, -1, -1):
        held = jnp.concatenate([held, swap(held, 1 << b, n_seq)], axis=0)

    got = {0: blocks[0]}
    for k in list(range(n_seq // 2, n_seq)) + list(range(1, n_seq // 2)):
        got[k] = swap(blocks[k], k, n_seq)

    heads = min(4, H // kvh)
    stack = heads if n_seq * toks <= 1024 else 1
    n_pad = max(16, n_seq)
    added, sel = pl.pallas_call(
        functools.partial(attend_kernel, n_seq, rows, pans, stack),
        grid=(H // heads,),
        out_shape=[
            jax.ShapeDtypeStruct((toks, width), F32),
            jax.ShapeDtypeStruct((toks, n_seq * rows), BF16),
        ],
        in_specs=[smem(), smem(), whole_block(held.shape), column_block(rank, heads * hd)],
        out_specs=[column_block(toks, heads * hd), whole_block((toks, n_seq * rows))],
        scratch_shapes=[
            pltpu.VMEM((kvh, n_seq * toks, hd), BF16),
            pltpu.VMEM((kvh, n_seq * toks, 2 * hd), BF16),
            pltpu.VMEM((toks, rank), BF16),
            pltpu.VMEM((toks, n_seq * toks), F32),
            pltpu.VMEM((toks, n_pad), BF16),
            pltpu.VMEM((n_pad, width), F32),
            pltpu.VMEM((n_pad, 128), F32),
        ],
        compiler_params=params(),
        name="attend",
    )(me, doc_lengths, held, w_qup)

    arrived = [got[k] for k in range(n_seq)]
    if merged:
        arrived = [jnp.concatenate(arrived, axis=0)]
    out_cols = width // 4
    return pl.pallas_call(
        place_kernel,
        grid=(4,),
        out_shape=jax.ShapeDtypeStruct((toks, width), BF16),
        in_specs=[whole_block(sel.shape), column_block(toks, out_cols)]
        + [column_block(a.shape[0], out_cols) for a in arrived],
        out_specs=column_block(toks, out_cols),
        compiler_params=params(),
        name="place",
    )(sel, added, *arrived)


def solution(mesh):
    in_specs = (P(("dp", "seq"), None), P(), P(), P(), P(), P(), P(), P("dp"), P(("dp", "seq")))
    out_specs = P(("dp", "seq"), None)
    return jax.shard_map(
        per_device, mesh=mesh, in_specs=in_specs, out_specs=out_specs, check_vma=False
    )
```

time: 133 us -> 106 us (0.80)
  the two profiles are of different devices: /device:TPU:0 before, /device:TPU:16 now
where the time goes in v1:
time: 106 us
  waiting for transfers between devices  62.2 us (59%)
  Pallas kernels  23.3 us (22%)
  starting transfers between devices  13.6 us (13%)
  local copies, waits for them, and re-layouts  6.55 us (6%)
    ppermute x10, waiting for transfers between devices, swap(): return lax.ppermute(array, 'seq', [(i, i ^ by) for i in range(size)])  62.2 us
    ppermute x10, starting transfers between devices, swap(): return lax.ppermute(array, 'seq', [(i, i ^ by) for i in range(size)])  13.6 us
    pallas_call x1, Pallas kernels, per_device(): pl.pallas_call(functools.partial(attend_kernel, n_seq, rows, pans, stack)...  13.6 us
    unnamed x16, local copies, waits for them, and re-layouts  6.55 us
    pallas_call x1, Pallas kernels, per_device(): pl.pallas_call(project_kernel, grid=(width // depth,), out_shape=jax.Shap...  3.93 us
    pallas_call x1, Pallas kernels, per_device(): pl.pallas_call(functools.partial(conv_kernel, n_seq, rows, merged), grid=...  3.43 us
    pallas_call x1, Pallas kernels, per_device(): pl.pallas_call(place_kernel, grid=(4,), out_shape=jax.ShapeDtypeStruct((t...  2.41 us
  transfers between devices with their start and end apart: 10, of which 6 were waited for; matrix products, arithmetic and copies ran while one was open for 0% of the time, Pallas kernels for 13%

profile of v1, /device:TPU:16, one launch (start us, length us, event | category | flops | bytes accessed | tf_op | source)
XLA Modules:
  0.0 106.1 jit_solution(503435996049602930)
XLA Ops:
  0.0 0.0 copy-start.2
  0.0 1.2 %copy-done.2 = bf16[512,1024]{1,0:T(8,128)(2,1)S(1)} copy-done((bf16[512,1024]{1,0:T(8,128)(2,1)S(1)}, bf16[512,1024]{1,0:T(8,128)(2,1)}, u32[]{:S(2)}) %copy-start.2) | copy-done | bytes 1048600
  1.2 0.0 copy-start.4
  1.2 0.7 copy-done.4
  1.9 0.0 copy-start.6
  1.9 0.7 copy-done.6
  2.6 0.0 copy-start.7
  2.6 0.7 copy-done.7
  3.3 0.0 copy-start.3
  3.3 3.4 %conv_panels.1 = (bf16[32,4096]{1,0:T(8,128)(2,1)S(1)}, bf16[32,4096]{1,0:T(8,128)(2,1)S(1)}, bf16[32,4096]{1,0:T(8,128)(2,1)S(1)}, bf16[32,4096]{1,0:T(8,128)(2...) custom-call(s32[1]{0:T(128)} %bitcast.me_ref, ...), custom_call_target="tpu_custom_call" | custom-call | tf_op jit(solution)/shard_map/conv_panels/pallas_call | solution.py:310
  6.7 0.0 copy-done.3
  6.7 0.0 copy-start
  6.7 1.6 %copy-done = bf16[4096,256]{1,0:T(8,128)(2,1)S(1)} copy-done((bf16[4096,256]{1,0:T(8,128)(2,1)S(1)}, bf16[4096,256]{1,0:T(8,128)(2,1)}, u32[]{:S(2)}) %copy-start) | copy-done | bytes 2097176
  8.3 0.0 copy-start.5
  8.3 0.7 copy-done.5
  9.0 3.9 %project.1 = bf16[160,640]{1,0:T(8,128)(2,1)S(1)} custom-call(s32[32]{0:T(128)S(1)} %copy-done.7, bf16[128,4096]{1,0:T(8,128)(2,1)S(1)} %get-tuple-element.17.short_ref, f32[8,4096]{1,0:T(8,128)S(1)} %get-tuple-element.18.corr_ref, f32[1,4096]{1,0:T(1,128)S(1)} %bitcast.7, bf16[4096,256]{1,0:T(8,128)(2,1)S(1)} %copy-done, bf16[4096,256]{1,0:T(8,128)(2,1)} %wv_ref.1, ...), custom_call_target="tpu_custom_call" | custom-call | tf_op jit(solution)/shard_map/project/pallas_call | solution.py:330
  13.0 0.1 collective-permute-start
  13.0 9.0 %collective-permute-done = bf16[1,160,640]{2,1,0:T(8,128)(2,1)S(1)} collective-permute-done((bf16[1,160,640]{2,1,0:T(8,128)(2,1)S(1)}, bf16[1,160,640]{2,1,0:T(8,128)(2,1)S(1)}, u32[]{:S(2)}, u32[]{:S(2)}) %collective-permute-start) | collective-permute-done | bytes 204832 | tf_op jit(solution)/shard_map/ppermute | solution.py:270
  22.1 4.6 %collective-permute-start.1 = (bf16[2,160,640]{2,1,0:T(8,128)(2,1)S(1)}, bf16[2,160,640]{2,1,0:T(8,128)(2,1)S(1)}, u32[]{:S(2)}, u32[]{:S(2)}) collective-permute-start(bf16[2,160,640]{2,1,0:T(8,128)(2,1)S(1)} %pad_maximum_fusion.2), channel_id=1, source_target_pairs={{0,2},{1,3},{2,0},{3,1},{4,6},{5,7},{6,4},{7,5},{8,10},{9,11},{10,... | collective-permute-start | bytes 1228808 | tf_op jit(solution)/shard_map/ppermute | solution.py:270
  26.7 9.6 %collective-permute-done.1 = bf16[2,160,640]{2,1,0:T(8,128)(2,1)S(1)} collective-permute-done((bf16[2,160,640]{2,1,0:T(8,128)(2,1)S(1)}, bf16[2,160,640]{2,1,0:T(8,128)(2,1)S(1)}, u32[]{:S(2)}, u32[]{:S(2)}) %collective-permute-start.1) | collective-permute-done | bytes 409632 | tf_op jit(solution)/shard_map/ppermute | solution.py:270
  36.4 0.1 pad_maximum_fusion.1
  36.5 1.6 %collective-permute-start.2 = (bf16[4,160,640]{2,1,0:T(8,128)(2,1)S(1)}, bf16[4,160,640]{2,1,0:T(8,128)(2,1)S(1)}, u32[]{:S(2)}, u32[]{:S(2)}) collective-permute-start(bf16[4,160,640]{2,1,0:T(8,128)(2,1)S(1)} %pad_maximum_fusion.1), channel_id=1, source_target_pairs={{0,1},{1,0},{2,3},{3,2},{4,5},{5,4},{6,7},{7,6},{8,9},{9,8},{10,11... | collective-permute-start | bytes 2457608 | tf_op jit(solution)/shard_map/ppermute | solution.py:270
  38.0 0.5 collective-permute-start.3
  38.5 1.7 %collective-permute-start.4 = (bf16[32,4096]{1,0:T(8,128)(2,1)S(1)}, bf16[32,4096]{1,0:T(8,128)(2,1)S(1)}, u32[]{:S(2)}, u32[]{:S(2)}) collective-permute-start(bf16[32,4096]{1,0:T(8,128)(2,1)S(1)} %get-tuple-element.23), channel_id=1, source_target_pairs={{0,2},{1,3},{2,0},{3,1},{4,6},{5,7},{6,4},{7,5},{8,10},{9,11},{10,... | collective-permute-start | bytes 786440 | tf_op jit(solution)/shard_map/ppermute | solution.py:270
  40.3 1.2 %collective-permute-start.5 = (bf16[32,4096]{1,0:T(8,128)(2,1)S(1)}, bf16[32,4096]{1,0:T(8,128)(2,1)S(1)}, u32[]{:S(2)}, u32[]{:S(2)}) collective-permute-start(bf16[32,4096]{1,0:T(8,128)(2,1)S(1)} %get-tuple-element.24), channel_id=1, source_target_pairs={{0,3},{1,2},{2,1},{3,0},{4,7},{5,6},{6,5},{7,4},{8,11},{9,10},{10,... | collective-permute-start | bytes 786440 | tf_op jit(solution)/shard_map/ppermute | solution.py:270
  41.5 0.0 collective-permute-start.6
  41.5 25.9 %collective-permute-done.3.refs_1_ = bf16[32,4096]{1,0:T(8,128)(2,1)S(1)} collective-permute-done((bf16[32,4096]{1,0:T(8,128)(2,1)S(1)}, bf16[32,4096]{1,0:T(8,128)(2,1)S(1)}, u32[]{:S(2)}, u32[]{:S(2)}) %collective-permute-start.3) | collective-permute-done | bytes 262176 | tf_op jit(solution)/shard_map/ppermute | solution.py:270
  67.4 0.0 collective-permute-start.7
  67.4 0.0 collective-permute-done.4.refs_2_
  67.4 3.8 %collective-permute-start.8 = (bf16[32,4096]{1,0:T(8,128)(2,1)S(1)}, bf16[32,4096]{1,0:T(8,128)(2,1)S(1)}, u32[]{:S(2)}, u32[]{:S(2)}) collective-permute-start(bf16[32,4096]{1,0:T(8,128)(2,1)S(1)} %get-tuple-element.27), channel_id=1, source_target_pairs={{0,6},{1,7},{2,4},{3,5},{4,2},{5,3},{6,0},{7,1},{8,14},{9,15},{10,... | collective-permute-start | bytes 786440 | tf_op jit(solution)/shard_map/ppermute | solution.py:270
  71.2 0.0 collective-permute-done.2
  71.2 0.0 copy-start.1
  71.2 0.0 collective-permute-start.9
  71.3 0.2 pad_maximum_fusion.all_ref
  71.5 1.0 copy-done.1
  72.5 13.6 %attend.1 = (f32[128,4096]{1,0:T(8,128)S(1)}, bf16[128,256]{1,0:T(8,128)(2,1)S(1)}) custom-call(s32[1]{0:T(128)} %bitcast.me_ref, s32[16]{0:T(128)S(1)} %copy-done.6, bf16[8,160,640]{2,1,0:T(8,128)(2,1)S(1)} %pad_maximum_fusion.all_ref, bf16[128,4096]{1,0:T(8,128)(2,1)S(1)} %copy-done.1), custom_call_target="tpu_custom_call" | custom-call | tf_op jit(solution)/shard_map/attend/pallas_call | solution.py:364
  86.0 0.0 collective-permute-done.5.refs_3_
  86.0 0.0 collective-permute-done.6.refs_4_
  86.1 3.7 %collective-permute-done.7.refs_5_ = bf16[32,4096]{1,0:T(8,128)(2,1)S(1)} collective-permute-done((bf16[32,4096]{1,0:T(8,128)(2,1)S(1)}, bf16[32,4096]{1,0:T(8,128)(2,1)S(1)}, u32[]{:S(2)}, u32[]{:S(2)}) %collective-permute-start.7) | collective-permute-done | bytes 262176 | tf_op jit(solution)/shard_map/ppermute | solution.py:270
  89.7 8.9 %collective-permute-done.8.refs_6_ = bf16[32,4096]{1,0:T(8,128)(2,1)S(1)} collective-permute-done((bf16[32,4096]{1,0:T(8,128)(2,1)S(1)}, bf16[32,4096]{1,0:T(8,128)(2,1)S(1)}, u32[]{:S(2)}, u32[]{:S(2)}) %collective-permute-start.8) | collective-permute-done | bytes 262176 | tf_op jit(solution)/shard_map/ppermute | solution.py:270
  98.7 5.0 %collective-permute-done.9.refs_7_ = bf16[32,4096]{1,0:T(8,128)(2,1)S(1)} collective-permute-done((bf16[32,4096]{1,0:T(8,128)(2,1)S(1)}, bf16[32,4096]{1,0:T(8,128)(2,1)S(1)}, u32[]{:S(2)}, u32[]{:S(2)}) %collective-permute-start.9) | collective-permute-done | bytes 262176 | tf_op jit(solution)/shard_map/ppermute | solution.py:270
  103.7 2.4 %place.1 = bf16[128,4096]{1,0:T(8,128)(2,1)} custom-call(bf16[128,256]{1,0:T(8,128)(2,1)S(1)} %get-tuple-element.19.sel_ref, f32[128,4096]{1,0:T(8,128)S(1)} %get-tuple-element.20.add_ref, bf16[32,4096]{1,0:T(8,128)(2,1)S(1)} %get-tuple-element.21.refs_0_, bf16[32,4096]{1,0:T(8,128)(2,1)S(1)} %collective-permute-done.3.refs_1_, ...), custom_call_target="tpu_custom_call" | custom-call | tf_op jit(solution)/shard_map/place/pallas_call | solution.py:390
  (1 shorter events, 0.0 us)
Async XLA Ops:
  0.0 1.2 %copy-start.2 = (bf16[512,1024]{1,0:T(8,128)(2,1)S(1)}, bf16[512,1024]{1,0:T(8,128)(2,1)}, u32[]{:S(2)}) copy-start(bf16[512,1024]{1,0:T(8,128)(2,1)} %x_ref.1) | copy-start | bytes 3145732
  1.2 0.7 copy-start.4
  1.9 0.7 copy-start.6
  2.6 0.7 copy-start.7
  3.3 3.4 %copy-start.3 = (bf16[4096,128]{1,0:T(8,128)(2,1)S(1)}, bf16[4096,128]{1,0:T(8,128)(2,1)}, u32[]{:S(2)}) copy-start(bf16[4096,128]{1,0:T(8,128)(2,1)} %wd_ref.1) | copy-start | bytes 3145732
  6.7 1.6 %copy-start = (bf16[4096,256]{1,0:T(8,128)(2,1)S(1)}, bf16[4096,256]{1,0:T(8,128)(2,1)}, u32[]{:S(2)}) copy-start(bf16[4096,256]{1,0:T(8,128)(2,1)} %wk_ref.1) | copy-start | bytes 6291460
  8.3 0.7 copy-start.5
  13.0 9.1 %collective-permute-start = (bf16[1,160,640]{2,1,0:T(8,128)(2,1)S(1)}, bf16[1,160,640]{2,1,0:T(8,128)(2,1)S(1)}, u32[]{:S(2)}, u32[]{:S(2)}) collective-permute-start(bf16[1,160,640]{2,1,0:T(8,128)(2,1)S(1)} %bitcast.3), channel_id=1, source_target_pairs={{0,4},{1,5},{2,6},{3,7},{4,0},{5,1},{6,2},{7,3},{8,12},{9,13},{10,... | collective-permute-start | bytes 614408 | tf_op jit(solution)/shard_map/ppermute | solution.py:270
  22.1 14.3 %collective-permute-start.1 = (bf16[2,160,640]{2,1,0:T(8,128)(2,1)S(1)}, bf16[2,160,640]{2,1,0:T(8,128)(2,1)S(1)}, u32[]{:S(2)}, u32[]{:S(2)}) collective-permute-start(bf16[2,160,640]{2,1,0:T(8,128)(2,1)S(1)} %pad_maximum_fusion.2), channel_id=1, source_target_pairs={{0,2},{1,3},{2,0},{3,1},{4,6},{5,7},{6,4},{7,5},{8,10},{9,11},{10,... | collective-permute-start | bytes 1228808 | tf_op jit(solution)/shard_map/ppermute | solution.py:270
  36.5 34.8 %collective-permute-start.2 = (bf16[4,160,640]{2,1,0:T(8,128)(2,1)S(1)}, bf16[4,160,640]{2,1,0:T(8,128)(2,1)S(1)}, u32[]{:S(2)}, u32[]{:S(2)}) collective-permute-start(bf16[4,160,640]{2,1,0:T(8,128)(2,1)S(1)} %pad_maximum_fusion.1), channel_id=1, source_target_pairs={{0,1},{1,0},{2,3},{3,2},{4,5},{5,4},{6,7},{7,6},{8,9},{9,8},{10,11... | collective-permute-start | bytes 2457608 | tf_op jit(solution)/shard_map/ppermute | solution.py:270
  38.0 29.4 %collective-permute-start.3 = (bf16[32,4096]{1,0:T(8,128)(2,1)S(1)}, bf16[32,4096]{1,0:T(8,128)(2,1)S(1)}, u32[]{:S(2)}, u32[]{:S(2)}) collective-permute-start(bf16[32,4096]{1,0:T(8,128)(2,1)S(1)} %get-tuple-element.22), channel_id=1, source_target_pairs={{0,1},{1,0},{2,3},{3,2},{4,5},{5,4},{6,7},{7,6},{8,9},{9,8},{10,11... | collective-permute-start | bytes 786440 | tf_op jit(solution)/shard_map/ppermute | solution.py:270
  38.5 28.9 %collective-permute-start.4 = (bf16[32,4096]{1,0:T(8,128)(2,1)S(1)}, bf16[32,4096]{1,0:T(8,128)(2,1)S(1)}, u32[]{:S(2)}, u32[]{:S(2)}) collective-permute-start(bf16[32,4096]{1,0:T(8,128)(2,1)S(1)} %get-tuple-element.23), channel_id=1, source_target_pairs={{0,2},{1,3},{2,0},{3,1},{4,6},{5,7},{6,4},{7,5},{8,10},{9,11},{10,... | collective-permute-start | bytes 786440 | tf_op jit(solution)/shard_map/ppermute | solution.py:270
  40.3 45.8 %collective-permute-start.5 = (bf16[32,4096]{1,0:T(8,128)(2,1)S(1)}, bf16[32,4096]{1,0:T(8,128)(2,1)S(1)}, u32[]{:S(2)}, u32[]{:S(2)}) collective-permute-start(bf16[32,4096]{1,0:T(8,128)(2,1)S(1)} %get-tuple-element.24), channel_id=1, source_target_pairs={{0,3},{1,2},{2,1},{3,0},{4,7},{5,6},{6,5},{7,4},{8,11},{9,10},{10,... | collective-permute-start | bytes 786440 | tf_op jit(solution)/shard_map/ppermute | solution.py:270
  41.5 44.5 %collective-permute-start.6 = (bf16[32,4096]{1,0:T(8,128)(2,1)S(1)}, bf16[32,4096]{1,0:T(8,128)(2,1)S(1)}, u32[]{:S(2)}, u32[]{:S(2)}) collective-permute-start(bf16[32,4096]{1,0:T(8,128)(2,1)S(1)} %get-tuple-element.25), channel_id=1, source_target_pairs={{0,4},{1,5},{2,6},{3,7},{4,0},{5,1},{6,2},{7,3},{8,12},{9,13},{10,... | collective-permute-start | bytes 786440 | tf_op jit(solution)/shard_map/ppermute | solution.py:270
  67.4 22.4 %collective-permute-start.7 = (bf16[32,4096]{1,0:T(8,128)(2,1)S(1)}, bf16[32,4096]{1,0:T(8,128)(2,1)S(1)}, u32[]{:S(2)}, u32[]{:S(2)}) collective-permute-start(bf16[32,4096]{1,0:T(8,128)(2,1)S(1)} %get-tuple-element.26), channel_id=1, source_target_pairs={{0,5},{1,4},{2,7},{3,6},{4,1},{5,0},{6,3},{7,2},{8,13},{9,12},{10,... | collective-permute-start | bytes 786440 | tf_op jit(solution)/shard_map/ppermute | solution.py:270
  67.4 31.3 %collective-permute-start.8 = (bf16[32,4096]{1,0:T(8,128)(2,1)S(1)}, bf16[32,4096]{1,0:T(8,128)(2,1)S(1)}, u32[]{:S(2)}, u32[]{:S(2)}) collective-permute-start(bf16[32,4096]{1,0:T(8,128)(2,1)S(1)} %get-tuple-element.27), channel_id=1, source_target_pairs={{0,6},{1,7},{2,4},{3,5},{4,2},{5,3},{6,0},{7,1},{8,14},{9,15},{10,... | collective-permute-start | bytes 786440 | tf_op jit(solution)/shard_map/ppermute | solution.py:270
  71.2 1.2 %copy-start.1 = (bf16[128,4096]{1,0:T(8,128)(2,1)S(1)}, bf16[128,4096]{1,0:T(8,128)(2,1)}, u32[]{:S(2)}) copy-start(bf16[128,4096]{1,0:T(8,128)(2,1)} %wq_ref.1) | copy-start | bytes 3145732
  71.2 32.5 %collective-permute-start.9 = (bf16[32,4096]{1,0:T(8,128)(2,1)S(1)}, bf16[32,4096]{1,0:T(8,128)(2,1)S(1)}, u32[]{:S(2)}, u32[]{:S(2)}) collective-permute-start(bf16[32,4096]{1,0:T(8,128)(2,1)S(1)} %get-tuple-element.28), channel_id=1, source_target_pairs={{0,7},{1,6},{2,5},{3,4},{4,3},{5,2},{6,1},{7,0},{8,15},{9,14},{10,... | collective-permute-start | bytes 786440 | tf_op jit(solution)/shard_map/ppermute | solution.py:270

commit v2 on v0

v2 whole, which is shorter than its diff:
```python
import functools
import math

import jax
import jax.numpy as jnp
from jax import lax
from jax.experimental import pallas as pl
from jax.experimental.pallas import tpu as pltpu
from jax.sharding import PartitionSpec as P

H = 32
SHORTEN = 4
KCONV = 4
PANEL = 4
BACK = 2
PAD = 8
EDGE = 16
MARK = 2.0**120
VMEM_BYTES = 48 * 1024 * 1024
ALL_VMEM = 60 * 1024 * 1024
F32 = jnp.float32
BF16 = jnp.bfloat16


def iota(shape, dim):
    return lax.broadcasted_iota(jnp.int32, shape, dim)


def project_kernel(
    me_ref, lens_hbm, x_hbm, taps_hbm, gain_hbm, wk_hbm, wv_hbm, wd_hbm,
    out_ref, short_ref, lat_ref, edge_ref,
    lens_ref, x_ref, taps_ref, gain_ref, w_ref, sems, wsems, wide_ref, keep_ref, u_ref, acc_ref, fold_ref,
):
    n_bytes, byte_dim = x_ref.shape
    toks, width = short_ref.shape
    kv = wk_hbm.shape[1]
    rank = wd_hbm.shape[1]
    me = me_ref[0]
    small = [
        pltpu.make_async_copy(lens_hbm, lens_ref, sems.at[0]),
        pltpu.make_async_copy(taps_hbm, taps_ref, sems.at[1]),
        pltpu.make_async_copy(gain_hbm, gain_ref, sems.at[2]),
    ]
    some = n_bytes // 4
    large = [
        pltpu.make_async_copy(
            x_hbm.at[pl.ds(i * some, some)], x_ref.at[pl.ds(i * some, some)], sems.at[3 + i]
        )
        for i in range(4)
    ]
    weights = []
    for i in range(SHORTEN):
        at = pl.ds(i * byte_dim, byte_dim)
        weights.append(
            [
                pltpu.make_async_copy(wk_hbm.at[at], w_ref.at[at, pl.ds(0, kv)], wsems.at[i, 0]),
                pltpu.make_async_copy(wv_hbm.at[at], w_ref.at[at, pl.ds(kv, kv)], wsems.at[i, 1]),
                pltpu.make_async_copy(wd_hbm.at[at], w_ref.at[at, pl.ds(2 * kv, rank)], wsems.at[i, 2]),
            ]
        )
    for copy in small + large + [copy for group in weights for copy in group]:
        copy.start()
    for c in range(byte_dim // 128):
        wide_ref[c, 0:PAD, :] = jnp.zeros((PAD, 128), F32)
        wide_ref[c, PAD + n_bytes :, :] = jnp.zeros((PAD, 128), F32)
    u_ref[toks:, :] = jnp.zeros((EDGE, width), BF16)
    for copy in small:
        copy.wait()
    token = me * toks + iota((toks + 8, 128), 0)

    def doc(d, carry):
        first, keep = carry
        return first + lens_ref[d], jnp.where(token == first, 0.0, keep)

    _, keep = lax.fori_loop(
        0, lens_ref.shape[0], doc, (jnp.int32(0), jnp.ones((toks + 8, 128), F32))
    )
    keep_ref[...] = keep
    for i, copy in enumerate(large):
        copy.wait()
        for c in range(byte_dim // 128):
            wide_ref[c, PAD + i * some : PAD + (i + 1) * some, :] = x_ref[
                i * some : (i + 1) * some, c * 128 : (c + 1) * 128
            ].astype(F32)

    part = width // 8
    squares = jnp.zeros((toks, 128), F32)
    for slot in range(SHORTEN):
        for c in range(byte_dim // 128):
            cols = slice(c * 128, (c + 1) * 128)
            at = slot * byte_dim + c * 128
            here = jnp.zeros((toks, 128), F32)
            before = jnp.zeros((toks, 128), F32)
            corr = jnp.zeros((1, 128), F32)
            for tap in range(KCONV):
                weight = taps_ref[tap : tap + 1, cols]
                term = wide_ref[c, pl.ds(PAD + slot - tap, toks, stride=SHORTEN), :] * weight
                if tap > slot:
                    before = before + term
                    spot = PAD + n_bytes + slot - tap
                    corr = corr + wide_ref[c, spot : spot + 1, :] * weight
                else:
                    here = here + term
            if slot < KCONV - 1:
                here = here + before * keep_ref[0:toks, :]
                corr = corr * keep_ref[toks : toks + 1, :]
            short = here.astype(BF16)
            short_ref[:, at : at + 128] = short
            short = short.astype(F32)
            squares = squares + short * short
            gain = gain_ref[:, at : at + 128]
            u_ref[0:toks, at : at + 128] = (short * gain).astype(BF16)
            row = iota((EDGE, 128), 0)
            u_ref[toks:, at : at + 128] = jnp.where(row == 0, corr * gain, 0.0).astype(BF16)
            r, o = at // part, at % part
            fold_ref[r : r + 1, o : o + 128] = short[0:1]
            fold_ref[8 + r : 9 + r, o : o + 128] = corr
        for copy in weights[slot]:
            copy.wait()
        span = slice(slot * byte_dim, (slot + 1) * byte_dim)
        got = jnp.dot(u_ref[:, span], w_ref[span, :], preferred_element_type=F32)
        if slot == 0:
            acc_ref[...] = got
        else:
            acc_ref[...] += got
    rs = lax.rsqrt(jnp.sum(squares, axis=1, keepdims=True) * (1.0 / width) + 1e-06)
    out_ref[0:toks, :] = (acc_ref[0:toks, 0 : 2 * kv] * rs).astype(BF16)
    lat_ref[...] = (acc_ref[0:toks, 2 * kv :] * rs).astype(BF16)
    edge_ref[...] = acc_ref[0:8, :]
    row = iota((EDGE, 2 * kv), 0)
    low = jnp.concatenate(
        [acc_ref[toks : toks + 1, 2 * kv :], jnp.zeros((1, 2 * kv - rank), F32)], axis=1
    )
    sums = jnp.where(row == 0, acc_ref[0:1, 0 : 2 * kv], 0.0)
    sums = jnp.where(row == 1, acc_ref[toks : toks + 1, 0 : 2 * kv], sums)
    out_ref[toks : toks + EDGE, :] = jnp.where(row == 2, low, sums).astype(BF16)
    out_ref[toks + EDGE : toks + 2 * EDGE, 0:part] = fold_ref[...].astype(BF16)


def plan_kernel(n_seq, rows, me_ref, lens_ref, dest_ref, bias_ref, pick_ref, fill_ref):
    toks, keys = bias_ref.shape
    me = me_ref[0]
    pos = me * toks + iota((toks, 128), 0)

    def doc(d, carry):
        first, begin = carry
        return first + lens_ref[d], jnp.where(pos >= first, first, begin)

    _, begin = lax.fori_loop(
        0, lens_ref.shape[0], doc, (jnp.int32(0), jnp.zeros((toks, 128), jnp.int32))
    )
    for at in range(0, keys, 128):
        key = (me - BACK) * toks + at + iota((toks, 128), 1)
        bias_ref[:, at : at + 128] = jnp.where((key >= begin) & (key <= pos), 0.0, -1e30)
    lane = iota((8, toks), 1)
    panel = lane // PANEL
    dest = jnp.full((8, toks), -1, jnp.int32)
    for p in range(toks // PANEL):
        dest = jnp.where(panel == p, dest_ref[p], dest)
    rank = jnp.zeros((8, toks), jnp.int32)
    for p in range(toks // PANEL):
        rank = rank + jnp.where((panel > p) & (dest == dest_ref[p]), 1, 0)
    place = (dest ^ me) * rows + rank * PANEL + lane % PANEL
    hit = jnp.where(iota((n_seq * rows, toks), 0) == place[0:1], 1.0, 0.0)
    pick_ref[...] = hit.astype(BF16)
    used = jnp.sum(hit, axis=1, keepdims=True)
    fill_ref[...] = jnp.broadcast_to((1.0 - used) * MARK, fill_ref.shape)


def attend_kernel(
    n_seq, rows, merged, lat_ref, edge_ref, own_ref, one_ref, two_ref, bias_ref, pick_ref, fill_ref,
    wq_ref, short_ref, *refs,
):
    n_out = 1 if merged else n_seq
    block_refs = refs[:n_out]
    k_ref, v_ref, query_ref, corr_ref = refs[n_out:]
    toks, hd = lat_ref.shape
    kvh = k_ref.shape[0]
    kv = kvh * hd
    width = corr_ref.shape[1]
    part = width // 8
    heads = wq_ref.shape[1] // hd
    keys = bias_ref.shape[1]
    step = pl.program_id(0)

    @pl.when(step == 0)
    def _():
        def root(first):
            total = jnp.sum(jnp.sum(first * first, axis=1, keepdims=True), axis=0, keepdims=True)
            return lax.rsqrt(total * (1.0 / width) + 1e-06)

        fold = slice(toks + EDGE, toks + 2 * EDGE)
        sums = slice(toks, toks + EDGE)
        own_fold = own_ref[fold, 0:part].astype(F32)
        one_fold = one_ref[fold, 0:part].astype(F32)
        two_fold = two_ref[fold, 0:part].astype(F32)
        one_sums = one_ref[sums, :].astype(F32)
        two_sums = two_ref[sums, :].astype(F32)
        scale = root((own_fold[0:8] + one_fold[8:16]).astype(BF16).astype(F32))
        own_kv = scale * (edge_ref[0:1, 0 : 2 * kv] + one_sums[1:2])
        own_lat = scale * (edge_ref[0:1, 2 * kv :] + one_sums[2:3, 0:hd])
        scale = root((one_fold[0:8] + two_fold[8:16]).astype(BF16).astype(F32))
        one_kv = scale * (one_sums[0:1] + two_sums[1:2])
        row = iota((EDGE, 2 * kv), 0)
        tops = [
            two_ref[0:EDGE, :],
            jnp.where(row == 0, one_kv, one_ref[0:EDGE, :].astype(F32)).astype(BF16),
            jnp.where(row == 0, own_kv, own_ref[0:EDGE, :].astype(F32)).astype(BF16),
        ]
        for b, ref in enumerate((two_ref, one_ref, own_ref)):
            at = b * toks
            for g in range(kvh):
                cols = slice(g * hd, (g + 1) * hd)
                k_ref[g, at : at + EDGE, :] = tops[b][:, cols]
                k_ref[g, at + EDGE : at + toks, :] = ref[EDGE:toks, cols]
                cols = slice(kv + g * hd, kv + (g + 1) * hd)
                v_ref[g, at : at + EDGE, 0:hd] = tops[b][:, cols]
                v_ref[g, at + EDGE : at + toks, 0:hd] = ref[EDGE:toks, cols]
                v_ref[g, at : at + toks, hd:] = jnp.ones((toks, hd), BF16)
        row = iota((EDGE, hd), 0)
        query_ref[0:EDGE, :] = jnp.where(row == 0, own_lat, lat_ref[0:EDGE, :].astype(F32)).astype(BF16)
        query_ref[EDGE:, :] = lat_ref[EDGE:, :]
        for c in range(8):
            corr_ref[:, c * part : (c + 1) * part] = one_fold[8 + c : 9 + c]

    log_scale = math.log2(math.e) / math.sqrt(hd)
    group = step // (pl.num_programs(0) // kvh)
    query = (jnp.dot(query_ref[...], wq_ref[...], preferred_element_type=F32) * log_scale).astype(BF16)
    query = jnp.concatenate([query[:, h * hd : (h + 1) * hd] for h in range(heads)], axis=0)
    scores = lax.dot_general(
        query, k_ref[group], (((1,), (1,)), ((), ())), preferred_element_type=F32
    )
    scores = scores.reshape(heads, toks, keys) + bias_ref[...][None]
    top = jnp.max(scores, axis=2, keepdims=True)
    probs = jnp.exp2(scores - top).astype(BF16).reshape(heads * toks, keys)
    mixed = jnp.dot(probs, v_ref[group], preferred_element_type=F32)
    mixed = mixed[:, 0:hd] / mixed[:, hd:]
    mixed = jnp.concatenate([mixed[h * toks : (h + 1) * toks] for h in range(heads)], axis=1)
    wide = heads * hd
    cols = pl.ds(pl.multiple_of(step * wide, wide), wide)
    short = short_ref[...].astype(F32)
    whole = (short[0:EDGE] + corr_ref[:, cols]).astype(BF16).astype(F32)
    first = jnp.where(iota((EDGE, wide), 0) == 0, whole, short[0:EDGE])
    layer = (mixed + jnp.concatenate([first, short[EDGE:]], axis=0)).astype(BF16)
    placed = jnp.dot(pick_ref[...], layer, preferred_element_type=F32)
    placed = (placed + fill_ref[:, 0:1]).astype(BF16)
    if merged:
        block_refs[0][...] = placed
    else:
        for k in range(n_seq):
            block_refs[k][...] = placed[k * rows : (k + 1) * rows]


def gather_kernel(order, rows, pans, me_ref, *refs):
    n_out = 3
    block_refs, (acc_ref, last_ref, sel_ref) = refs[:-n_out], refs[-n_out:]
    toks = acc_ref.shape[0]
    n_seq = len(order)
    blocks = [r[...] for r in block_refs]
    got = blocks[0] if len(blocks) == 1 else jnp.concatenate(blocks, axis=0)
    step = pl.program_id(0)
    me = me_ref[0]

    @pl.when(step == 0)
    def _():
        n_pad = max(16, n_seq)
        used = jnp.where(got[:, 0:128].astype(F32) < 0.5 * MARK, 1.0, 0.0).astype(BF16)
        member = iota((n_pad, got.shape[0]), 0) == iota((n_pad, got.shape[0]), 1) // rows
        count = jnp.dot(jnp.where(member, 1.0, 0.0).astype(BF16), used, preferred_element_type=F32)
        rest = pans * PANEL - jnp.sum(count, axis=0, keepdims=True)
        place = iota((n_pad, 128), 0)
        count = jnp.where(place == n_seq - 1, rest, count)
        source = jnp.full((n_pad, 128), n_seq, jnp.int32)
        for q in range(n_seq):
            source = jnp.where(place == q, me ^ order[q], source)
        offset = jnp.zeros((n_pad, 128), F32)
        for q in range(n_seq):
            offset = offset + jnp.where(source > (me ^ order[q]), count[q : q + 1], 0.0)

        def targets(parts, wide):
            lane = iota((1, wide), 1)
            within = (lane % rows).astype(F32)
            target = jnp.full((1, wide), -1.0, F32)
            for i, q in enumerate(parts):
                valid = (lane // rows == i) & (within < count[q : q + 1, 0:1])
                target = jnp.where(valid, offset[q : q + 1, 0:1] + within, target)
            row = iota((toks, wide), 0).astype(F32)
            return jnp.where(row == target, 1.0, 0.0).astype(BF16)

        sel_ref[...] = targets(range(n_seq - 1), got.shape[0])
        last_ref[...] = targets([n_seq - 1], last_ref.shape[1])

    acc_ref[...] = jnp.dot(sel_ref[...], got, preferred_element_type=F32)


def finish_kernel(acc_ref, last_ref, block_ref, out_ref):
    out_ref[...] = (
        acc_ref[...] + jnp.dot(last_ref[...], block_ref[...], preferred_element_type=F32)
    ).astype(BF16)


def smem():
    return pl.BlockSpec(memory_space=pltpu.SMEM)


def vmem():
    return pl.BlockSpec(memory_space=pltpu.VMEM)


def hbm():
    return pl.BlockSpec(memory_space=pltpu.HBM)


def whole_block(shape):
    return pl.BlockSpec(shape, lambda i: (0,) * len(shape))


def column_block(rows, cols):
    return pl.BlockSpec((rows, cols), lambda i: (0, i))


def params(limit=VMEM_BYTES):
    return pltpu.CompilerParams(vmem_limit_bytes=limit)


def per_device(
    byte_embed, conv_taps, norm_gain, w_qdown, w_qup, w_key, w_value, doc_lengths, panel_dest
):
    n_seq = lax.axis_size("seq")
    me = lax.axis_index("seq").astype(jnp.int32).reshape(1)
    n_bytes, byte_dim = byte_embed.shape
    toks = n_bytes // SHORTEN
    width = SHORTEN * byte_dim
    hd = width // H
    kv = w_key.shape[1]
    kvh = kv // hd
    rank = w_qdown.shape[1]
    pans = toks // PANEL
    slots = (2 * pans + n_seq - 1) // n_seq
    rows = slots * PANEL
    merged = rows % 16 != 0
    keys = (BACK + 1) * toks
    held_rows = toks + 2 * EDGE

    held, short, latent, edge = pl.pallas_call(
        project_kernel,
        out_shape=[
            jax.ShapeDtypeStruct((held_rows, 2 * kv), BF16),
            jax.ShapeDtypeStruct((toks, width), BF16),
            jax.ShapeDtypeStruct((toks, rank), BF16),
            jax.ShapeDtypeStruct((8, 2 * kv + rank), F32),
        ],
        in_specs=[smem()] + [hbm()] * 7,
        out_specs=[vmem()] * 4,
        scratch_shapes=[
            pltpu.SMEM(doc_lengths.shape, jnp.int32),
            pltpu.VMEM((n_bytes, byte_dim), BF16),
            pltpu.VMEM((KCONV, byte_dim), F32),
            pltpu.VMEM((1, width), F32),
            pltpu.VMEM((width, 2 * kv + rank), BF16),
            pltpu.SemaphoreType.DMA((7,)),
            pltpu.SemaphoreType.DMA((SHORTEN, 3)),
            pltpu.VMEM((byte_dim // 128, n_bytes + 2 * PAD, 128), F32),
            pltpu.VMEM((toks + 8, 128), F32),
            pltpu.VMEM((toks + EDGE, width), BF16),
            pltpu.VMEM((toks + EDGE, 2 * kv + rank), F32),
            pltpu.VMEM((16, width // 8), F32),
        ],
        compiler_params=params(ALL_VMEM),
        name="project",
    )(me, doc_lengths, byte_embed, conv_taps, norm_gain.reshape(1, width), w_key, w_value, w_qdown)

    behind = [
        lax.ppermute(held, "seq", [(i, i + by) for i in range(n_seq - by)])
        for by in range(1, BACK + 1)
    ]

    bias, pick, fill = pl.pallas_call(
        functools.partial(plan_kernel, n_seq, rows),
        out_shape=[
            jax.ShapeDtypeStruct((toks, keys), F32),
            jax.ShapeDtypeStruct((n_seq * rows, toks), BF16),
            jax.ShapeDtypeStruct((n_seq * rows, 128), F32),
        ],
        in_specs=[smem()] * 3,
        out_specs=[vmem()] * 3,
        compiler_params=params(),
        name="plan",
    )(me, doc_lengths, panel_dest)

    heads = min(4, H // kvh)
    wide = heads * hd
    block_rows = n_seq * rows if merged else rows
    n_out = 1 if merged else n_seq
    blocks = pl.pallas_call(
        functools.partial(attend_kernel, n_seq, rows, merged),
        grid=(H // heads,),
        out_shape=[jax.ShapeDtypeStruct((block_rows, width), BF16)] * n_out,
        in_specs=[
            whole_block(latent.shape),
            whole_block(edge.shape),
            whole_block(held.shape),
            whole_block(held.shape),
            whole_block(held.shape),
            whole_block(bias.shape),
            whole_block(pick.shape),
            whole_block(fill.shape),
            column_block(rank, wide),
            column_block(toks, wide),
        ],
        out_specs=[column_block(block_rows, wide)] * n_out,
        scratch_shapes=[
            pltpu.VMEM((kvh, keys, hd), BF16),
            pltpu.VMEM((kvh, keys, 2 * hd), BF16),
            pltpu.VMEM((toks, rank), BF16),
            pltpu.VMEM((1, width), F32),
        ],
        compiler_params=params(),
        name="attend",
    )(latent, edge, held, behind[0], behind[1], bias, pick, fill, w_qup, short)
    if merged:
        blocks = [blocks[0][k * rows : (k + 1) * rows] for k in range(n_seq)]

    order = [0] + list(range(n_seq // 2, n_seq)) + list(range(1, n_seq // 2))
    got = [blocks[0]] + [
        lax.ppermute(blocks[k], "seq", [(i, i ^ k) for i in range(n_seq)]) for k in order[1:]
    ]
    last_at = n_seq // 2
    order = order[:last_at] + order[last_at + 1 :] + [order[last_at]]
    got = got[:last_at] + got[last_at + 1 :] + [got[last_at]]
    last = got.pop()
    if merged:
        got = [jnp.concatenate(got, axis=0)]
        last = jnp.pad(last, ((0, -rows % 16), (0, 0)))
    out_cols = width // 4
    n_rows = (n_seq - 1) * rows
    acc, sel = pl.pallas_call(
        functools.partial(gather_kernel, order, rows, pans),
        grid=(4,),
        out_shape=[
            jax.ShapeDtypeStruct((toks, width), F32),
            jax.ShapeDtypeStruct((toks, last.shape[0]), BF16),
        ],
        in_specs=[smem()] + [column_block(g.shape[0], out_cols) for g in got],
        out_specs=[column_block(toks, out_cols), whole_block((toks, last.shape[0]))],
        scratch_shapes=[pltpu.VMEM((toks, n_rows), BF16)],
        compiler_params=params(),
        name="gather",
    )(me, *got)
    return pl.pallas_call(
        finish_kernel,
        grid=(4,),
        out_shape=jax.ShapeDtypeStruct((toks, width), BF16),
        in_specs=[
            column_block(toks, out_cols),
            whole_block(sel.shape),
            column_block(last.shape[0], out_cols),
        ],
        out_specs=column_block(toks, out_cols),
        compiler_params=params(),
        name="finish",
    )(acc, sel, last)


def solution(mesh):
    in_specs = (P(("dp", "seq"), None), P(), P(), P(), P(), P(), P(), P("dp"), P(("dp", "seq")))
    out_specs = P(("dp", "seq"), None)
    return jax.shard_map(
        per_device, mesh=mesh, in_specs=in_specs, out_specs=out_specs, check_vma=False
    )
```

time: 133 us -> 82 us (0.62)
  the two profiles are of different devices: /device:TPU:0 before, /device:TPU:23 now
where the time goes in v2:
time: 82 us; the launch traced here: 81.7 us
  waiting for transfers between devices  36.4 us (44%)
  starting transfers between devices  21.2 us (26%)
  Pallas kernels  20.3 us (25%)
  local copies, waits for them, and re-layouts  3.64 us (4%)
    ppermute x7, waiting for transfers between devices, per_device(): lax.ppermute(blocks[k], 'seq', [(i, i ^ k) for i in range(n_seq)])  32.4 us
    ppermute x7, starting transfers between devices, per_device(): lax.ppermute(blocks[k], 'seq', [(i, i ^ k) for i in range(n_seq)])  16 us
    pallas_call x1, Pallas kernels, per_device(): pl.pallas_call(functools.partial(attend_kernel, n_seq, rows, merged), gri...  9.43 us
    pallas_call x1, Pallas kernels, per_device(): pl.pallas_call(project_kernel, out_shape=[jax.ShapeDtypeStruct((held_rows...  6.21 us
    ppermute x2, starting transfers between devices, per_device(): lax.ppermute(held, 'seq', [(i, i + by) for i in range(n_seq - by)])  5.12 us
    ppermute x2, waiting for transfers between devices, per_device(): lax.ppermute(held, 'seq', [(i, i + by) for i in range(n_seq - by)])  4.01 us
    unnamed x14, local copies, waits for them, and re-layouts  3.64 us
    pallas_call x1, Pallas kernels, per_device(): pl.pallas_call(finish_kernel, grid=(4,), out_shape=jax.ShapeDtypeStruct((...  2.17 us
  transfers between devices with their start and end apart: 9, of which 6 were waited for; matrix products, arithmetic and copies ran while one was open for 0% of the time, Pallas kernels for 3%

profile of v2, /device:TPU:23, one launch (start us, length us, event | category | flops | bytes accessed | tf_op | source)
XLA Modules:
  0.0 81.7 jit_solution(5922363632948705637)
XLA Ops:
  0.0 0.0 copy-start.5
  0.0 0.0 copy-start.6
  0.0 0.0 copy-start
  0.0 6.2 %project.1 = (bf16[160,512]{1,0:T(8,128)(2,1)}, bf16[128,4096]{1,0:T(8,128)(2,1)}, bf16[128,128]{1,0:T(8,128)(2,1)}, f32[8,640]{1,0:T(8,128)}) custom-call(s32[1]{0:T(128)} %bitcast.me_ref, s32[16]{0:T(128)} %lens_ref.1, bf16[512,1024]{1,0:T(8,128)(2,1)} %x_hbm.1, f32[4,1024]{1,0:T(4,128)} %taps_hbm.1, f32[1,4096]{1,0:T(1,128)} %bitcast.2, ...), custom_call_target="tpu_custom_call" | custom-call | tf_op jit(solution)/shard_map/project/pallas_call | solution.py:345
  6.2 3.2 %collective-permute-start.1 = (bf16[160,512]{1,0:T(8,128)(2,1)}, bf16[160,512]{1,0:T(8,128)(2,1)S(1)}, u32[]{:S(2)}, u32[]{:S(2)}) collective-permute-start(bf16[160,512]{1,0:T(8,128)(2,1)} %get-tuple-element.24.own_ref), channel_id=1, source_target_pairs={{0,2},{1,3},{2,4},{3,5},{4,6},{5,7},{8,10},{9,11},{10,12},{11,13},... | collective-permute-start | bytes 491528 | tf_op jit(solution)/shard_map/ppermute | solution.py:374
  9.4 1.9 %collective-permute-start = (bf16[160,512]{1,0:T(8,128)(2,1)}, bf16[160,512]{1,0:T(8,128)(2,1)S(1)}, u32[]{:S(2)}, u32[]{:S(2)}) collective-permute-start(bf16[160,512]{1,0:T(8,128)(2,1)} %get-tuple-element.24.own_ref), channel_id=1, source_target_pairs={{0,1},{1,2},{2,3},{3,4},{4,5},{5,6},{6,7},{8,9},{9,10},{10,11},{11... | collective-permute-start | bytes 491528 | tf_op jit(solution)/shard_map/ppermute | solution.py:374
  11.4 0.0 copy-done.5
  11.4 0.0 copy-done.6
  11.4 0.9 %plan.1 = (f32[128,384]{1,0:T(8,128)S(1)}, bf16[256,128]{1,0:T(8,128)(2,1)S(1)}, f32[256,128]{1,0:T(8,128)S(1)}) custom-call(s32[1]{0:T(128)} %bitcast.me_ref, s32[16]{0:T(128)S(1)} %copy-done.5, s32[32]{0:T(128)S(1)} %copy-done.6), custom_call_target="tpu_custom_call" | custom-call | tf_op jit(solution)/shard_map/plan/pallas_call | solution.py:378
  12.3 1.1 %collective-permute-done.1.two_ref = bf16[160,512]{1,0:T(8,128)(2,1)S(1)} collective-permute-done((bf16[160,512]{1,0:T(8,128)(2,1)}, bf16[160,512]{1,0:T(8,128)(2,1)S(1)}, u32[]{:S(2)}, u32[]{:S(2)}) %collective-permute-start.1) | collective-permute-done | bytes 163872 | tf_op jit(solution)/shard_map/ppermute | solution.py:374
  13.4 2.9 %collective-permute-done.one_ref = bf16[160,512]{1,0:T(8,128)(2,1)S(1)} collective-permute-done((bf16[160,512]{1,0:T(8,128)(2,1)}, bf16[160,512]{1,0:T(8,128)(2,1)S(1)}, u32[]{:S(2)}, u32[]{:S(2)}) %collective-permute-start) | collective-permute-done | bytes 163872 | tf_op jit(solution)/shard_map/ppermute | solution.py:374
  16.3 0.0 copy-done
  16.3 0.0 copy-start.1
  16.3 1.2 %copy-done.1 = bf16[128,4096]{1,0:T(8,128)(2,1)S(1)} copy-done((bf16[128,4096]{1,0:T(8,128)(2,1)S(1)}, bf16[128,4096]{1,0:T(8,128)(2,1)}, u32[]{:S(2)}) %copy-start.1) | copy-done | bytes 1048600
  17.5 0.0 copy-start.2
  17.5 0.9 %copy-done.2 = bf16[160,512]{1,0:T(8,128)(2,1)S(1)} copy-done((bf16[160,512]{1,0:T(8,128)(2,1)S(1)}, bf16[160,512]{1,0:T(8,128)(2,1)}, u32[]{:S(2)}) %copy-start.2) | copy-done | bytes 163864
  18.4 0.0 copy-start.3
  18.4 0.8 copy-done.3
  19.2 0.0 copy-start.4
  19.2 0.7 copy-done.4
  19.9 9.4 %attend.1 = (bf16[32,4096]{1,0:T(8,128)(2,1)S(1)}, bf16[32,4096]{1,0:T(8,128)(2,1)S(1)}, bf16[32,4096]{1,0:T(8,128)(2,1)S(1)}, bf16[32,4096]{1,0:T(8,128)(2,1)S(...) custom-call(bf16[128,128]{1,0:T(8,128)(2,1)S(1)} %copy-done.3, ...), custom_call_target="tpu_custom_call" | custom-call | tf_op jit(solution)/shard_map/attend/pallas_call | solution.py:395
  29.4 0.1 collective-permute-start.2
  29.5 3.9 %collective-permute-start.3 = (bf16[32,4096]{1,0:T(8,128)(2,1)S(1)}, bf16[32,4096]{1,0:T(8,128)(2,1)S(1)}, u32[]{:S(2)}, u32[]{:S(2)}) collective-permute-start(bf16[32,4096]{1,0:T(8,128)(2,1)S(1)} %get-tuple-element.31), channel_id=1, source_target_pairs={{0,5},{1,4},{2,7},{3,6},{4,1},{5,0},{6,3},{7,2},{8,13},{9,12},{10,... | collective-permute-start | bytes 786440 | tf_op jit(solution)/shard_map/ppermute | solution.py:426
  33.3 0.2 collective-permute-start.4
  33.5 0.2 collective-permute-start.5
  33.7 1.1 %collective-permute-start.6 = (bf16[32,4096]{1,0:T(8,128)(2,1)S(1)}, bf16[32,4096]{1,0:T(8,128)(2,1)S(1)}, u32[]{:S(2)}, u32[]{:S(2)}) collective-permute-start(bf16[32,4096]{1,0:T(8,128)(2,1)S(1)} %get-tuple-element.34), channel_id=1, source_target_pairs={{0,2},{1,3},{2,0},{3,1},{4,6},{5,7},{6,4},{7,5},{8,10},{9,11},{10,... | collective-permute-start | bytes 786440 | tf_op jit(solution)/shard_map/ppermute | solution.py:426
  34.8 16.5 %collective-permute-done.2.refs_1_ = bf16[32,4096]{1,0:T(8,128)(2,1)S(1)} collective-permute-done((bf16[32,4096]{1,0:T(8,128)(2,1)S(1)}, bf16[32,4096]{1,0:T(8,128)(2,1)S(1)}, u32[]{:S(2)}, u32[]{:S(2)}) %collective-permute-start.2) | collective-permute-done | bytes 262176 | tf_op jit(solution)/shard_map/ppermute | solution.py:426
  51.3 6.8 %collective-permute-start.7 = (bf16[32,4096]{1,0:T(8,128)(2,1)S(1)}, bf16[32,4096]{1,0:T(8,128)(2,1)S(1)}, u32[]{:S(2)}, u32[]{:S(2)}) collective-permute-start(bf16[32,4096]{1,0:T(8,128)(2,1)S(1)} %get-tuple-element.35), channel_id=1, source_target_pairs={{0,3},{1,2},{2,1},{3,0},{4,7},{5,6},{6,5},{7,4},{8,11},{9,10},{10,... | collective-permute-start | bytes 786440 | tf_op jit(solution)/shard_map/ppermute | solution.py:426
  58.1 0.0 collective-permute-done.3.refs_2_
  58.1 3.7 %collective-permute-start.8 = (bf16[32,4096]{1,0:T(8,128)(2,1)S(1)}, bf16[32,4096]{1,0:T(8,128)(2,1)S(1)}, u32[]{:S(2)}, u32[]{:S(2)}) collective-permute-start(bf16[32,4096]{1,0:T(8,128)(2,1)S(1)} %get-tuple-element.38), channel_id=1, source_target_pairs={{0,7},{1,6},{2,5},{3,4},{4,3},{5,2},{6,1},{7,0},{8,15},{9,14},{10,... | collective-permute-start | bytes 786440 | tf_op jit(solution)/shard_map/ppermute | solution.py:426
  61.9 1.9 %collective-permute-done.4.refs_3_ = bf16[32,4096]{1,0:T(8,128)(2,1)S(1)} collective-permute-done((bf16[32,4096]{1,0:T(8,128)(2,1)S(1)}, bf16[32,4096]{1,0:T(8,128)(2,1)S(1)}, u32[]{:S(2)}, u32[]{:S(2)}) %collective-permute-start.4) | collective-permute-done | bytes 262176 | tf_op jit(solution)/shard_map/ppermute | solution.py:426
  63.7 0.0 collective-permute-done.5.refs_4_
  63.8 0.0 collective-permute-done.6.refs_5_
  63.8 6.2 %collective-permute-done.7.refs_6_ = bf16[32,4096]{1,0:T(8,128)(2,1)S(1)} collective-permute-done((bf16[32,4096]{1,0:T(8,128)(2,1)S(1)}, bf16[32,4096]{1,0:T(8,128)(2,1)S(1)}, u32[]{:S(2)}, u32[]{:S(2)}) %collective-permute-start.7) | collective-permute-done | bytes 262176 | tf_op jit(solution)/shard_map/ppermute | solution.py:426
  70.0 1.6 %gather.1 = (f32[128,4096]{1,0:T(8,128)S(1)}, bf16[128,32]{1,0:T(8,128)(2,1)S(1)}) custom-call(s32[1]{0:T(128)} %bitcast.me_ref, bf16[32,4096]{1,0:T(8,128)(2,1)S(1)} %get-tuple-element.29.refs_0_, bf16[32,4096]{1,0:T(8,128)(2,1)S(1)} %collective-permute-done.2.refs_1_, bf16[32,4096]{1,0:T(8,128)(2,1)S(1)} %collective-permute-done.3.refs_2_, ...), custom_call_target="tpu_custom_call" | custom-call | tf_op jit(solution)/shard_map/gather/pallas_call | solution.py:437
  71.6 7.9 %collective-permute-done.8.block_ref = bf16[32,4096]{1,0:T(8,128)(2,1)S(1)} collective-permute-done((bf16[32,4096]{1,0:T(8,128)(2,1)S(1)}, bf16[32,4096]{1,0:T(8,128)(2,1)S(1)}, u32[]{:S(2)}, u32[]{:S(2)}) %collective-permute-start.8) | collective-permute-done | bytes 262176 | tf_op jit(solution)/shard_map/ppermute | solution.py:426
  79.5 2.2 %finish.1 = bf16[128,4096]{1,0:T(8,128)(2,1)} custom-call(f32[128,4096]{1,0:T(8,128)S(1)} %get-tuple-element.36.acc_ref, bf16[128,32]{1,0:T(8,128)(2,1)S(1)} %get-tuple-element.37.last_ref, bf16[32,4096]{1,0:T(8,128)(2,1)S(1)} %collective-permute-done.8.block_ref), custom_call_target="tpu_custom_call" | custom-call | tf_op jit(solution)/shard_map/finish/pallas_call | solution.py:450
Async XLA Ops:
  0.0 11.4 %copy-start.5 = (s32[16]{0:T(128)S(1)}, s32[16]{0:T(128)}, u32[]{:S(2)}) copy-start(s32[16]{0:T(128)} %lens_ref.1) | copy-start | bytes 196
  0.0 11.4 %copy-start.6 = (s32[32]{0:T(128)S(1)}, s32[32]{0:T(128)}, u32[]{:S(2)}) copy-start(s32[32]{0:T(128)} %dest_ref.1) | copy-start | bytes 388
  0.0 16.3 %copy-start = (bf16[128,4096]{1,0:T(8,128)(2,1)S(1)}, bf16[128,4096]{1,0:T(8,128)(2,1)}, u32[]{:S(2)}) copy-start(bf16[128,4096]{1,0:T(8,128)(2,1)} %wq_ref.1) | copy-start | bytes 3145732
  6.2 7.2 %collective-permute-start.1 = (bf16[160,512]{1,0:T(8,128)(2,1)}, bf16[160,512]{1,0:T(8,128)(2,1)S(1)}, u32[]{:S(2)}, u32[]{:S(2)}) collective-permute-start(bf16[160,512]{1,0:T(8,128)(2,1)} %get-tuple-element.24.own_ref), channel_id=1, source_target_pairs={{0,2},{1,3},{2,4},{3,5},{4,6},{5,7},{8,10},{9,11},{10,12},{11,13},... | collective-permute-start | bytes 491528 | tf_op jit(solution)/shard_map/ppermute | solution.py:374
  9.4 6.8 %collective-permute-start = (bf16[160,512]{1,0:T(8,128)(2,1)}, bf16[160,512]{1,0:T(8,128)(2,1)S(1)}, u32[]{:S(2)}, u32[]{:S(2)}) collective-permute-start(bf16[160,512]{1,0:T(8,128)(2,1)} %get-tuple-element.24.own_ref), channel_id=1, source_target_pairs={{0,1},{1,2},{2,3},{3,4},{4,5},{5,6},{6,7},{8,9},{9,10},{10,11},{11... | collective-permute-start | bytes 491528 | tf_op jit(solution)/shard_map/ppermute | solution.py:374
  16.3 1.2 %copy-start.1 = (bf16[128,4096]{1,0:T(8,128)(2,1)S(1)}, bf16[128,4096]{1,0:T(8,128)(2,1)}, u32[]{:S(2)}) copy-start(bf16[128,4096]{1,0:T(8,128)(2,1)} %get-tuple-element.28.short_ref) | copy-start | bytes 3145732
  17.5 0.9 %copy-start.2 = (bf16[160,512]{1,0:T(8,128)(2,1)S(1)}, bf16[160,512]{1,0:T(8,128)(2,1)}, u32[]{:S(2)}) copy-start(bf16[160,512]{1,0:T(8,128)(2,1)} %get-tuple-element.24.own_ref) | copy-start | bytes 491524
  18.4 0.8 copy-start.3
  19.2 0.7 copy-start.4
  29.4 21.9 %collective-permute-start.2 = (bf16[32,4096]{1,0:T(8,128)(2,1)S(1)}, bf16[32,4096]{1,0:T(8,128)(2,1)S(1)}, u32[]{:S(2)}, u32[]{:S(2)}) collective-permute-start(bf16[32,4096]{1,0:T(8,128)(2,1)S(1)} %get-tuple-element.30), channel_id=1, source_target_pairs={{0,4},{1,5},{2,6},{3,7},{4,0},{5,1},{6,2},{7,3},{8,12},{9,13},{10,... | collective-permute-start | bytes 786440 | tf_op jit(solution)/shard_map/ppermute | solution.py:426
  29.5 28.7 %collective-permute-start.3 = (bf16[32,4096]{1,0:T(8,128)(2,1)S(1)}, bf16[32,4096]{1,0:T(8,128)(2,1)S(1)}, u32[]{:S(2)}, u32[]{:S(2)}) collective-permute-start(bf16[32,4096]{1,0:T(8,128)(2,1)S(1)} %get-tuple-element.31), channel_id=1, source_target_pairs={{0,5},{1,4},{2,7},{3,6},{4,1},{5,0},{6,3},{7,2},{8,13},{9,12},{10,... | collective-permute-start | bytes 786440 | tf_op jit(solution)/shard_map/ppermute | solution.py:426
  33.3 30.4 %collective-permute-start.4 = (bf16[32,4096]{1,0:T(8,128)(2,1)S(1)}, bf16[32,4096]{1,0:T(8,128)(2,1)S(1)}, u32[]{:S(2)}, u32[]{:S(2)}) collective-permute-start(bf16[32,4096]{1,0:T(8,128)(2,1)S(1)} %get-tuple-element.32), channel_id=1, source_target_pairs={{0,6},{1,7},{2,4},{3,5},{4,2},{5,3},{6,0},{7,1},{8,14},{9,15},{10,... | collective-permute-start | bytes 786440 | tf_op jit(solution)/shard_map/ppermute | solution.py:426
  33.5 30.2 %collective-permute-start.5 = (bf16[32,4096]{1,0:T(8,128)(2,1)S(1)}, bf16[32,4096]{1,0:T(8,128)(2,1)S(1)}, u32[]{:S(2)}, u32[]{:S(2)}) collective-permute-start(bf16[32,4096]{1,0:T(8,128)(2,1)S(1)} %get-tuple-element.33), channel_id=1, source_target_pairs={{0,1},{1,0},{2,3},{3,2},{4,5},{5,4},{6,7},{7,6},{8,9},{9,8},{10,11... | collective-permute-start | bytes 786440 | tf_op jit(solution)/shard_map/ppermute | solution.py:426
  33.7 30.0 %collective-permute-start.6 = (bf16[32,4096]{1,0:T(8,128)(2,1)S(1)}, bf16[32,4096]{1,0:T(8,128)(2,1)S(1)}, u32[]{:S(2)}, u32[]{:S(2)}) collective-permute-start(bf16[32,4096]{1,0:T(8,128)(2,1)S(1)} %get-tuple-element.34), channel_id=1, source_target_pairs={{0,2},{1,3},{2,0},{3,1},{4,6},{5,7},{6,4},{7,5},{8,10},{9,11},{10,... | collective-permute-start | bytes 786440 | tf_op jit(solution)/shard_map/ppermute | solution.py:426
  51.3 18.7 %collective-permute-start.7 = (bf16[32,4096]{1,0:T(8,128)(2,1)S(1)}, bf16[32,4096]{1,0:T(8,128)(2,1)S(1)}, u32[]{:S(2)}, u32[]{:S(2)}) collective-permute-start(bf16[32,4096]{1,0:T(8,128)(2,1)S(1)} %get-tuple-element.35), channel_id=1, source_target_pairs={{0,3},{1,2},{2,1},{3,0},{4,7},{5,6},{6,5},{7,4},{8,11},{9,10},{10,... | collective-permute-start | bytes 786440 | tf_op jit(solution)/shard_map/ppermute | solution.py:426
  58.1 21.3 %collective-permute-start.8 = (bf16[32,4096]{1,0:T(8,128)(2,1)S(1)}, bf16[32,4096]{1,0:T(8,128)(2,1)S(1)}, u32[]{:S(2)}, u32[]{:S(2)}) collective-permute-start(bf16[32,4096]{1,0:T(8,128)(2,1)S(1)} %get-tuple-element.38), channel_id=1, source_target_pairs={{0,7},{1,6},{2,5},{3,4},{4,3},{5,2},{6,1},{7,0},{8,15},{9,14},{10,... | collective-permute-start | bytes 786440 | tf_op jit(solution)/shard_map/ppermute | solution.py:426

commit v3 on v2

v3 whole, which is shorter than its diff:
```python
import functools
import math

import jax
import jax.numpy as jnp
from jax import lax
from jax.experimental import pallas as pl
from jax.experimental.pallas import tpu as pltpu
from jax.sharding import PartitionSpec as P

H = 32
SHORTEN = 4
KCONV = 4
PANEL = 4
BACK = 2
PAD = 8
EDGE = 16
MARK = 2.0**120
BATCH = 8
MIB = 1024 * 1024
F32 = jnp.float32
BF16 = jnp.bfloat16


def iota(shape, dim):
    return lax.broadcasted_iota(jnp.int32, shape, dim)


def project_kernel(
    lens_hbm, x_hbm, taps_hbm, gain_hbm, wk_hbm, wv_hbm, wd_hbm,
    out_ref, short_ref, lat_ref, edge_ref,
    lens_ref, x_ref, taps_ref, gain_ref, w_ref, sems, wsems, wide_ref, keep_ref, u_ref, acc_ref, fold_ref,
):
    n_bytes, byte_dim = x_ref.shape
    toks, width = short_ref.shape
    kv = wk_hbm.shape[1]
    rank = wd_hbm.shape[1]
    me = lax.axis_index("seq")
    pieces = 2
    some = n_bytes // pieces
    large = [
        pltpu.make_async_copy(
            x_hbm.at[pl.ds(i * some, some)], x_ref.at[pl.ds(i * some, some)], sems.at[3 + i]
        )
        for i in range(pieces)
    ]
    small = [
        pltpu.make_async_copy(lens_hbm, lens_ref, sems.at[0]),
        pltpu.make_async_copy(taps_hbm, taps_ref, sems.at[1]),
        pltpu.make_async_copy(gain_hbm, gain_ref, sems.at[2]),
    ]
    weights = []
    for i in range(SHORTEN):
        at = pl.ds(i * byte_dim, byte_dim)
        weights.append(
            [
                pltpu.make_async_copy(wk_hbm.at[at], w_ref.at[at, pl.ds(0, kv)], wsems.at[i, 0]),
                pltpu.make_async_copy(wv_hbm.at[at], w_ref.at[at, pl.ds(kv, kv)], wsems.at[i, 1]),
                pltpu.make_async_copy(wd_hbm.at[at], w_ref.at[at, pl.ds(2 * kv, rank)], wsems.at[i, 2]),
            ]
        )
    for copy in small + large:
        copy.start()
    for c in range(byte_dim // 128):
        wide_ref[c, 0:PAD, :] = jnp.zeros((PAD, 128), F32)
        wide_ref[c, PAD + n_bytes :, :] = jnp.zeros((PAD, 128), F32)
    u_ref[toks:, :] = jnp.zeros((EDGE, width), BF16)
    for copy in small:
        copy.wait()
    token = me * toks + iota((toks + 8, 128), 0)

    def doc(d, carry):
        first, keep = carry
        return first + lens_ref[d], jnp.where(token == first, 0.0, keep)

    _, keep = lax.fori_loop(
        0, lens_ref.shape[0], doc, (jnp.int32(0), jnp.ones((toks + 8, 128), F32))
    )
    keep_ref[...] = keep
    for i, copy in enumerate(large):
        copy.wait()
        if i == 0:
            for group in weights:
                for one in group:
                    one.start()
        for c in range(byte_dim // 128):
            wide_ref[c, PAD + i * some : PAD + (i + 1) * some, :] = x_ref[
                i * some : (i + 1) * some, c * 128 : (c + 1) * 128
            ].astype(F32)

    part = width // 8
    squares = [jnp.zeros((toks, 128), F32)]

    def conv(slot):
        for c in range(byte_dim // 128):
            cols = slice(c * 128, (c + 1) * 128)
            at = slot * byte_dim + c * 128
            here = jnp.zeros((toks, 128), F32)
            before = jnp.zeros((toks, 128), F32)
            corr = jnp.zeros((1, 128), F32)
            for tap in range(KCONV):
                weight = taps_ref[tap : tap + 1, cols]
                term = wide_ref[c, pl.ds(PAD + slot - tap, toks, stride=SHORTEN), :] * weight
                if tap > slot:
                    before = before + term
                    spot = PAD + n_bytes + slot - tap
                    corr = corr + wide_ref[c, spot : spot + 1, :] * weight
                else:
                    here = here + term
            if slot < KCONV - 1:
                here = here + before * keep_ref[0:toks, :]
                corr = corr * keep_ref[toks : toks + 1, :]
            short = here.astype(BF16)
            short_ref[:, at : at + 128] = short
            short = short.astype(F32)
            squares[0] = squares[0] + short * short
            gain = gain_ref[:, at : at + 128]
            u_ref[0:toks, at : at + 128] = (short * gain).astype(BF16)
            row = iota((EDGE, 128), 0)
            u_ref[toks:, at : at + 128] = jnp.where(row == 0, corr * gain, 0.0).astype(BF16)
            r, o = at // part, at % part
            fold_ref[r : r + 1, o : o + 128] = short[0:1]
            fold_ref[8 + r : 9 + r, o : o + 128] = corr

    def project(slot):
        for copy in weights[slot]:
            copy.wait()
        span = slice(slot * byte_dim, (slot + 1) * byte_dim)
        got = jnp.dot(u_ref[:, span], w_ref[span, :], preferred_element_type=F32)
        if slot == 0:
            acc_ref[...] = got
        else:
            acc_ref[...] += got

    conv(0)
    for slot in range(1, SHORTEN):
        conv(slot)
        project(slot - 1)
    project(SHORTEN - 1)
    rs = lax.rsqrt(jnp.sum(squares[0], axis=1, keepdims=True) * (1.0 / width) + 1e-06)
    out_ref[0:toks, :] = (acc_ref[0:toks, 0 : 2 * kv] * rs).astype(BF16)
    lat_ref[...] = (acc_ref[0:toks, 2 * kv :] * rs).astype(BF16)
    edge_ref[...] = acc_ref[0:8, :]
    row = iota((EDGE, 2 * kv), 0)
    low = jnp.concatenate(
        [acc_ref[toks : toks + 1, 2 * kv :], jnp.zeros((1, 2 * kv - rank), F32)], axis=1
    )
    sums = jnp.where(row == 0, acc_ref[0:1, 0 : 2 * kv], 0.0)
    sums = jnp.where(row == 1, acc_ref[toks : toks + 1, 0 : 2 * kv], sums)
    out_ref[toks : toks + EDGE, :] = jnp.where(row == 2, low, sums).astype(BF16)
    out_ref[toks + EDGE : toks + 2 * EDGE, 0:part] = fold_ref[...].astype(BF16)


def plan_kernel(n_seq, rows, lens_ref, dest_ref, bias_ref, pick_ref):
    toks, keys = bias_ref.shape
    me = lax.axis_index("seq")
    pos = me * toks + iota((toks, 128), 0)

    def doc(d, carry):
        first, begin = carry
        return first + lens_ref[d], jnp.where(pos >= first, first, begin)

    _, begin = lax.fori_loop(
        0, lens_ref.shape[0], doc, (jnp.int32(0), jnp.zeros((toks, 128), jnp.int32))
    )
    for at in range(0, keys, 128):
        key = (me - BACK) * toks + at + iota((toks, 128), 1)
        bias_ref[:, at : at + 128] = jnp.where((key >= begin) & (key <= pos), 0.0, -1e30)
    lane = iota((8, toks), 1)
    panel = lane // PANEL
    dest = jnp.full((8, toks), -1, jnp.int32)
    for p in range(toks // PANEL):
        dest = jnp.where(panel == p, dest_ref[p], dest)
    rank = jnp.zeros((8, toks), jnp.int32)
    for p in range(toks // PANEL):
        rank = rank + jnp.where((panel > p) & (dest == dest_ref[p]), 1, 0)
    place = (dest ^ me) * rows + rank * PANEL + lane % PANEL
    row = iota((n_seq * rows, toks), 0)
    pick_ref[...] = jnp.where(row == place[0:1], 1.0, 0.0).astype(BF16)


def put_blocks(pick, layer, refs):
    empty = (1.0 - jnp.sum(pick.astype(F32), axis=1, keepdims=True)) * MARK
    placed = (jnp.dot(pick, layer, preferred_element_type=F32) + empty).astype(BF16)
    rows = refs[0].shape[0]
    for k, ref in enumerate(refs):
        ref[...] = placed[k * rows : (k + 1) * rows]


def attend_kernel(half, batch, lat_ref, edge_ref, own_ref, one_ref, two_ref, bias_ref, pick_ref, wq_ref, short_ref, *refs):
    refs, (k_ref, v_ref, query_ref, corr_ref, layer_ref) = refs[:-5], refs[-5:]
    if half == 0:
        cross_refs, out_layer_ref = refs[:-1], refs[-1]
    else:
        past_ref, refs = refs[0], refs[1:]
        cross_refs, near_refs = refs[: len(refs) // 2], refs[len(refs) // 2 :]
    toks, hd = lat_ref.shape
    wide = layer_ref.shape[1]
    heads = wide // hd
    kv = own_ref.shape[1] // 2
    part = own_ref.shape[1]
    width = 8 * part
    keys = bias_ref.shape[1]

    def root(first):
        total = jnp.sum(jnp.sum(first * first, axis=1, keepdims=True), axis=0, keepdims=True)
        return lax.rsqrt(total * (1.0 / width) + 1e-06)

    fold = slice(toks + EDGE, toks + 2 * EDGE)
    sums = slice(toks, toks + EDGE)
    own_fold = own_ref[fold, :].astype(F32)
    one_fold = one_ref[fold, :].astype(F32)
    two_fold = two_ref[fold, :].astype(F32)
    one_sums = one_ref[sums, :].astype(F32)
    two_sums = two_ref[sums, :].astype(F32)
    scale = root((own_fold[0:8] + one_fold[8:16]).astype(BF16).astype(F32))
    own_kv = scale * (edge_ref[0:1, 0 : 2 * kv] + one_sums[1:2])
    own_lat = scale * (edge_ref[0:1, 2 * kv :] + one_sums[2:3, 0:hd])
    scale = root((one_fold[0:8] + two_fold[8:16]).astype(BF16).astype(F32))
    one_kv = scale * (one_sums[0:1] + two_sums[1:2])
    row = iota((EDGE, 2 * kv), 0)
    tops = [
        two_ref[0:EDGE, :],
        jnp.where(row == 0, one_kv, one_ref[0:EDGE, :].astype(F32)).astype(BF16),
        jnp.where(row == 0, own_kv, own_ref[0:EDGE, :].astype(F32)).astype(BF16),
    ]
    k_cols = slice(half * hd, (half + 1) * hd)
    v_cols = slice(kv + half * hd, kv + (half + 1) * hd)
    for b, ref in enumerate((two_ref, one_ref, own_ref)):
        at = b * toks
        k_ref[at : at + EDGE, :] = tops[b][:, k_cols]
        k_ref[at + EDGE : at + toks, :] = ref[EDGE:toks, k_cols]
        v_ref[at : at + EDGE, 0:hd] = tops[b][:, v_cols]
        v_ref[at + EDGE : at + toks, 0:hd] = ref[EDGE:toks, v_cols]
        v_ref[at : at + toks, hd:] = jnp.ones((toks, hd), BF16)
    row = iota((EDGE, hd), 0)
    query_ref[0:EDGE, :] = jnp.where(row == 0, own_lat, lat_ref[0:EDGE, :].astype(F32)).astype(BF16)
    query_ref[EDGE:, :] = lat_ref[EDGE:, :]
    for c in range(wide // part):
        at = half * (wide // part) + c
        corr_ref[:, c * part : (c + 1) * part] = one_fold[8 + at : 9 + at]

    log_scale = math.log2(math.e) / math.sqrt(hd)
    wq = wq_ref[:, half * wide : (half + 1) * wide]
    query = (jnp.dot(query_ref[...], wq, preferred_element_type=F32) * log_scale).astype(BF16)
    key_all, value_all = k_ref[...], v_ref[...]
    for at in range(0, heads, batch):
        part_q = [query[:, h * hd : (h + 1) * hd] for h in range(at, at + batch)]
        scores = lax.dot_general(
            jnp.concatenate(part_q, axis=0), key_all, (((1,), (1,)), ((), ())), preferred_element_type=F32
        )
        scores = scores.reshape(batch, toks, keys) + bias_ref[...][None]
        top = jnp.max(scores, axis=2, keepdims=True)
        probs = jnp.exp2(scores - top).astype(BF16).reshape(batch * toks, keys)
        mixed = jnp.dot(probs, value_all, preferred_element_type=F32)
        mixed = mixed[:, 0:hd] / mixed[:, hd:]
        for h in range(batch):
            cols = slice((at + h) * hd, (at + h + 1) * hd)
            short = short_ref[:, half * wide + (at + h) * hd : half * wide + (at + h + 1) * hd].astype(F32)
            whole = (short[0:8] + corr_ref[:, cols]).astype(BF16).astype(F32)
            first = jnp.where(iota((8, hd), 0) == 0, whole, short[0:8])
            short = jnp.concatenate([first, short[8:]], axis=0)
            layer_ref[:, cols] = (mixed[h * toks : (h + 1) * toks] + short).astype(BF16)
    middle = pick_ref.shape[0] // 2
    put_blocks(pick_ref[middle:, :], layer_ref[...], cross_refs)
    if half == 0:
        out_layer_ref[...] = layer_ref[...]
    else:
        layer = jnp.concatenate([past_ref[...], layer_ref[...]], axis=1)
        put_blocks(pick_ref[0:middle, :], layer, near_refs)


def first_kernel(n_seq, rows, *refs):
    block_refs, (out_ref, sel_ref, pick_ref) = refs[:-3], refs[-3:]
    toks = out_ref.shape[0]
    got = jnp.concatenate([r[...] for r in block_refs], axis=0)
    me = lax.axis_index("seq")

    @pl.when(pl.program_id(0) == 0)
    def _():
        n_pad = max(16, n_seq)
        n_rows = got.shape[0]
        used = jnp.where(got[:, 0:128].astype(F32) < 0.5 * MARK, 1.0, 0.0).astype(BF16)
        member = iota((n_pad, n_rows), 0) == iota((n_pad, n_rows), 1) // rows
        count = jnp.dot(jnp.where(member, 1.0, 0.0).astype(BF16), used, preferred_element_type=F32)
        source = me ^ iota((n_pad, 128), 0)
        offset = jnp.zeros((n_pad, 128), F32)
        for q in range(n_seq):
            offset = offset + jnp.where(source > (me ^ q), count[q : q + 1], 0.0)
        lane = iota((1, n_rows), 1)
        within = (lane % rows).astype(F32)
        target = jnp.full((1, n_rows), -1.0, F32)
        for q in range(n_seq):
            valid = (lane // rows == q) & (within < count[q : q + 1, 0:1])
            target = jnp.where(valid, offset[q : q + 1, 0:1] + within, target)
        row = iota((toks, n_rows), 0).astype(F32)
        pick_ref[...] = jnp.where(row == target, 1.0, 0.0).astype(BF16)
        sel_ref[...] = pick_ref[...]

    out_ref[...] = jnp.dot(pick_ref[...], got, preferred_element_type=F32).astype(BF16)


def second_kernel(sel_ref, *refs):
    block_refs, out_ref = refs[:-2], refs[-1]
    got = jnp.concatenate([r[...] for r in block_refs], axis=0)
    out_ref[...] = jnp.dot(sel_ref[...], got, preferred_element_type=F32).astype(BF16)


def swap(array, by, size):
    return lax.ppermute(array, "seq", [(i, i ^ by) for i in range(size)])


def smem():
    return pl.BlockSpec(memory_space=pltpu.SMEM)


def vmem():
    return pl.BlockSpec(memory_space=pltpu.VMEM)


def hbm():
    return pl.BlockSpec(memory_space=pltpu.HBM)


def in_hbm(array):
    return pltpu.with_memory_space_constraint(array, pltpu.HBM)


def whole_block(shape):
    return pl.BlockSpec(shape, lambda i: (0,) * len(shape))


def column_block(rows, cols):
    return pl.BlockSpec((rows, cols), lambda i: (0, i))


def params(limit=32 * MIB):
    return pltpu.CompilerParams(vmem_limit_bytes=limit)


def per_device(
    byte_embed, conv_taps, norm_gain, w_qdown, w_qup, w_key, w_value, doc_lengths, panel_dest
):
    n_seq = lax.axis_size("seq")
    n_bytes, byte_dim = byte_embed.shape
    toks = n_bytes // SHORTEN
    width = SHORTEN * byte_dim
    hd = width // H
    kv = w_key.shape[1]
    kvh = kv // hd
    rank = w_qdown.shape[1]
    pans = toks // PANEL
    slots = (2 * pans + n_seq - 1) // n_seq
    rows = slots * PANEL
    merged = rows % 16 != 0
    keys = (BACK + 1) * toks
    held_rows = toks + 2 * EDGE

    held, short, latent, edge = pl.pallas_call(
        project_kernel,
        out_shape=[
            pltpu.VMEM((held_rows, 2 * kv), BF16),
            pltpu.VMEM((toks, width), BF16),
            pltpu.VMEM((toks, rank), BF16),
            pltpu.VMEM((8, 2 * kv + rank), F32),
        ],
        in_specs=[hbm()] * 7,
        out_specs=[vmem()] * 4,
        scratch_shapes=[
            pltpu.SMEM(doc_lengths.shape, jnp.int32),
            pltpu.VMEM((n_bytes, byte_dim), BF16),
            pltpu.VMEM((KCONV, byte_dim), F32),
            pltpu.VMEM((1, width), F32),
            pltpu.VMEM((width, 2 * kv + rank), BF16),
            pltpu.SemaphoreType.DMA((5,)),
            pltpu.SemaphoreType.DMA((SHORTEN, 3)),
            pltpu.VMEM((byte_dim // 128, n_bytes + 2 * PAD, 128), F32),
            pltpu.VMEM((toks + 8, 128), F32),
            pltpu.VMEM((toks + EDGE, width), BF16),
            pltpu.VMEM((toks + EDGE, 2 * kv + rank), F32),
            pltpu.VMEM((16, width // 8), F32),
        ],
        compiler_params=params(24 * MIB),
        name="project",
    )(
        *[
            in_hbm(a)
            for a in (
                doc_lengths, byte_embed, conv_taps, norm_gain.reshape(1, width), w_key, w_value, w_qdown
            )
        ]
    )

    behind = [
        lax.ppermute(held, "seq", [(i, i + by) for i in range(n_seq - by)])
        for by in range(1, BACK + 1)
    ]

    bias, pick = pl.pallas_call(
        functools.partial(plan_kernel, n_seq, rows),
        out_shape=[
            pltpu.VMEM((toks, keys), F32),
            pltpu.VMEM((n_seq * rows, toks), BF16),
        ],
        in_specs=[smem()] * 2,
        out_specs=[vmem()] * 2,
        compiler_params=params(),
        name="plan",
    )(doc_lengths, panel_dest)

    middle = n_seq // 2
    span = width // kvh
    batch = BATCH
    n_out, out_rows = (1, middle * rows) if merged else (middle, rows)

    def split(blocks):
        if merged:
            return [blocks[0][k * rows : (k + 1) * rows] for k in range(middle)]
        return list(blocks)

    def attend(half, more):
        cross = [pltpu.VMEM((out_rows, span), BF16)] * n_out
        near = [pltpu.VMEM((out_rows, width), BF16)] * n_out
        outs = cross + ([pltpu.VMEM((toks, span), BF16)] if half == 0 else near)
        operands = [latent, edge, held, *behind, bias, pick, w_qup, short, *more]
        return pl.pallas_call(
            functools.partial(attend_kernel, half, batch),
            out_shape=outs,
            in_specs=[vmem()] * len(operands),
            out_specs=[vmem()] * len(outs),
            scratch_shapes=[
                pltpu.VMEM((keys, hd), BF16),
                pltpu.VMEM((keys, 2 * hd), BF16),
                pltpu.VMEM((toks, rank), BF16),
                pltpu.VMEM((1, span), F32),
                pltpu.VMEM((toks, span), BF16),
            ],
            compiler_params=params(),
            name=f"attend_half_{half}",
        )(*operands)

    *first_cross, layer = attend(0, [])
    got_first = [swap(x, middle + k, n_seq) for k, x in enumerate(split(first_cross))]
    outs = attend(1, [layer])
    got_second = [swap(x, middle + k, n_seq) for k, x in enumerate(split(outs[:n_out]))]
    near = split(outs[n_out:])
    got_near = [near[0]] + [swap(near[k], k, n_seq) for k in range(1, middle)]
    if merged:
        got_first, got_second, got_near = (
            [jnp.concatenate(g, axis=0)] for g in (got_first, got_second, got_near)
        )

    steps = 4
    cols = span // steps

    def columns(arrays, start):
        return [pl.BlockSpec((a.shape[0], cols), lambda i: (0, start + i)) for a in arrays]

    out, sel = pl.pallas_call(
        functools.partial(first_kernel, n_seq, rows),
        grid=(steps,),
        out_shape=[
            jax.ShapeDtypeStruct((toks, width), BF16),
            jax.ShapeDtypeStruct((toks, n_seq * rows), BF16),
        ],
        in_specs=columns(got_near, 0) + columns(got_first, 0),
        out_specs=[
            pl.BlockSpec((toks, cols), lambda i: (0, i)),
            whole_block((toks, n_seq * rows)),
        ],
        scratch_shapes=[pltpu.VMEM((toks, n_seq * rows), BF16)],
        compiler_params=params(),
        name="place_first",
    )(*got_near, *got_first)
    operands = [sel, *got_near, *got_second, out]
    return pl.pallas_call(
        second_kernel,
        grid=(steps,),
        out_shape=jax.ShapeDtypeStruct((toks, width), BF16),
        in_specs=[whole_block(sel.shape)]
        + columns(got_near, steps)
        + columns(got_second, 0)
        + [pl.BlockSpec(memory_space=pl.ANY)],
        out_specs=pl.BlockSpec((toks, cols), lambda i: (0, steps + i)),
        input_output_aliases={len(operands) - 1: 0},
        compiler_params=params(),
        name="place_second",
    )(*operands)


def solution(mesh):
    in_specs = (P(("dp", "seq"), None), P(), P(), P(), P(), P(), P(), P("dp"), P(("dp", "seq")))
    out_specs = P(("dp", "seq"), None)
    return jax.shard_map(
        per_device, mesh=mesh, in_specs=in_specs, out_specs=out_specs, check_vma=False
    )
```

time: 82 us -> 70.3 us (0.86)
  Pallas kernels: 20.3 us -> 14.4 us
  local copies, waits for them, and re-layouts: 3.64 us -> 0.01 us
  starting transfers between devices: 21.2 us -> 19.5 us
    pallas_call x5 -> x6, Pallas kernels: 20.3 us -> 14.4 us  [the longest x1 4.66 us: per_device(): pl.pallas_call(project_kernel, out_shape=[pltpu.VMEM((held_rows, 2 * kv),...]
    unnamed x14 -> x6, local copies, waits for them, and re-layouts: 3.64 us -> 0.01 us
    ppermute x7 -> x11, starting transfers between devices: 16 us -> 14.4 us  [swap(): return lax.ppermute(array, 'seq', [(i, i ^ by) for i in range(size)])]
    ppermute x7 -> x11, waiting for transfers between devices: 32.4 us -> 32.1 us  [swap(): return lax.ppermute(array, 'seq', [(i, i ^ by) for i in range(size)])]
  transfers between devices with their start and end apart: 9 -> 13, of which waited for: 6 -> 8; matrix products, arithmetic and copies ran while one was open for 0% -> 0% of each run, Pallas kernels for 3% -> 8%
where the time goes in v3:
time: 70.3 us; the launch traced here: 70.1 us
  waiting for transfers between devices  36 us (51%)
  starting transfers between devices  19.5 us (28%)
  Pallas kernels  14.4 us (20%)
    ppermute x11, waiting for transfers between devices, swap(): return lax.ppermute(array, 'seq', [(i, i ^ by) for i in range(size)])  32.1 us
    ppermute x11, starting transfers between devices, swap(): return lax.ppermute(array, 'seq', [(i, i ^ by) for i in range(size)])  14.4 us
    ppermute x2, starting transfers between devices, per_device(): lax.ppermute(held, 'seq', [(i, i + by) for i in range(n_seq - by)])  5.12 us
    pallas_call x1, Pallas kernels, per_device(): pl.pallas_call(project_kernel, out_shape=[pltpu.VMEM((held_rows, 2 * kv),...  4.66 us
    pallas_call x2, Pallas kernels, attend(): pl.pallas_call(functools.partial(attend_kernel, half, batch), out_shape=o...  4.61 us
    ppermute x2, waiting for transfers between devices, per_device(): lax.ppermute(held, 'seq', [(i, i + by) for i in range(n_seq - by)])  3.88 us
    pallas_call x1, Pallas kernels, per_device(): pl.pallas_call(functools.partial(first_kernel, n_seq, rows), grid=(steps,...  2.34 us
    pallas_call x1, Pallas kernels, per_device(): pl.pallas_call(second_kernel, grid=(steps,), out_shape=jax.ShapeDtypeStru...  2.02 us
  transfers between devices with their start and end apart: 13, of which 8 were waited for; matrix products, arithmetic and copies ran while one was open for 0% of the time, Pallas kernels for 8%

profile of v3, /device:TPU:23, one launch (start us, length us, event | category | flops | bytes accessed | tf_op | source)
XLA Modules:
  0.0 70.1 jit_solution(12981575997792761482)
XLA Ops:
  0.0 0.0 copy-start.1
  0.0 0.0 copy-start.2
  0.0 0.0 copy-start
  0.0 4.7 %project.1 = (bf16[160,512]{1,0:T(8,128)(2,1)S(1)}, bf16[128,4096]{1,0:T(8,128)(2,1)S(1)}, bf16[128,128]{1,0:T(8,128)(2,1)S(1)}, f32[8,640]{1,0:T(8,128)S(1)}) custom-call(s32[16]{0:T(128)} %lens_ref.1, bf16[512,1024]{1,0:T(8,128)(2,1)} %x_hbm.1, f32[4,1024]{1,0:T(4,128)} %taps_hbm.1, f32[1,4096]{1,0:T(1,128)} %bitcast.1, bf16[4096,256]{1,0:T(8,128)(2,1)} %wk_hbm.1, ...), custom_call_target="tpu_custom_call" | custom-call | tf_op jit(solution)/shard_map/project/pallas_call | solution.py:359
  4.7 3.2 %collective-permute-start.1 = (bf16[160,512]{1,0:T(8,128)(2,1)S(1)}, bf16[160,512]{1,0:T(8,128)(2,1)S(1)}, u32[]{:S(2)}, u32[]{:S(2)}) collective-permute-start(bf16[160,512]{1,0:T(8,128)(2,1)S(1)} %get-tuple-element.28.own_ref), channel_id=1, source_target_pairs={{0,2},{1,3},{2,4},{3,5},{4,6},{5,7},{8,10},{9,11},{10,12},{11,13},... | collective-permute-start | bytes 491528 | tf_op jit(solution)/shard_map/ppermute | solution.py:395
  7.9 1.9 %collective-permute-start = (bf16[160,512]{1,0:T(8,128)(2,1)S(1)}, bf16[160,512]{1,0:T(8,128)(2,1)S(1)}, u32[]{:S(2)}, u32[]{:S(2)}) collective-permute-start(bf16[160,512]{1,0:T(8,128)(2,1)S(1)} %get-tuple-element.28.own_ref), channel_id=1, source_target_pairs={{0,1},{1,2},{2,3},{3,4},{4,5},{5,6},{6,7},{8,9},{9,10},{10,11},{11... | collective-permute-start | bytes 491528 | tf_op jit(solution)/shard_map/ppermute | solution.py:395
  9.8 0.0 copy-done.1
  9.8 0.0 copy-done.2
  9.8 0.8 %plan.1 = (f32[128,384]{1,0:T(8,128)S(1)}, bf16[256,128]{1,0:T(8,128)(2,1)S(1)}) custom-call(s32[16]{0:T(128)S(1)} %copy-done.1, s32[32]{0:T(128)S(1)} %copy-done.2), custom_call_target="tpu_custom_call" | custom-call | tf_op jit(solution)/shard_map/plan/pallas_call | solution.py:399
  10.6 1.0 %collective-permute-done.1.two_ref = bf16[160,512]{1,0:T(8,128)(2,1)S(1)} collective-permute-done((bf16[160,512]{1,0:T(8,128)(2,1)S(1)}, bf16[160,512]{1,0:T(8,128)(2,1)S(1)}, u32[]{:S(2)}, u32[]{:S(2)}) %collective-permute-start.1) | collective-permute-done | bytes 163872 | tf_op jit(solution)/shard_map/ppermute | solution.py:395
  11.6 2.9 %collective-permute-done.one_ref = bf16[160,512]{1,0:T(8,128)(2,1)S(1)} collective-permute-done((bf16[160,512]{1,0:T(8,128)(2,1)S(1)}, bf16[160,512]{1,0:T(8,128)(2,1)S(1)}, u32[]{:S(2)}, u32[]{:S(2)}) %collective-permute-start) | collective-permute-done | bytes 163872 | tf_op jit(solution)/shard_map/ppermute | solution.py:395
  14.5 0.0 copy-done
  14.5 2.1 %attend_half_0.1 = (bf16[32,2048]{1,0:T(8,128)(2,1)S(1)}, bf16[32,2048]{1,0:T(8,128)(2,1)S(1)}, bf16[32,2048]{1,0:T(8,128)(2,1)S(1)}, bf16[32,2048]{1,0:T(8,128)(2,1)S(1)}, bf16[128,2048]{1,0:T(8,128)(2,1)S(1)}) custom-call(bf16[128,128]{1,0:T(8,128)(2,1)S(1)} %get-tuple-element.26.lat_ref, f32[8,640]{1,0:T(8,128)S(1)} %get-tuple-element.27.edge_ref, ...), custom_call_target="tpu_custom_call" | custom-call | tf_op jit(solution)/shard_map/attend_half_0/pallas_call | solution.py:426
  16.6 0.1 collective-permute-start.5
  16.7 3.8 %collective-permute-start.6 = (bf16[32,2048]{1,0:T(8,128)(2,1)S(1)}, bf16[32,2048]{1,0:T(8,128)(2,1)S(1)}, u32[]{:S(2)}, u32[]{:S(2)}) collective-permute-start(bf16[32,2048]{1,0:T(8,128)(2,1)S(1)} %get-tuple-element.38), channel_id=1, source_target_pairs={{0,5},{1,4},{2,7},{3,6},{4,1},{5,0},{6,3},{7,2},{8,13},{9,12},{10,... | collective-permute-start | bytes 393224 | tf_op jit(solution)/shard_map/ppermute | solution.py:310
  20.6 2.5 %attend_half_1.1 = (bf16[32,2048]{1,0:T(8,128)(2,1)S(1)}, bf16[32,2048]{1,0:T(8,128)(2,1)S(1)}, bf16[32,2048]{1,0:T(8,128)(2,1)S(1)}, bf16[32,2048]{1,0:T(8,128)...) custom-call(bf16[128,128]{1,0:T(8,128)(2,1)S(1)} %get-tuple-element., ...), custom_call_target="tpu_custom_call" | custom-call | tf_op jit(solution)/shard_map/attend_half_1/pallas_call | solution.py:426
  23.1 0.1 collective-permute-start.2
  23.2 1.3 %collective-permute-start.3 = (bf16[32,4096]{1,0:T(8,128)(2,1)S(1)}, bf16[32,4096]{1,0:T(8,128)(2,1)S(1)}, u32[]{:S(2)}, u32[]{:S(2)}) collective-permute-start(bf16[32,4096]{1,0:T(8,128)(2,1)S(1)} %get-tuple-element.35), channel_id=1, source_target_pairs={{0,2},{1,3},{2,0},{3,1},{4,6},{5,7},{6,4},{7,5},{8,10},{9,11},{10,... | collective-permute-start | bytes 786440 | tf_op jit(solution)/shard_map/ppermute | solution.py:310
  24.5 0.0 collective-permute-start.7
  24.5 0.0 collective-permute-done.5.refs_4_
  24.5 4.9 %collective-permute-start.8 = (bf16[32,2048]{1,0:T(8,128)(2,1)S(1)}, bf16[32,2048]{1,0:T(8,128)(2,1)S(1)}, u32[]{:S(2)}, u32[]{:S(2)}) collective-permute-start(bf16[32,2048]{1,0:T(8,128)(2,1)S(1)} %get-tuple-element.40), channel_id=1, source_target_pairs={{0,7},{1,6},{2,5},{3,4},{4,3},{5,2},{6,1},{7,0},{8,15},{9,14},{10,... | collective-permute-start | bytes 393224 | tf_op jit(solution)/shard_map/ppermute | solution.py:310
  29.5 0.0 collective-permute-done.6.refs_5_
  29.5 1.9 %collective-permute-start.4 = (bf16[32,4096]{1,0:T(8,128)(2,1)S(1)}, bf16[32,4096]{1,0:T(8,128)(2,1)S(1)}, u32[]{:S(2)}, u32[]{:S(2)}) collective-permute-start(bf16[32,4096]{1,0:T(8,128)(2,1)S(1)} %get-tuple-element.36), channel_id=1, source_target_pairs={{0,3},{1,2},{2,1},{3,0},{4,7},{5,6},{6,5},{7,4},{8,11},{9,10},{10,... | collective-permute-start | bytes 786440 | tf_op jit(solution)/shard_map/ppermute | solution.py:310
  31.4 1.8 %collective-permute-done.7.refs_6_ = bf16[32,2048]{1,0:T(8,128)(2,1)S(1)} collective-permute-done((bf16[32,2048]{1,0:T(8,128)(2,1)S(1)}, bf16[32,2048]{1,0:T(8,128)(2,1)S(1)}, u32[]{:S(2)}, u32[]{:S(2)}) %collective-permute-start.7) | collective-permute-done | bytes 131104 | tf_op jit(solution)/shard_map/ppermute | solution.py:310
  33.2 2.1 %collective-permute-start.9 = (bf16[32,2048]{1,0:T(8,128)(2,1)S(1)}, bf16[32,2048]{1,0:T(8,128)(2,1)S(1)}, u32[]{:S(2)}, u32[]{:S(2)}) collective-permute-start(bf16[32,2048]{1,0:T(8,128)(2,1)S(1)} %get-tuple-element.42), channel_id=1, source_target_pairs={{0,4},{1,5},{2,6},{3,7},{4,0},{5,1},{6,2},{7,3},{8,12},{9,13},{10,... | collective-permute-start | bytes 393224 | tf_op jit(solution)/shard_map/ppermute | solution.py:310
  35.3 11.0 %collective-permute-done.8.refs_7_ = bf16[32,2048]{1,0:T(8,128)(2,1)S(1)} collective-permute-done((bf16[32,2048]{1,0:T(8,128)(2,1)S(1)}, bf16[32,2048]{1,0:T(8,128)(2,1)S(1)}, u32[]{:S(2)}, u32[]{:S(2)}) %collective-permute-start.8) | collective-permute-done | bytes 131104 | tf_op jit(solution)/shard_map/ppermute | solution.py:310
  46.4 0.0 collective-permute-start.10
  46.4 0.0 collective-permute-done.2.refs_1_
  46.4 0.0 collective-permute-start.11
  46.4 0.0 collective-permute-done.3.refs_2_
  46.4 0.1 collective-permute-start.12
  46.5 2.9 %collective-permute-done.4.refs_3_ = bf16[32,4096]{1,0:T(8,128)(2,1)S(1)} collective-permute-done((bf16[32,4096]{1,0:T(8,128)(2,1)S(1)}, bf16[32,4096]{1,0:T(8,128)(2,1)S(1)}, u32[]{:S(2)}, u32[]{:S(2)}) %collective-permute-start.4) | collective-permute-done | bytes 262176 | tf_op jit(solution)/shard_map/ppermute | solution.py:310
  49.4 2.3 %place_first.1 = (bf16[128,4096]{1,0:T(8,128)(2,1)}, bf16[128,256]{1,0:T(8,128)(2,1)S(1)}) custom-call(bf16[32,4096]{1,0:T(8,128)(2,1)S(1)} %get-tuple-element.33.refs_0_, bf16[32,4096]{1,0:T(8,128)(2,1)S(1)} %collective-permute-done.2.refs_1_, bf16[32,4096]{1,0:T(8,128)(2,1)S(1)} %collective-permute-done.3.refs_2_, ...), custom_call_target="tpu_custom_call" | custom-call | tf_op jit(solution)/shard_map/place_first/pallas_call | solution.py:459
  51.7 0.0 collective-permute-done.9.refs_4_
  51.7 7.1 %collective-permute-done.10.refs_5_ = bf16[32,2048]{1,0:T(8,128)(2,1)S(1)} collective-permute-done((bf16[32,2048]{1,0:T(8,128)(2,1)S(1)}, bf16[32,2048]{1,0:T(8,128)(2,1)S(1)}, u32[]{:S(2)}, u32[]{:S(2)}) %collective-permute-start.10) | collective-permute-done | bytes 131104 | tf_op jit(solution)/shard_map/ppermute | solution.py:310
  58.8 2.8 %collective-permute-done.11.refs_6_ = bf16[32,2048]{1,0:T(8,128)(2,1)S(1)} collective-permute-done((bf16[32,2048]{1,0:T(8,128)(2,1)S(1)}, bf16[32,2048]{1,0:T(8,128)(2,1)S(1)}, u32[]{:S(2)}, u32[]{:S(2)}) %collective-permute-start.11) | collective-permute-done | bytes 131104 | tf_op jit(solution)/shard_map/ppermute | solution.py:310
  61.6 6.4 %collective-permute-done.12.refs_7_ = bf16[32,2048]{1,0:T(8,128)(2,1)S(1)} collective-permute-done((bf16[32,2048]{1,0:T(8,128)(2,1)S(1)}, bf16[32,2048]{1,0:T(8,128)(2,1)S(1)}, u32[]{:S(2)}, u32[]{:S(2)}) %collective-permute-start.12) | collective-permute-done | bytes 131104 | tf_op jit(solution)/shard_map/ppermute | solution.py:310
  68.1 2.0 %place_second.1 = bf16[128,4096]{1,0:T(8,128)(2,1)} custom-call(bf16[128,256]{1,0:T(8,128)(2,1)S(1)} %get-tuple-element.41.sel_ref, bf16[32,4096]{1,0:T(8,128)(2,1)S(1)} %get-tuple-element.33.refs_0_, bf16[32,4096]{1,0:T(8,128)(2,1)S(1)} %collective-permute-done.2.refs_1_, ...), custom_call_target="tpu_custom_call", output_to_operand_aliasing={{}: (9, {})} | custom-call | tf_op jit(solution)/shard_map/place_second/pallas_call | solution.py:476
Async XLA Ops:
  0.0 9.8 %copy-start.1 = (s32[16]{0:T(128)S(1)}, s32[16]{0:T(128)}, u32[]{:S(2)}) copy-start(s32[16]{0:T(128)} %lens_ref.1) | copy-start | bytes 196
  0.0 9.8 %copy-start.2 = (s32[32]{0:T(128)S(1)}, s32[32]{0:T(128)}, u32[]{:S(2)}) copy-start(s32[32]{0:T(128)} %dest_ref.1) | copy-start | bytes 388
  0.0 14.5 %copy-start = (bf16[128,4096]{1,0:T(8,128)(2,1)S(1)}, bf16[128,4096]{1,0:T(8,128)(2,1)}, u32[]{:S(2)}) copy-start(bf16[128,4096]{1,0:T(8,128)(2,1)} %wq_ref.3) | copy-start | bytes 3145732
  4.7 6.9 %collective-permute-start.1 = (bf16[160,512]{1,0:T(8,128)(2,1)S(1)}, bf16[160,512]{1,0:T(8,128)(2,1)S(1)}, u32[]{:S(2)}, u32[]{:S(2)}) collective-permute-start(bf16[160,512]{1,0:T(8,128)(2,1)S(1)} %get-tuple-element.28.own_ref), channel_id=1, source_target_pairs={{0,2},{1,3},{2,4},{3,5},{4,6},{5,7},{8,10},{9,11},{10,12},{11,13},... | collective-permute-start | bytes 491528 | tf_op jit(solution)/shard_map/ppermute | solution.py:395
  7.9 6.6 %collective-permute-start = (bf16[160,512]{1,0:T(8,128)(2,1)S(1)}, bf16[160,512]{1,0:T(8,128)(2,1)S(1)}, u32[]{:S(2)}, u32[]{:S(2)}) collective-permute-start(bf16[160,512]{1,0:T(8,128)(2,1)S(1)} %get-tuple-element.28.own_ref), channel_id=1, source_target_pairs={{0,1},{1,2},{2,3},{3,4},{4,5},{5,6},{6,7},{8,9},{9,10},{10,11},{11... | collective-permute-start | bytes 491528 | tf_op jit(solution)/shard_map/ppermute | solution.py:395
  16.6 7.9 %collective-permute-start.5 = (bf16[32,2048]{1,0:T(8,128)(2,1)S(1)}, bf16[32,2048]{1,0:T(8,128)(2,1)S(1)}, u32[]{:S(2)}, u32[]{:S(2)}) collective-permute-start(bf16[32,2048]{1,0:T(8,128)(2,1)S(1)} %get-tuple-element.37), channel_id=1, source_target_pairs={{0,4},{1,5},{2,6},{3,7},{4,0},{5,1},{6,2},{7,3},{8,12},{9,13},{10,... | collective-permute-start | bytes 393224 | tf_op jit(solution)/shard_map/ppermute | solution.py:310
  16.7 12.7 %collective-permute-start.6 = (bf16[32,2048]{1,0:T(8,128)(2,1)S(1)}, bf16[32,2048]{1,0:T(8,128)(2,1)S(1)}, u32[]{:S(2)}, u32[]{:S(2)}) collective-permute-start(bf16[32,2048]{1,0:T(8,128)(2,1)S(1)} %get-tuple-element.38), channel_id=1, source_target_pairs={{0,5},{1,4},{2,7},{3,6},{4,1},{5,0},{6,3},{7,2},{8,13},{9,12},{10,... | collective-permute-start | bytes 393224 | tf_op jit(solution)/shard_map/ppermute | solution.py:310
  23.1 23.2 %collective-permute-start.2 = (bf16[32,4096]{1,0:T(8,128)(2,1)S(1)}, bf16[32,4096]{1,0:T(8,128)(2,1)S(1)}, u32[]{:S(2)}, u32[]{:S(2)}) collective-permute-start(bf16[32,4096]{1,0:T(8,128)(2,1)S(1)} %get-tuple-element.34), channel_id=1, source_target_pairs={{0,1},{1,0},{2,3},{3,2},{4,5},{5,4},{6,7},{7,6},{8,9},{9,8},{10,11... | collective-permute-start | bytes 786440 | tf_op jit(solution)/shard_map/ppermute | solution.py:310
  23.2 23.2 %collective-permute-start.3 = (bf16[32,4096]{1,0:T(8,128)(2,1)S(1)}, bf16[32,4096]{1,0:T(8,128)(2,1)S(1)}, u32[]{:S(2)}, u32[]{:S(2)}) collective-permute-start(bf16[32,4096]{1,0:T(8,128)(2,1)S(1)} %get-tuple-element.35), channel_id=1, source_target_pairs={{0,2},{1,3},{2,0},{3,1},{4,6},{5,7},{6,4},{7,5},{8,10},{9,11},{10,... | collective-permute-start | bytes 786440 | tf_op jit(solution)/shard_map/ppermute | solution.py:310
  24.5 8.7 %collective-permute-start.7 = (bf16[32,2048]{1,0:T(8,128)(2,1)S(1)}, bf16[32,2048]{1,0:T(8,128)(2,1)S(1)}, u32[]{:S(2)}, u32[]{:S(2)}) collective-permute-start(bf16[32,2048]{1,0:T(8,128)(2,1)S(1)} %get-tuple-element.39), channel_id=1, source_target_pairs={{0,6},{1,7},{2,4},{3,5},{4,2},{5,3},{6,0},{7,1},{8,14},{9,15},{10,... | collective-permute-start | bytes 393224 | tf_op jit(solution)/shard_map/ppermute | solution.py:310
  24.5 21.8 %collective-permute-start.8 = (bf16[32,2048]{1,0:T(8,128)(2,1)S(1)}, bf16[32,2048]{1,0:T(8,128)(2,1)S(1)}, u32[]{:S(2)}, u32[]{:S(2)}) collective-permute-start(bf16[32,2048]{1,0:T(8,128)(2,1)S(1)} %get-tuple-element.40), channel_id=1, source_target_pairs={{0,7},{1,6},{2,5},{3,4},{4,3},{5,2},{6,1},{7,0},{8,15},{9,14},{10,... | collective-permute-start | bytes 393224 | tf_op jit(solution)/shard_map/ppermute | solution.py:310
  29.5 19.9 %collective-permute-start.4 = (bf16[32,4096]{1,0:T(8,128)(2,1)S(1)}, bf16[32,4096]{1,0:T(8,128)(2,1)S(1)}, u32[]{:S(2)}, u32[]{:S(2)}) collective-permute-start(bf16[32,4096]{1,0:T(8,128)(2,1)S(1)} %get-tuple-element.36), channel_id=1, source_target_pairs={{0,3},{1,2},{2,1},{3,0},{4,7},{5,6},{6,5},{7,4},{8,11},{9,10},{10,... | collective-permute-start | bytes 786440 | tf_op jit(solution)/shard_map/ppermute | solution.py:310
  33.2 18.5 %collective-permute-start.9 = (bf16[32,2048]{1,0:T(8,128)(2,1)S(1)}, bf16[32,2048]{1,0:T(8,128)(2,1)S(1)}, u32[]{:S(2)}, u32[]{:S(2)}) collective-permute-start(bf16[32,2048]{1,0:T(8,128)(2,1)S(1)} %get-tuple-element.42), channel_id=1, source_target_pairs={{0,4},{1,5},{2,6},{3,7},{4,0},{5,1},{6,2},{7,3},{8,12},{9,13},{10,... | collective-permute-start | bytes 393224 | tf_op jit(solution)/shard_map/ppermute | solution.py:310
  46.4 12.5 %collective-permute-start.10 = (bf16[32,2048]{1,0:T(8,128)(2,1)S(1)}, bf16[32,2048]{1,0:T(8,128)(2,1)S(1)}, u32[]{:S(2)}, u32[]{:S(2)}) collective-permute-start(bf16[32,2048]{1,0:T(8,128)(2,1)S(1)} %get-tuple-element.43), channel_id=1, source_target_pairs={{0,5},{1,4},{2,7},{3,6},{4,1},{5,0},{6,3},{7,2},{8,13},{9,12},{10,... | collective-permute-start | bytes 393224 | tf_op jit(solution)/shard_map/ppermute | solution.py:310
  46.4 15.3 %collective-permute-start.11 = (bf16[32,2048]{1,0:T(8,128)(2,1)S(1)}, bf16[32,2048]{1,0:T(8,128)(2,1)S(1)}, u32[]{:S(2)}, u32[]{:S(2)}) collective-permute-start(bf16[32,2048]{1,0:T(8,128)(2,1)S(1)} %get-tuple-element.44), channel_id=1, source_target_pairs={{0,6},{1,7},{2,4},{3,5},{4,2},{5,3},{6,0},{7,1},{8,14},{9,15},{10,... | collective-permute-start | bytes 393224 | tf_op jit(solution)/shard_map/ppermute | solution.py:310
  46.4 21.7 %collective-permute-start.12 = (bf16[32,2048]{1,0:T(8,128)(2,1)S(1)}, bf16[32,2048]{1,0:T(8,128)(2,1)S(1)}, u32[]{:S(2)}, u32[]{:S(2)}) collective-permute-start(bf16[32,2048]{1,0:T(8,128)(2,1)S(1)} %get-tuple-element.45), channel_id=1, source_target_pairs={{0,7},{1,6},{2,5},{3,4},{4,3},{5,2},{6,1},{7,0},{8,15},{9,14},{10,... | collective-permute-start | bytes 393224 | tf_op jit(solution)/shard_map/ppermute | solution.py:310

commit v4 on v3

--- a/solution.py
+++ b/solution.py
@@ -61,6 +61,9 @@
         )
     for copy in small + large:
         copy.start()
+    for group in weights:
+        for copy in group:
+            copy.start(priority=1)
     for c in range(byte_dim // 128):
         wide_ref[c, 0:PAD, :] = jnp.zeros((PAD, 128), F32)
         wide_ref[c, PAD + n_bytes :, :] = jnp.zeros((PAD, 128), F32)
@@ -79,10 +82,6 @@
     keep_ref[...] = keep
     for i, copy in enumerate(large):
         copy.wait()
-        if i == 0:
-            for group in weights:
-                for one in group:
-                    one.start()
         for c in range(byte_dim // 128):
             wide_ref[c, PAD + i * some : PAD + (i + 1) * some, :] = x_ref[
                 i * some : (i + 1) * some, c * 128 : (c + 1) * 128
@@ -122,21 +121,20 @@
             fold_ref[r : r + 1, o : o + 128] = short[0:1]
             fold_ref[8 + r : 9 + r, o : o + 128] = corr
 
-    def project(slot):
-        for copy in weights[slot]:
-            copy.wait()
-        span = slice(slot * byte_dim, (slot + 1) * byte_dim)
-        got = jnp.dot(u_ref[:, span], w_ref[span, :], preferred_element_type=F32)
-        if slot == 0:
-            acc_ref[...] = got
-        else:
-            acc_ref[...] += got
-
-    conv(0)
-    for slot in range(1, SHORTEN):
+    def project(first, count):
+        for group in weights[first : first + count]:
+            for copy in group:
+                copy.wait()
+        span = slice(first * byte_dim, (first + count) * byte_dim)
+        return jnp.dot(u_ref[:, span], w_ref[span, :], preferred_element_type=F32)
+
+    middle = SHORTEN // 2
+    for slot in range(middle):
         conv(slot)
-        project(slot - 1)
-    project(SHORTEN - 1)
+    acc_ref[...] = project(0, middle)
+    for slot in range(middle, SHORTEN):
+        conv(slot)
+    acc_ref[...] += project(middle, SHORTEN - middle)
     rs = lax.rsqrt(jnp.sum(squares[0], axis=1, keepdims=True) * (1.0 / width) + 1e-06)
     out_ref[0:toks, :] = (acc_ref[0:toks, 0 : 2 * kv] * rs).astype(BF16)
     lat_ref[...] = (acc_ref[0:toks, 2 * kv :] * rs).astype(BF16)
@@ -300,10 +298,25 @@
     out_ref[...] = jnp.dot(pick_ref[...], got, preferred_element_type=F32).astype(BF16)
 
 
-def second_kernel(sel_ref, *refs):
-    block_refs, out_ref = refs[:-2], refs[-1]
-    got = jnp.concatenate([r[...] for r in block_refs], axis=0)
-    out_ref[...] = jnp.dot(sel_ref[...], got, preferred_element_type=F32).astype(BF16)
+def second_kernel(span, sel_ref, *refs):
+    block_refs, (out_ref, stage_ref, sems) = refs[:-4], refs[-3:]
+    pieces, _, cols = stage_ref.shape
+    copies = []
+    for i in range(pieces):
+        parts = []
+        for ref in block_refs:
+            at = ref.shape[1] - span + i * cols
+            parts.append(ref[:, at : at + cols])
+        got = jnp.concatenate(parts, axis=0)
+        stage_ref[i] = jnp.dot(sel_ref[...], got, preferred_element_type=F32).astype(BF16)
+        copies.append(
+            pltpu.make_async_copy(
+                stage_ref.at[i], out_ref.at[:, pl.ds(out_ref.shape[1] - span + i * cols, cols)], sems.at[i]
+            )
+        )
+        copies[-1].start()
+    for copy in copies:
+        copy.wait()
 
 
 def swap(array, by, size):
@@ -474,14 +487,11 @@
     )(*got_near, *got_first)
     operands = [sel, *got_near, *got_second, out]
     return pl.pallas_call(
-        second_kernel,
-        grid=(steps,),
+        functools.partial(second_kernel, span),
         out_shape=jax.ShapeDtypeStruct((toks, width), BF16),
-        in_specs=[whole_block(sel.shape)]
-        + columns(got_near, steps)
-        + columns(got_second, 0)
-        + [pl.BlockSpec(memory_space=pl.ANY)],
-        out_specs=pl.BlockSpec((toks, cols), lambda i: (0, steps + i)),
+        in_specs=[vmem()] * (len(operands) - 1) + [pl.BlockSpec(memory_space=pl.ANY)],
+        out_specs=pl.BlockSpec(memory_space=pl.ANY),
+        scratch_shapes=[pltpu.VMEM((steps, toks, cols), BF16), pltpu.SemaphoreType.DMA((steps,))],
         input_output_aliases={len(operands) - 1: 0},
         compiler_params=params(),
         name="place_second",

time: 70.3 us -> 68.7 us (0.977)
  the two profiles are of different devices: /device:TPU:23 before, /device:TPU:21 now
where the time goes in v4:
time: 68.7 us; the launch traced here: 68.5 us
  waiting for transfers between devices  36 us (52%)
  starting transfers between devices  19.5 us (28%)
  Pallas kernels  12.8 us (19%)
    ppermute x11, waiting for transfers between devices, swap(): return lax.ppermute(array, 'seq', [(i, i ^ by) for i in range(size)])  32.1 us
    ppermute x11, starting transfers between devices, swap(): return lax.ppermute(array, 'seq', [(i, i ^ by) for i in range(size)])  14.4 us
    ppermute x2, starting transfers between devices, per_device(): lax.ppermute(held, 'seq', [(i, i + by) for i in range(n_seq - by)])  5.13 us
    pallas_call x2, Pallas kernels, attend(): pl.pallas_call(functools.partial(attend_kernel, half, batch), out_shape=o...  4.6 us
    pallas_call x1, Pallas kernels, per_device(): pl.pallas_call(project_kernel, out_shape=[pltpu.VMEM((held_rows, 2 * kv),...  4.03 us
    ppermute x2, waiting for transfers between devices, per_device(): lax.ppermute(held, 'seq', [(i, i + by) for i in range(n_seq - by)])  3.89 us
    pallas_call x1, Pallas kernels, per_device(): pl.pallas_call(functools.partial(first_kernel, n_seq, rows), grid=(steps,...  2.34 us
  transfers between devices with their start and end apart: 13, of which 8 were waited for; matrix products, arithmetic and copies ran while one was open for 0% of the time, Pallas kernels for 8%

profile of v4, /device:TPU:21, one launch (start us, length us, event | category | flops | bytes accessed | tf_op | source)
XLA Modules:
  0.0 68.5 jit_solution(10370821604540994920)
XLA Ops:
  0.0 0.0 copy-start.1
  0.0 0.0 copy-start.2
  0.0 0.0 copy-start
  0.0 4.0 %project.1 = (bf16[160,512]{1,0:T(8,128)(2,1)S(1)}, bf16[128,4096]{1,0:T(8,128)(2,1)S(1)}, bf16[128,128]{1,0:T(8,128)(2,1)S(1)}, f32[8,640]{1,0:T(8,128)S(1)}) custom-call(s32[16]{0:T(128)} %lens_ref.1, bf16[512,1024]{1,0:T(8,128)(2,1)} %x_hbm.1, f32[4,1024]{1,0:T(4,128)} %taps_hbm.1, f32[1,4096]{1,0:T(1,128)} %bitcast.1, bf16[4096,256]{1,0:T(8,128)(2,1)} %wk_hbm.1, ...), custom_call_target="tpu_custom_call" | custom-call | tf_op jit(solution)/shard_map/project/pallas_call | solution.py:372
  4.0 3.2 %collective-permute-start.1 = (bf16[160,512]{1,0:T(8,128)(2,1)S(1)}, bf16[160,512]{1,0:T(8,128)(2,1)S(1)}, u32[]{:S(2)}, u32[]{:S(2)}) collective-permute-start(bf16[160,512]{1,0:T(8,128)(2,1)S(1)} %get-tuple-element.28.own_ref), channel_id=1, source_target_pairs={{0,2},{1,3},{2,4},{3,5},{4,6},{5,7},{8,10},{9,11},{10,12},{11,13},... | collective-permute-start | bytes 491528 | tf_op jit(solution)/shard_map/ppermute | solution.py:408
  7.3 1.9 %collective-permute-start = (bf16[160,512]{1,0:T(8,128)(2,1)S(1)}, bf16[160,512]{1,0:T(8,128)(2,1)S(1)}, u32[]{:S(2)}, u32[]{:S(2)}) collective-permute-start(bf16[160,512]{1,0:T(8,128)(2,1)S(1)} %get-tuple-element.28.own_ref), channel_id=1, source_target_pairs={{0,1},{1,2},{2,3},{3,4},{4,5},{5,6},{6,7},{8,9},{9,10},{10,11},{11... | collective-permute-start | bytes 491528 | tf_op jit(solution)/shard_map/ppermute | solution.py:408
  9.2 0.0 copy-done.1
  9.2 0.0 copy-done.2
  9.2 0.8 %plan.1 = (f32[128,384]{1,0:T(8,128)S(1)}, bf16[256,128]{1,0:T(8,128)(2,1)S(1)}) custom-call(s32[16]{0:T(128)S(1)} %copy-done.1, s32[32]{0:T(128)S(1)} %copy-done.2), custom_call_target="tpu_custom_call" | custom-call | tf_op jit(solution)/shard_map/plan/pallas_call | solution.py:412
  10.0 1.0 %collective-permute-done.1.two_ref = bf16[160,512]{1,0:T(8,128)(2,1)S(1)} collective-permute-done((bf16[160,512]{1,0:T(8,128)(2,1)S(1)}, bf16[160,512]{1,0:T(8,128)(2,1)S(1)}, u32[]{:S(2)}, u32[]{:S(2)}) %collective-permute-start.1) | collective-permute-done | bytes 163872 | tf_op jit(solution)/shard_map/ppermute | solution.py:408
  11.0 2.9 %collective-permute-done.one_ref = bf16[160,512]{1,0:T(8,128)(2,1)S(1)} collective-permute-done((bf16[160,512]{1,0:T(8,128)(2,1)S(1)}, bf16[160,512]{1,0:T(8,128)(2,1)S(1)}, u32[]{:S(2)}, u32[]{:S(2)}) %collective-permute-start) | collective-permute-done | bytes 163872 | tf_op jit(solution)/shard_map/ppermute | solution.py:408
  13.9 0.0 copy-done
  13.9 2.1 %attend_half_0.1 = (bf16[32,2048]{1,0:T(8,128)(2,1)S(1)}, bf16[32,2048]{1,0:T(8,128)(2,1)S(1)}, bf16[32,2048]{1,0:T(8,128)(2,1)S(1)}, bf16[32,2048]{1,0:T(8,128)(2,1)S(1)}, bf16[128,2048]{1,0:T(8,128)(2,1)S(1)}) custom-call(bf16[128,128]{1,0:T(8,128)(2,1)S(1)} %get-tuple-element.26.lat_ref, f32[8,640]{1,0:T(8,128)S(1)} %get-tuple-element.27.edge_ref, ...), custom_call_target="tpu_custom_call" | custom-call | tf_op jit(solution)/shard_map/attend_half_0/pallas_call | solution.py:439
  16.0 0.1 collective-permute-start.5
  16.1 3.9 %collective-permute-start.6 = (bf16[32,2048]{1,0:T(8,128)(2,1)S(1)}, bf16[32,2048]{1,0:T(8,128)(2,1)S(1)}, u32[]{:S(2)}, u32[]{:S(2)}) collective-permute-start(bf16[32,2048]{1,0:T(8,128)(2,1)S(1)} %get-tuple-element.38), channel_id=1, source_target_pairs={{0,5},{1,4},{2,7},{3,6},{4,1},{5,0},{6,3},{7,2},{8,13},{9,12},{10,... | collective-permute-start | bytes 393224 | tf_op jit(solution)/shard_map/ppermute | solution.py:323
  20.0 2.5 %attend_half_1.1 = (bf16[32,2048]{1,0:T(8,128)(2,1)S(1)}, bf16[32,2048]{1,0:T(8,128)(2,1)S(1)}, bf16[32,2048]{1,0:T(8,128)(2,1)S(1)}, bf16[32,2048]{1,0:T(8,128)...) custom-call(bf16[128,128]{1,0:T(8,128)(2,1)S(1)} %get-tuple-element., ...), custom_call_target="tpu_custom_call" | custom-call | tf_op jit(solution)/shard_map/attend_half_1/pallas_call | solution.py:439
  22.5 0.1 collective-permute-start.2
  22.6 1.3 %collective-permute-start.3 = (bf16[32,4096]{1,0:T(8,128)(2,1)S(1)}, bf16[32,4096]{1,0:T(8,128)(2,1)S(1)}, u32[]{:S(2)}, u32[]{:S(2)}) collective-permute-start(bf16[32,4096]{1,0:T(8,128)(2,1)S(1)} %get-tuple-element.35), channel_id=1, source_target_pairs={{0,2},{1,3},{2,0},{3,1},{4,6},{5,7},{6,4},{7,5},{8,10},{9,11},{10,... | collective-permute-start | bytes 786440 | tf_op jit(solution)/shard_map/ppermute | solution.py:323
  23.9 0.0 collective-permute-start.7
  23.9 0.0 collective-permute-done.5.refs_4_
  23.9 4.9 %collective-permute-start.8 = (bf16[32,2048]{1,0:T(8,128)(2,1)S(1)}, bf16[32,2048]{1,0:T(8,128)(2,1)S(1)}, u32[]{:S(2)}, u32[]{:S(2)}) collective-permute-start(bf16[32,2048]{1,0:T(8,128)(2,1)S(1)} %get-tuple-element.40), channel_id=1, source_target_pairs={{0,7},{1,6},{2,5},{3,4},{4,3},{5,2},{6,1},{7,0},{8,15},{9,14},{10,... | collective-permute-start | bytes 393224 | tf_op jit(solution)/shard_map/ppermute | solution.py:323
  28.8 0.0 collective-permute-done.6.refs_5_
  28.9 1.9 %collective-permute-start.4 = (bf16[32,4096]{1,0:T(8,128)(2,1)S(1)}, bf16[32,4096]{1,0:T(8,128)(2,1)S(1)}, u32[]{:S(2)}, u32[]{:S(2)}) collective-permute-start(bf16[32,4096]{1,0:T(8,128)(2,1)S(1)} %get-tuple-element.36), channel_id=1, source_target_pairs={{0,3},{1,2},{2,1},{3,0},{4,7},{5,6},{6,5},{7,4},{8,11},{9,10},{10,... | collective-permute-start | bytes 786440 | tf_op jit(solution)/shard_map/ppermute | solution.py:323
  30.8 1.8 %collective-permute-done.7.refs_6_ = bf16[32,2048]{1,0:T(8,128)(2,1)S(1)} collective-permute-done((bf16[32,2048]{1,0:T(8,128)(2,1)S(1)}, bf16[32,2048]{1,0:T(8,128)(2,1)S(1)}, u32[]{:S(2)}, u32[]{:S(2)}) %collective-permute-start.7) | collective-permute-done | bytes 131104 | tf_op jit(solution)/shard_map/ppermute | solution.py:323
  32.6 2.1 %collective-permute-start.9 = (bf16[32,2048]{1,0:T(8,128)(2,1)S(1)}, bf16[32,2048]{1,0:T(8,128)(2,1)S(1)}, u32[]{:S(2)}, u32[]{:S(2)}) collective-permute-start(bf16[32,2048]{1,0:T(8,128)(2,1)S(1)} %get-tuple-element.42), channel_id=1, source_target_pairs={{0,4},{1,5},{2,6},{3,7},{4,0},{5,1},{6,2},{7,3},{8,12},{9,13},{10,... | collective-permute-start | bytes 393224 | tf_op jit(solution)/shard_map/ppermute | solution.py:323
  34.7 11.1 %collective-permute-done.8.refs_7_ = bf16[32,2048]{1,0:T(8,128)(2,1)S(1)} collective-permute-done((bf16[32,2048]{1,0:T(8,128)(2,1)S(1)}, bf16[32,2048]{1,0:T(8,128)(2,1)S(1)}, u32[]{:S(2)}, u32[]{:S(2)}) %collective-permute-start.8) | collective-permute-done | bytes 131104 | tf_op jit(solution)/shard_map/ppermute | solution.py:323
  45.7 0.0 collective-permute-start.10
  45.7 0.0 collective-permute-done.2.refs_1_
  45.7 0.0 collective-permute-start.11
  45.7 0.0 collective-permute-done.3.refs_2_
  45.8 0.1 collective-permute-start.12
  45.8 3.2 %collective-permute-done.4.refs_3_ = bf16[32,4096]{1,0:T(8,128)(2,1)S(1)} collective-permute-done((bf16[32,4096]{1,0:T(8,128)(2,1)S(1)}, bf16[32,4096]{1,0:T(8,128)(2,1)S(1)}, u32[]{:S(2)}, u32[]{:S(2)}) %collective-permute-start.4) | collective-permute-done | bytes 262176 | tf_op jit(solution)/shard_map/ppermute | solution.py:323
  49.0 2.3 %place_first.1 = (bf16[128,4096]{1,0:T(8,128)(2,1)}, bf16[128,256]{1,0:T(8,128)(2,1)S(1)}) custom-call(bf16[32,4096]{1,0:T(8,128)(2,1)S(1)} %get-tuple-element.33.refs_0_, bf16[32,4096]{1,0:T(8,128)(2,1)S(1)} %collective-permute-done.2.refs_1_, bf16[32,4096]{1,0:T(8,128)(2,1)S(1)} %collective-permute-done.3.refs_2_, ...), custom_call_target="tpu_custom_call" | custom-call | tf_op jit(solution)/shard_map/place_first/pallas_call | solution.py:472
  51.4 0.0 collective-permute-done.9.refs_4_
  51.4 6.8 %collective-permute-done.10.refs_5_ = bf16[32,2048]{1,0:T(8,128)(2,1)S(1)} collective-permute-done((bf16[32,2048]{1,0:T(8,128)(2,1)S(1)}, bf16[32,2048]{1,0:T(8,128)(2,1)S(1)}, u32[]{:S(2)}, u32[]{:S(2)}) %collective-permute-start.10) | collective-permute-done | bytes 131104 | tf_op jit(solution)/shard_map/ppermute | solution.py:323
  58.2 2.8 %collective-permute-done.11.refs_6_ = bf16[32,2048]{1,0:T(8,128)(2,1)S(1)} collective-permute-done((bf16[32,2048]{1,0:T(8,128)(2,1)S(1)}, bf16[32,2048]{1,0:T(8,128)(2,1)S(1)}, u32[]{:S(2)}, u32[]{:S(2)}) %collective-permute-start.11) | collective-permute-done | bytes 131104 | tf_op jit(solution)/shard_map/ppermute | solution.py:323
  61.0 6.4 %collective-permute-done.12.refs_7_ = bf16[32,2048]{1,0:T(8,128)(2,1)S(1)} collective-permute-done((bf16[32,2048]{1,0:T(8,128)(2,1)S(1)}, bf16[32,2048]{1,0:T(8,128)(2,1)S(1)}, u32[]{:S(2)}, u32[]{:S(2)}) %collective-permute-start.12) | collective-permute-done | bytes 131104 | tf_op jit(solution)/shard_map/ppermute | solution.py:323
  67.4 1.0 %place_second.1 = bf16[128,4096]{1,0:T(8,128)(2,1)} custom-call(bf16[128,256]{1,0:T(8,128)(2,1)S(1)} %get-tuple-element.41.sel_ref, bf16[32,4096]{1,0:T(8,128)(2,1)S(1)} %get-tuple-element.33.refs_0_, bf16[32,4096]{1,0:T(8,128)(2,1)S(1)} %collective-permute-done.2.refs_1_, ...), custom_call_target="tpu_custom_call", output_to_operand_aliasing={{}: (9, {})} | custom-call | tf_op jit(solution)/shard_map/place_second/pallas_call | solution.py:489
Async XLA Ops:
  0.0 9.2 %copy-start.1 = (s32[16]{0:T(128)S(1)}, s32[16]{0:T(128)}, u32[]{:S(2)}) copy-start(s32[16]{0:T(128)} %lens_ref.1) | copy-start | bytes 196
  0.0 9.2 %copy-start.2 = (s32[32]{0:T(128)S(1)}, s32[32]{0:T(128)}, u32[]{:S(2)}) copy-start(s32[32]{0:T(128)} %dest_ref.1) | copy-start | bytes 388
  0.0 13.9 %copy-start = (bf16[128,4096]{1,0:T(8,128)(2,1)S(1)}, bf16[128,4096]{1,0:T(8,128)(2,1)}, u32[]{:S(2)}) copy-start(bf16[128,4096]{1,0:T(8,128)(2,1)} %wq_ref.3) | copy-start | bytes 3145732
  4.0 7.0 %collective-permute-start.1 = (bf16[160,512]{1,0:T(8,128)(2,1)S(1)}, bf16[160,512]{1,0:T(8,128)(2,1)S(1)}, u32[]{:S(2)}, u32[]{:S(2)}) collective-permute-start(bf16[160,512]{1,0:T(8,128)(2,1)S(1)} %get-tuple-element.28.own_ref), channel_id=1, source_target_pairs={{0,2},{1,3},{2,4},{3,5},{4,6},{5,7},{8,10},{9,11},{10,12},{11,13},... | collective-permute-start | bytes 491528 | tf_op jit(solution)/shard_map/ppermute | solution.py:408
  7.3 6.6 %collective-permute-start = (bf16[160,512]{1,0:T(8,128)(2,1)S(1)}, bf16[160,512]{1,0:T(8,128)(2,1)S(1)}, u32[]{:S(2)}, u32[]{:S(2)}) collective-permute-start(bf16[160,512]{1,0:T(8,128)(2,1)S(1)} %get-tuple-element.28.own_ref), channel_id=1, source_target_pairs={{0,1},{1,2},{2,3},{3,4},{4,5},{5,6},{6,7},{8,9},{9,10},{10,11},{11... | collective-permute-start | bytes 491528 | tf_op jit(solution)/shard_map/ppermute | solution.py:408
  16.0 7.9 %collective-permute-start.5 = (bf16[32,2048]{1,0:T(8,128)(2,1)S(1)}, bf16[32,2048]{1,0:T(8,128)(2,1)S(1)}, u32[]{:S(2)}, u32[]{:S(2)}) collective-permute-start(bf16[32,2048]{1,0:T(8,128)(2,1)S(1)} %get-tuple-element.37), channel_id=1, source_target_pairs={{0,4},{1,5},{2,6},{3,7},{4,0},{5,1},{6,2},{7,3},{8,12},{9,13},{10,... | collective-permute-start | bytes 393224 | tf_op jit(solution)/shard_map/ppermute | solution.py:323
  16.1 12.7 %collective-permute-start.6 = (bf16[32,2048]{1,0:T(8,128)(2,1)S(1)}, bf16[32,2048]{1,0:T(8,128)(2,1)S(1)}, u32[]{:S(2)}, u32[]{:S(2)}) collective-permute-start(bf16[32,2048]{1,0:T(8,128)(2,1)S(1)} %get-tuple-element.38), channel_id=1, source_target_pairs={{0,5},{1,4},{2,7},{3,6},{4,1},{5,0},{6,3},{7,2},{8,13},{9,12},{10,... | collective-permute-start | bytes 393224 | tf_op jit(solution)/shard_map/ppermute | solution.py:323
  22.5 23.2 %collective-permute-start.2 = (bf16[32,4096]{1,0:T(8,128)(2,1)S(1)}, bf16[32,4096]{1,0:T(8,128)(2,1)S(1)}, u32[]{:S(2)}, u32[]{:S(2)}) collective-permute-start(bf16[32,4096]{1,0:T(8,128)(2,1)S(1)} %get-tuple-element.34), channel_id=1, source_target_pairs={{0,1},{1,0},{2,3},{3,2},{4,5},{5,4},{6,7},{7,6},{8,9},{9,8},{10,11... | collective-permute-start | bytes 786440 | tf_op jit(solution)/shard_map/ppermute | solution.py:323
  22.6 23.2 %collective-permute-start.3 = (bf16[32,4096]{1,0:T(8,128)(2,1)S(1)}, bf16[32,4096]{1,0:T(8,128)(2,1)S(1)}, u32[]{:S(2)}, u32[]{:S(2)}) collective-permute-start(bf16[32,4096]{1,0:T(8,128)(2,1)S(1)} %get-tuple-element.35), channel_id=1, source_target_pairs={{0,2},{1,3},{2,0},{3,1},{4,6},{5,7},{6,4},{7,5},{8,10},{9,11},{10,... | collective-permute-start | bytes 786440 | tf_op jit(solution)/shard_map/ppermute | solution.py:323
  23.9 8.7 %collective-permute-start.7 = (bf16[32,2048]{1,0:T(8,128)(2,1)S(1)}, bf16[32,2048]{1,0:T(8,128)(2,1)S(1)}, u32[]{:S(2)}, u32[]{:S(2)}) collective-permute-start(bf16[32,2048]{1,0:T(8,128)(2,1)S(1)} %get-tuple-element.39), channel_id=1, source_target_pairs={{0,6},{1,7},{2,4},{3,5},{4,2},{5,3},{6,0},{7,1},{8,14},{9,15},{10,... | collective-permute-start | bytes 393224 | tf_op jit(solution)/shard_map/ppermute | solution.py:323
  23.9 21.8 %collective-permute-start.8 = (bf16[32,2048]{1,0:T(8,128)(2,1)S(1)}, bf16[32,2048]{1,0:T(8,128)(2,1)S(1)}, u32[]{:S(2)}, u32[]{:S(2)}) collective-permute-start(bf16[32,2048]{1,0:T(8,128)(2,1)S(1)} %get-tuple-element.40), channel_id=1, source_target_pairs={{0,7},{1,6},{2,5},{3,4},{4,3},{5,2},{6,1},{7,0},{8,15},{9,14},{10,... | collective-permute-start | bytes 393224 | tf_op jit(solution)/shard_map/ppermute | solution.py:323
  28.9 20.2 %collective-permute-start.4 = (bf16[32,4096]{1,0:T(8,128)(2,1)S(1)}, bf16[32,4096]{1,0:T(8,128)(2,1)S(1)}, u32[]{:S(2)}, u32[]{:S(2)}) collective-permute-start(bf16[32,4096]{1,0:T(8,128)(2,1)S(1)} %get-tuple-element.36), channel_id=1, source_target_pairs={{0,3},{1,2},{2,1},{3,0},{4,7},{5,6},{6,5},{7,4},{8,11},{9,10},{10,... | collective-permute-start | bytes 786440 | tf_op jit(solution)/shard_map/ppermute | solution.py:323
  32.6 18.8 %collective-permute-start.9 = (bf16[32,2048]{1,0:T(8,128)(2,1)S(1)}, bf16[32,2048]{1,0:T(8,128)(2,1)S(1)}, u32[]{:S(2)}, u32[]{:S(2)}) collective-permute-start(bf16[32,2048]{1,0:T(8,128)(2,1)S(1)} %get-tuple-element.42), channel_id=1, source_target_pairs={{0,4},{1,5},{2,6},{3,7},{4,0},{5,1},{6,2},{7,3},{8,12},{9,13},{10,... | collective-permute-start | bytes 393224 | tf_op jit(solution)/shard_map/ppermute | solution.py:323
  45.7 12.5 %collective-permute-start.10 = (bf16[32,2048]{1,0:T(8,128)(2,1)S(1)}, bf16[32,2048]{1,0:T(8,128)(2,1)S(1)}, u32[]{:S(2)}, u32[]{:S(2)}) collective-permute-start(bf16[32,2048]{1,0:T(8,128)(2,1)S(1)} %get-tuple-element.43), channel_id=1, source_target_pairs={{0,5},{1,4},{2,7},{3,6},{4,1},{5,0},{6,3},{7,2},{8,13},{9,12},{10,... | collective-permute-start | bytes 393224 | tf_op jit(solution)/shard_map/ppermute | solution.py:323
  45.7 15.3 %collective-permute-start.11 = (bf16[32,2048]{1,0:T(8,128)(2,1)S(1)}, bf16[32,2048]{1,0:T(8,128)(2,1)S(1)}, u32[]{:S(2)}, u32[]{:S(2)}) collective-permute-start(bf16[32,2048]{1,0:T(8,128)(2,1)S(1)} %get-tuple-element.44), channel_id=1, source_target_pairs={{0,6},{1,7},{2,4},{3,5},{4,2},{5,3},{6,0},{7,1},{8,14},{9,15},{10,... | collective-permute-start | bytes 393224 | tf_op jit(solution)/shard_map/ppermute | solution.py:323
  45.8 21.7 %collective-permute-start.12 = (bf16[32,2048]{1,0:T(8,128)(2,1)S(1)}, bf16[32,2048]{1,0:T(8,128)(2,1)S(1)}, u32[]{:S(2)}, u32[]{:S(2)}) collective-permute-start(bf16[32,2048]{1,0:T(8,128)(2,1)S(1)} %get-tuple-element.45), channel_id=1, source_target_pairs={{0,7},{1,6},{2,5},{3,4},{4,3},{5,2},{6,1},{7,0},{8,15},{9,14},{10,... | collective-permute-start | bytes 393224 | tf_op jit(solution)/shard_map/ppermute | solution.py:323

commit v5 on v4

--- a/solution.py
+++ b/solution.py
@@ -185,13 +185,13 @@
         ref[...] = placed[k * rows : (k + 1) * rows]
 
 
-def attend_kernel(half, batch, lat_ref, edge_ref, own_ref, one_ref, two_ref, bias_ref, pick_ref, wq_ref, short_ref, *refs):
+def attend_kernel(half, batch, n_cross, lat_ref, edge_ref, own_ref, one_ref, two_ref, bias_ref, pick_ref, wq_ref, short_ref, *refs):
     refs, (k_ref, v_ref, query_ref, corr_ref, layer_ref) = refs[:-5], refs[-5:]
     if half == 0:
         cross_refs, out_layer_ref = refs[:-1], refs[-1]
     else:
         past_ref, refs = refs[0], refs[1:]
-        cross_refs, near_refs = refs[: len(refs) // 2], refs[len(refs) // 2 :]
+        cross_refs, far_refs, near_refs = refs[:n_cross], refs[n_cross : 2 * n_cross], refs[2 * n_cross :]
     toks, hd = lat_ref.shape
     wide = layer_ref.shape[1]
     heads = wide // hd
@@ -260,59 +260,62 @@
             short = jnp.concatenate([first, short[8:]], axis=0)
             layer_ref[:, cols] = (mixed[h * toks : (h + 1) * toks] + short).astype(BF16)
     middle = pick_ref.shape[0] // 2
-    put_blocks(pick_ref[middle:, :], layer_ref[...], cross_refs)
+    far = middle + middle // 2
+    put_blocks(pick_ref[middle:far, :], layer_ref[...], cross_refs)
     if half == 0:
         out_layer_ref[...] = layer_ref[...]
     else:
         layer = jnp.concatenate([past_ref[...], layer_ref[...]], axis=1)
+        put_blocks(pick_ref[far:, :], layer, far_refs)
         put_blocks(pick_ref[0:middle, :], layer, near_refs)
 
 
-def first_kernel(n_seq, rows, *refs):
-    block_refs, (out_ref, sel_ref, pick_ref) = refs[:-3], refs[-3:]
-    toks = out_ref.shape[0]
-    got = jnp.concatenate([r[...] for r in block_refs], axis=0)
-    me = lax.axis_index("seq")
-
-    @pl.when(pl.program_id(0) == 0)
-    def _():
-        n_pad = max(16, n_seq)
-        n_rows = got.shape[0]
-        used = jnp.where(got[:, 0:128].astype(F32) < 0.5 * MARK, 1.0, 0.0).astype(BF16)
-        member = iota((n_pad, n_rows), 0) == iota((n_pad, n_rows), 1) // rows
-        count = jnp.dot(jnp.where(member, 1.0, 0.0).astype(BF16), used, preferred_element_type=F32)
+def read_parts(parts, refs, at, cols):
+    return jnp.concatenate([refs[i][row : row + rows, col + at : col + at + cols] for i, row, rows, col in parts], axis=0)
+
+
+def count_marks(first, block, rows, n_pad):
+    used = jnp.where(rows.astype(F32) < 0.5 * MARK, 1.0, 0.0).astype(BF16)
+    shape = (n_pad, rows.shape[0])
+    member = iota(shape, 0) == first + iota(shape, 1) // block
+    return jnp.dot(jnp.where(member, 1.0, 0.0).astype(BF16), used, preferred_element_type=F32)
+
+
+def count_kernel(first, block, parts, *refs):
+    count_ref = refs[-1]
+    count_ref[...] = count_marks(first, block, read_parts(parts, refs, 0, 128), count_ref.shape[0])
+
+
+def place_kernel(n_seq, block, near, half, parts, *refs):
+    if half == 0:
+        count_ref, *got_refs, out_ref, sel_ref, stage_ref, sems = refs
+    else:
+        sel_ref, *got_refs, _, out_ref, stage_ref, sems = refs
+    pieces, toks, cols = stage_ref.shape
+    if half == 0:
+        me = lax.axis_index("seq")
+        n_pad = count_ref.shape[0]
+        n_rows = n_seq * block
+        head = read_parts(parts, got_refs, 0, 128)[near * block :]
+        count = count_ref[...] + count_marks(near, block, head, n_pad)
         source = me ^ iota((n_pad, 128), 0)
         offset = jnp.zeros((n_pad, 128), F32)
         for q in range(n_seq):
             offset = offset + jnp.where(source > (me ^ q), count[q : q + 1], 0.0)
         lane = iota((1, n_rows), 1)
-        within = (lane % rows).astype(F32)
+        within = (lane % block).astype(F32)
         target = jnp.full((1, n_rows), -1.0, F32)
         for q in range(n_seq):
-            valid = (lane // rows == q) & (within < count[q : q + 1, 0:1])
+            valid = (lane // block == q) & (within < count[q : q + 1, 0:1])
             target = jnp.where(valid, offset[q : q + 1, 0:1] + within, target)
-        row = iota((toks, n_rows), 0).astype(F32)
-        pick_ref[...] = jnp.where(row == target, 1.0, 0.0).astype(BF16)
-        sel_ref[...] = pick_ref[...]
-
-    out_ref[...] = jnp.dot(pick_ref[...], got, preferred_element_type=F32).astype(BF16)
-
-
-def second_kernel(span, sel_ref, *refs):
-    block_refs, (out_ref, stage_ref, sems) = refs[:-4], refs[-3:]
-    pieces, _, cols = stage_ref.shape
+        sel_ref[...] = jnp.where(iota((toks, n_rows), 0).astype(F32) == target, 1.0, 0.0).astype(BF16)
     copies = []
     for i in range(pieces):
-        parts = []
-        for ref in block_refs:
-            at = ref.shape[1] - span + i * cols
-            parts.append(ref[:, at : at + cols])
-        got = jnp.concatenate(parts, axis=0)
+        got = read_parts(parts, got_refs, i * cols, cols)
         stage_ref[i] = jnp.dot(sel_ref[...], got, preferred_element_type=F32).astype(BF16)
+        at = half * pieces * cols + i * cols
         copies.append(
-            pltpu.make_async_copy(
-                stage_ref.at[i], out_ref.at[:, pl.ds(out_ref.shape[1] - span + i * cols, cols)], sems.at[i]
-            )
+            pltpu.make_async_copy(stage_ref.at[i], out_ref.at[:, pl.ds(at, cols)], sems.at[i])
         )
         copies[-1].start()
     for copy in copies:
@@ -423,21 +426,20 @@
 
     middle = n_seq // 2
     span = width // kvh
-    batch = BATCH
-    n_out, out_rows = (1, middle * rows) if merged else (middle, rows)
-
-    def split(blocks):
-        if merged:
-            return [blocks[0][k * rows : (k + 1) * rows] for k in range(middle)]
-        return list(blocks)
-
-    def attend(half, more):
-        cross = [pltpu.VMEM((out_rows, span), BF16)] * n_out
-        near = [pltpu.VMEM((out_rows, width), BF16)] * n_out
-        outs = cross + ([pltpu.VMEM((toks, span), BF16)] if half == 0 else near)
+    def shapes(count, height, cols):
+        count, height = (1, count * height) if merged else (count, height)
+        return [pltpu.VMEM((height, cols), BF16)] * count
+
+    def split(arrays, count):
+        if len(arrays) == count:
+            return list(arrays)
+        height = arrays[0].shape[0] // count
+        return [arrays[0][i * height : (i + 1) * height] for i in range(count)]
+
+    def attend(half, outs, n_cross, more):
         operands = [latent, edge, held, *behind, bias, pick, w_qup, short, *more]
         return pl.pallas_call(
-            functools.partial(attend_kernel, half, batch),
+            functools.partial(attend_kernel, half, BATCH, n_cross),
             out_shape=outs,
             in_specs=[vmem()] * len(operands),
             out_specs=[vmem()] * len(outs),
@@ -452,50 +454,67 @@
             name=f"attend_half_{half}",
         )(*operands)
 
-    *first_cross, layer = attend(0, [])
-    got_first = [swap(x, middle + k, n_seq) for k, x in enumerate(split(first_cross))]
-    outs = attend(1, [layer])
-    got_second = [swap(x, middle + k, n_seq) for k, x in enumerate(split(outs[:n_out]))]
-    near = split(outs[n_out:])
+    half_cross = middle // 2
+    cross = shapes(half_cross, rows, span)
+    *first, layer = attend(0, cross + [pltpu.VMEM((toks, span), BF16)], len(cross), [])
+    first = split(first, half_cross)
+    got_first = [swap(first[k], middle + k, n_seq) for k in range(half_cross)]
+    far, near = shapes(half_cross, rows, width), shapes(middle, rows, width)
+    outs = attend(1, cross + far + near, len(cross), [layer])
+    second, outs = split(outs[: len(cross)], half_cross), outs[len(cross) :]
+    far, near = split(outs[: len(far)], half_cross), split(outs[len(far) :], middle)
+    got_far = [swap(far[k], middle + half_cross + k, n_seq) for k in range(half_cross)]
     got_near = [near[0]] + [swap(near[k], k, n_seq) for k in range(1, middle)]
-    if merged:
-        got_first, got_second, got_near = (
-            [jnp.concatenate(g, axis=0)] for g in (got_first, got_second, got_near)
-        )
+    got_second = [swap(second[k], middle + k, n_seq) for k in range(half_cross)]
+
+    def parts(found):
+        if merged:
+            pieces = [a[r : r + rows, c : c + span] for a, r, c in found]
+            return [jnp.concatenate(pieces, axis=0)], [(0, 0, len(found) * rows, 0)]
+        return [a for a, _, _ in found], [(i, r, rows, c) for i, (_, r, c) in enumerate(found)]
+
+    near_parts = [[(a, 0, half * span) for a in got_near] for half in range(kvh)]
+    cross_parts = [
+        [(a, 0, 0) for a in got] + [(a, 0, half * span) for a in got_far]
+        for half, got in enumerate((got_first, got_second))
+    ]
+    arrays, where = parts(near_parts[0])
+    waits = got_first
+    count = pl.pallas_call(
+        functools.partial(count_kernel, 0, rows, where),
+        out_shape=pltpu.VMEM((max(16, n_seq), 128), F32),
+        in_specs=[vmem()] * len(arrays) + [pl.BlockSpec(memory_space=pl.ANY)] * len(waits),
+        out_specs=vmem(),
+        compiler_params=params(),
+        name="count",
+    )(*arrays, *waits)
 
     steps = 4
     cols = span // steps
-
-    def columns(arrays, start):
-        return [pl.BlockSpec((a.shape[0], cols), lambda i: (0, start + i)) for a in arrays]
-
+    scratch = [pltpu.VMEM((steps, toks, cols), BF16), pltpu.SemaphoreType.DMA((steps,))]
+    out_shape = jax.ShapeDtypeStruct((toks, width), BF16)
+    anywhere = pl.BlockSpec(memory_space=pl.ANY)
+    arrays, where = parts(near_parts[0] + cross_parts[0])
     out, sel = pl.pallas_call(
-        functools.partial(first_kernel, n_seq, rows),
-        grid=(steps,),
-        out_shape=[
-            jax.ShapeDtypeStruct((toks, width), BF16),
-            jax.ShapeDtypeStruct((toks, n_seq * rows), BF16),
-        ],
-        in_specs=columns(got_near, 0) + columns(got_first, 0),
-        out_specs=[
-            pl.BlockSpec((toks, cols), lambda i: (0, i)),
-            whole_block((toks, n_seq * rows)),
-        ],
-        scratch_shapes=[pltpu.VMEM((toks, n_seq * rows), BF16)],
+        functools.partial(place_kernel, n_seq, rows, middle, 0, where),
+        out_shape=[out_shape, pltpu.VMEM((toks, n_seq * rows), BF16)],
+        in_specs=[vmem()] * (1 + len(arrays)),
+        out_specs=[anywhere, vmem()],
+        scratch_shapes=scratch,
         compiler_params=params(),
         name="place_first",
-    )(*got_near, *got_first)
-    operands = [sel, *got_near, *got_second, out]
+    )(count, *arrays)
+    arrays, where = parts(near_parts[1] + cross_parts[1])
     return pl.pallas_call(
-        functools.partial(second_kernel, span),
-        out_shape=jax.ShapeDtypeStruct((toks, width), BF16),
-        in_specs=[vmem()] * (len(operands) - 1) + [pl.BlockSpec(memory_space=pl.ANY)],
-        out_specs=pl.BlockSpec(memory_space=pl.ANY),
-        scratch_shapes=[pltpu.VMEM((steps, toks, cols), BF16), pltpu.SemaphoreType.DMA((steps,))],
-        input_output_aliases={len(operands) - 1: 0},
+        functools.partial(place_kernel, n_seq, rows, middle, 1, where),
+        out_shape=out_shape,
+        in_specs=[vmem()] * (1 + len(arrays)) + [anywhere],
+        out_specs=anywhere,
+        scratch_shapes=scratch,
+        input_output_aliases={1 + len(arrays): 0},
         compiler_params=params(),
         name="place_second",
-    )(*operands)
+    )(sel, *arrays, out)
 
 
 def solution(mesh):

time: 68.7 us -> 67.9 us (0.988)
  the two profiles are of different devices: /device:TPU:21 before, /device:TPU:0 now
where the time goes in v5:
time: 67.9 us; the launch traced here: 67.8 us
  waiting for transfers between devices  32.7 us (48%)
  starting transfers between devices  23 us (34%)
  Pallas kernels  12 us (18%)
    ppermute x9, waiting for transfers between devices, swap(): return lax.ppermute(array, 'seq', [(i, i ^ by) for i in range(size)])  30.3 us
    ppermute x9, starting transfers between devices, swap(): return lax.ppermute(array, 'seq', [(i, i ^ by) for i in range(size)])  14.6 us
    ppermute x2, starting transfers between devices, per_device(): lax.ppermute(held, 'seq', [(i, i + by) for i in range(n_seq - by)])  8.38 us
    pallas_call x2, Pallas kernels, attend(): pl.pallas_call(functools.partial(attend_kernel, half, BATCH, n_cross), ou...  4.82 us
    pallas_call x1, Pallas kernels, per_device(): pl.pallas_call(project_kernel, out_shape=[pltpu.VMEM((held_rows, 2 * kv),...  4.02 us
    ppermute x2, waiting for transfers between devices, per_device(): lax.ppermute(held, 'seq', [(i, i + by) for i in range(n_seq - by)])  2.32 us
  transfers between devices with their start and end apart: 11, of which 7 were waited for; matrix products, arithmetic and copies ran while one was open for 0% of the time, Pallas kernels for 7%

profile of v5, /device:TPU:0, one launch (start us, length us, event | category | flops | bytes accessed | tf_op | source)
XLA Modules:
  0.0 67.8 jit_solution(16042734536050817076)
XLA Ops:
  0.0 0.0 copy-start.1
  0.0 0.0 copy-start.2
  0.0 0.0 copy-start
  0.0 4.0 %project.1 = (bf16[160,512]{1,0:T(8,128)(2,1)S(1)}, bf16[128,4096]{1,0:T(8,128)(2,1)S(1)}, bf16[128,128]{1,0:T(8,128)(2,1)S(1)}, f32[8,640]{1,0:T(8,128)S(1)}) custom-call(s32[16]{0:T(128)} %lens_ref.1, bf16[512,1024]{1,0:T(8,128)(2,1)} %x_hbm.1, f32[4,1024]{1,0:T(4,128)} %taps_hbm.1, f32[1,4096]{1,0:T(1,128)} %bitcast.1, bf16[4096,256]{1,0:T(8,128)(2,1)} %wk_hbm.1, ...), custom_call_target="tpu_custom_call" | custom-call | tf_op jit(solution)/shard_map/project/pallas_call | solution.py:375
  4.0 4.9 %collective-permute-start.1 = (bf16[160,512]{1,0:T(8,128)(2,1)S(1)}, bf16[160,512]{1,0:T(8,128)(2,1)S(1)}, u32[]{:S(2)}, u32[]{:S(2)}) collective-permute-start(bf16[160,512]{1,0:T(8,128)(2,1)S(1)} %get-tuple-element.26.own_ref), channel_id=1, source_target_pairs={{0,2},{1,3},{2,4},{3,5},{4,6},{5,7},{8,10},{9,11},{10,12},{11,13},... | collective-permute-start | bytes 491528 | tf_op jit(solution)/shard_map/ppermute | solution.py:411
  9.0 3.4 %collective-permute-start = (bf16[160,512]{1,0:T(8,128)(2,1)S(1)}, bf16[160,512]{1,0:T(8,128)(2,1)S(1)}, u32[]{:S(2)}, u32[]{:S(2)}) collective-permute-start(bf16[160,512]{1,0:T(8,128)(2,1)S(1)} %get-tuple-element.26.own_ref), channel_id=1, source_target_pairs={{0,1},{1,2},{2,3},{3,4},{4,5},{5,6},{6,7},{8,9},{9,10},{10,11},{11... | collective-permute-start | bytes 491528 | tf_op jit(solution)/shard_map/ppermute | solution.py:411
  12.4 0.0 copy-done.1
  12.4 0.0 copy-done.2
  12.5 0.8 %plan.1 = (f32[128,384]{1,0:T(8,128)S(1)}, bf16[256,128]{1,0:T(8,128)(2,1)S(1)}) custom-call(s32[16]{0:T(128)S(1)} %copy-done.1, s32[32]{0:T(128)S(1)} %copy-done.2), custom_call_target="tpu_custom_call" | custom-call | tf_op jit(solution)/shard_map/plan/pallas_call | solution.py:415
  13.3 0.0 collective-permute-done.1.two_ref
  13.3 2.3 %collective-permute-done.one_ref = bf16[160,512]{1,0:T(8,128)(2,1)S(1)} collective-permute-done((bf16[160,512]{1,0:T(8,128)(2,1)S(1)}, bf16[160,512]{1,0:T(8,128)(2,1)S(1)}, u32[]{:S(2)}, u32[]{:S(2)}) %collective-permute-start) | collective-permute-done | bytes 163872 | tf_op jit(solution)/shard_map/ppermute | solution.py:411
  15.6 0.0 copy-done
  15.6 2.0 %attend_half_0.1 = (bf16[32,2048]{1,0:T(8,128)(2,1)S(1)}, bf16[32,2048]{1,0:T(8,128)(2,1)S(1)}, bf16[128,2048]{1,0:T(8,128)(2,1)S(1)}) custom-call(bf16[128,128]{1,0:T(8,128)(2,1)S(1)} %get-tuple-element.24.lat_ref, f32[8,640]{1,0:T(8,128)S(1)} %get-tuple-element.25.edge_ref, bf16[160,512]{1,0:T(8,128)(2,1)S(1)} %get-tuple-element.26.own_ref, ...), custom_call_target="tpu_custom_call" | custom-call | tf_op jit(solution)/shard_map/attend_half_0/pallas_call | solution.py:441
  17.6 4.9 %collective-permute-start.5 = (bf16[32,2048]{1,0:T(8,128)(2,1)S(1)}, bf16[32,2048]{1,0:T(8,128)(2,1)S(1)}, u32[]{:S(2)}, u32[]{:S(2)}) collective-permute-start(bf16[32,2048]{1,0:T(8,128)(2,1)S(1)} %get-tuple-element.35), channel_id=1, source_target_pairs={{0,4},{1,5},{2,6},{3,7},{4,0},{5,1},{6,2},{7,3},{8,12},{9,13},{10,... | collective-permute-start | bytes 393224 | tf_op jit(solution)/shard_map/ppermute | solution.py:326
  22.5 0.0 collective-permute-start.6
  22.5 2.8 %attend_half_1.1 = (bf16[32,2048]{1,0:T(8,128)(2,1)S(1)}, bf16[32,2048]{1,0:T(8,128)(2,1)S(1)}, bf16[32,4096]{1,0:T(8,128)(2,1)S(1)}, bf16[32,4096]{1,0:T(8,128)...) custom-call(bf16[128,128]{1,0:T(8,128)(2,1)S(1)} %get-tuple-element., ...), custom_call_target="tpu_custom_call" | custom-call | tf_op jit(solution)/shard_map/attend_half_1/pallas_call | solution.py:441
  25.3 1.6 %collective-permute-start.2 = (bf16[32,4096]{1,0:T(8,128)(2,1)S(1)}, bf16[32,4096]{1,0:T(8,128)(2,1)S(1)}, u32[]{:S(2)}, u32[]{:S(2)}) collective-permute-start(bf16[32,4096]{1,0:T(8,128)(2,1)S(1)} %get-tuple-element.32), channel_id=1, source_target_pairs={{0,1},{1,0},{2,3},{3,2},{4,5},{5,4},{6,7},{7,6},{8,9},{9,8},{10,11... | collective-permute-start | bytes 786440 | tf_op jit(solution)/shard_map/ppermute | solution.py:326
  26.9 1.8 %collective-permute-start.3 = (bf16[32,4096]{1,0:T(8,128)(2,1)S(1)}, bf16[32,4096]{1,0:T(8,128)(2,1)S(1)}, u32[]{:S(2)}, u32[]{:S(2)}) collective-permute-start(bf16[32,4096]{1,0:T(8,128)(2,1)S(1)} %get-tuple-element.33), channel_id=1, source_target_pairs={{0,2},{1,3},{2,0},{3,1},{4,6},{5,7},{6,4},{7,5},{8,10},{9,11},{10,... | collective-permute-start | bytes 786440 | tf_op jit(solution)/shard_map/ppermute | solution.py:326
  28.7 0.2 collective-permute-start.4
  28.9 3.2 %collective-permute-done.5.refs_4_.refs_5_ = bf16[32,2048]{1,0:T(8,128)(2,1)S(1)} collective-permute-done((bf16[32,2048]{1,0:T(8,128)(2,1)S(1)}, bf16[32,2048]{1,0:T(8,128)(2,1)S(1)}, u32[]{:S(2)}, u32[]{:S(2)}) %collective-permute-start.5) | collective-permute-done | bytes 131104 | tf_op jit(solution)/shard_map/ppermute | solution.py:326
  32.1 2.4 %collective-permute-start.7 = (bf16[32,4096]{1,0:T(8,128)(2,1)S(1)}, bf16[32,4096]{1,0:T(8,128)(2,1)S(1)}, u32[]{:S(2)}, u32[]{:S(2)}) collective-permute-start(bf16[32,4096]{1,0:T(8,128)(2,1)S(1)} %get-tuple-element.37), channel_id=1, source_target_pairs={{0,6},{1,7},{2,4},{3,5},{4,2},{5,3},{6,0},{7,1},{8,14},{9,15},{10,... | collective-permute-start | bytes 786440 | tf_op jit(solution)/shard_map/ppermute | solution.py:326
  34.5 0.0 collective-permute-done.6.refs_5_.refs_6_
  34.5 3.7 %collective-permute-start.8 = (bf16[32,4096]{1,0:T(8,128)(2,1)S(1)}, bf16[32,4096]{1,0:T(8,128)(2,1)S(1)}, u32[]{:S(2)}, u32[]{:S(2)}) collective-permute-start(bf16[32,4096]{1,0:T(8,128)(2,1)S(1)} %get-tuple-element.38), channel_id=1, source_target_pairs={{0,7},{1,6},{2,5},{3,4},{4,3},{5,2},{6,1},{7,0},{8,15},{9,14},{10,... | collective-permute-start | bytes 786440 | tf_op jit(solution)/shard_map/ppermute | solution.py:326
  38.2 0.0 collective-permute-done.2.refs_1_.refs_2_
  38.2 0.0 collective-permute-start.9
  38.2 2.2 %collective-permute-done.3.refs_2_.refs_3_ = bf16[32,4096]{1,0:T(8,128)(2,1)S(1)} collective-permute-done((bf16[32,4096]{1,0:T(8,128)(2,1)S(1)}, bf16[32,4096]{1,0:T(8,128)(2,1)S(1)}, u32[]{:S(2)}, u32[]{:S(2)}) %collective-permute-start.3) | collective-permute-done | bytes 262176 | tf_op jit(solution)/shard_map/ppermute | solution.py:326
  40.4 0.0 collective-permute-start.10
  40.4 12.3 %collective-permute-done.4.refs_3_.refs_4_ = bf16[32,4096]{1,0:T(8,128)(2,1)S(1)} collective-permute-done((bf16[32,4096]{1,0:T(8,128)(2,1)S(1)}, bf16[32,4096]{1,0:T(8,128)(2,1)S(1)}, u32[]{:S(2)}, u32[]{:S(2)}) %collective-permute-start.4) | collective-permute-done | bytes 262176 | tf_op jit(solution)/shard_map/ppermute | solution.py:326
  52.7 0.1 count.1.refs_0_
  52.8 0.0 collective-permute-done.7.refs_7_
  52.8 2.3 %collective-permute-done.8.refs_8_ = bf16[32,4096]{1,0:T(8,128)(2,1)S(1)} collective-permute-done((bf16[32,4096]{1,0:T(8,128)(2,1)S(1)}, bf16[32,4096]{1,0:T(8,128)(2,1)S(1)}, u32[]{:S(2)}, u32[]{:S(2)}) %collective-permute-start.8) | collective-permute-done | bytes 262176 | tf_op jit(solution)/shard_map/ppermute | solution.py:326
  55.1 1.2 %place_first.1 = (bf16[128,4096]{1,0:T(8,128)(2,1)}, bf16[128,256]{1,0:T(8,128)(2,1)S(1)}) custom-call(f32[16,128]{1,0:T(8,128)S(1)} %count.1.refs_0_, bf16[32,4096]{1,0:T(8,128)(2,1)S(1)} %get-tuple-element.31.refs_0_.refs_1_, bf16[32,4096]{1,0:T(8,128)(2,1)S(1)} %collective-permute-done.2.refs_1_.refs_2_, ...), custom_call_target="tpu_custom_call" | custom-call | tf_op jit(solution)/shard_map/place_first/pallas_call | solution.py:498
  56.4 9.2 %collective-permute-done.9.refs_5_ = bf16[32,2048]{1,0:T(8,128)(2,1)S(1)} collective-permute-done((bf16[32,2048]{1,0:T(8,128)(2,1)S(1)}, bf16[32,2048]{1,0:T(8,128)(2,1)S(1)}, u32[]{:S(2)}, u32[]{:S(2)}) %collective-permute-start.9) | collective-permute-done | bytes 131104 | tf_op jit(solution)/shard_map/ppermute | solution.py:326
  65.5 1.2 %collective-permute-done.10.refs_6_ = bf16[32,2048]{1,0:T(8,128)(2,1)S(1)} collective-permute-done((bf16[32,2048]{1,0:T(8,128)(2,1)S(1)}, bf16[32,2048]{1,0:T(8,128)(2,1)S(1)}, u32[]{:S(2)}, u32[]{:S(2)}) %collective-permute-start.10) | collective-permute-done | bytes 131104 | tf_op jit(solution)/shard_map/ppermute | solution.py:326
  66.7 1.0 %place_second.1 = bf16[128,4096]{1,0:T(8,128)(2,1)} custom-call(bf16[128,256]{1,0:T(8,128)(2,1)S(1)} %get-tuple-element.39.refs_0_, bf16[32,4096]{1,0:T(8,128)(2,1)S(1)} %get-tuple-element.31.refs_0_.refs_1_, bf16[32,4096]{1,0:T(8,128)(2,1)S(1)} %collective-permute-done.2.refs_1_.refs_2_, ...), custom_call_target="tpu_custom_call", output_to_operand_aliasing={{}: (9, {})} | custom-call | tf_op jit(solution)/shard_map/place_second/pallas_call | solution.py:508
Async XLA Ops:
  0.0 12.4 %copy-start.1 = (s32[16]{0:T(128)S(1)}, s32[16]{0:T(128)}, u32[]{:S(2)}) copy-start(s32[16]{0:T(128)} %lens_ref.1) | copy-start | bytes 196
  0.0 12.4 %copy-start.2 = (s32[32]{0:T(128)S(1)}, s32[32]{0:T(128)}, u32[]{:S(2)}) copy-start(s32[32]{0:T(128)} %dest_ref.1) | copy-start | bytes 388
  0.0 15.6 %copy-start = (bf16[128,4096]{1,0:T(8,128)(2,1)S(1)}, bf16[128,4096]{1,0:T(8,128)(2,1)}, u32[]{:S(2)}) copy-start(bf16[128,4096]{1,0:T(8,128)(2,1)} %wq_ref.3) | copy-start | bytes 3145732
  4.0 9.2 %collective-permute-start.1 = (bf16[160,512]{1,0:T(8,128)(2,1)S(1)}, bf16[160,512]{1,0:T(8,128)(2,1)S(1)}, u32[]{:S(2)}, u32[]{:S(2)}) collective-permute-start(bf16[160,512]{1,0:T(8,128)(2,1)S(1)} %get-tuple-element.26.own_ref), channel_id=1, source_target_pairs={{0,2},{1,3},{2,4},{3,5},{4,6},{5,7},{8,10},{9,11},{10,12},{11,13},... | collective-permute-start | bytes 491528 | tf_op jit(solution)/shard_map/ppermute | solution.py:411
  9.0 6.6 %collective-permute-start = (bf16[160,512]{1,0:T(8,128)(2,1)S(1)}, bf16[160,512]{1,0:T(8,128)(2,1)S(1)}, u32[]{:S(2)}, u32[]{:S(2)}) collective-permute-start(bf16[160,512]{1,0:T(8,128)(2,1)S(1)} %get-tuple-element.26.own_ref), channel_id=1, source_target_pairs={{0,1},{1,2},{2,3},{3,4},{4,5},{5,6},{6,7},{8,9},{9,10},{10,11},{11... | collective-permute-start | bytes 491528 | tf_op jit(solution)/shard_map/ppermute | solution.py:411
  17.6 14.5 %collective-permute-start.5 = (bf16[32,2048]{1,0:T(8,128)(2,1)S(1)}, bf16[32,2048]{1,0:T(8,128)(2,1)S(1)}, u32[]{:S(2)}, u32[]{:S(2)}) collective-permute-start(bf16[32,2048]{1,0:T(8,128)(2,1)S(1)} %get-tuple-element.35), channel_id=1, source_target_pairs={{0,4},{1,5},{2,6},{3,7},{4,0},{5,1},{6,2},{7,3},{8,12},{9,13},{10,... | collective-permute-start | bytes 393224 | tf_op jit(solution)/shard_map/ppermute | solution.py:326
  22.5 12.0 %collective-permute-start.6 = (bf16[32,2048]{1,0:T(8,128)(2,1)S(1)}, bf16[32,2048]{1,0:T(8,128)(2,1)S(1)}, u32[]{:S(2)}, u32[]{:S(2)}) collective-permute-start(bf16[32,2048]{1,0:T(8,128)(2,1)S(1)} %get-tuple-element.36), channel_id=1, source_target_pairs={{0,5},{1,4},{2,7},{3,6},{4,1},{5,0},{6,3},{7,2},{8,13},{9,12},{10,... | collective-permute-start | bytes 393224 | tf_op jit(solution)/shard_map/ppermute | solution.py:326
  25.3 12.9 %collective-permute-start.2 = (bf16[32,4096]{1,0:T(8,128)(2,1)S(1)}, bf16[32,4096]{1,0:T(8,128)(2,1)S(1)}, u32[]{:S(2)}, u32[]{:S(2)}) collective-permute-start(bf16[32,4096]{1,0:T(8,128)(2,1)S(1)} %get-tuple-element.32), channel_id=1, source_target_pairs={{0,1},{1,0},{2,3},{3,2},{4,5},{5,4},{6,7},{7,6},{8,9},{9,8},{10,11... | collective-permute-start | bytes 786440 | tf_op jit(solution)/shard_map/ppermute | solution.py:326
  26.9 13.5 %collective-permute-start.3 = (bf16[32,4096]{1,0:T(8,128)(2,1)S(1)}, bf16[32,4096]{1,0:T(8,128)(2,1)S(1)}, u32[]{:S(2)}, u32[]{:S(2)}) collective-permute-start(bf16[32,4096]{1,0:T(8,128)(2,1)S(1)} %get-tuple-element.33), channel_id=1, source_target_pairs={{0,2},{1,3},{2,0},{3,1},{4,6},{5,7},{6,4},{7,5},{8,10},{9,11},{10,... | collective-permute-start | bytes 786440 | tf_op jit(solution)/shard_map/ppermute | solution.py:326
  28.7 24.0 %collective-permute-start.4 = (bf16[32,4096]{1,0:T(8,128)(2,1)S(1)}, bf16[32,4096]{1,0:T(8,128)(2,1)S(1)}, u32[]{:S(2)}, u32[]{:S(2)}) collective-permute-start(bf16[32,4096]{1,0:T(8,128)(2,1)S(1)} %get-tuple-element.34), channel_id=1, source_target_pairs={{0,3},{1,2},{2,1},{3,0},{4,7},{5,6},{6,5},{7,4},{8,11},{9,10},{10,... | collective-permute-start | bytes 786440 | tf_op jit(solution)/shard_map/ppermute | solution.py:326
  32.1 20.7 %collective-permute-start.7 = (bf16[32,4096]{1,0:T(8,128)(2,1)S(1)}, bf16[32,4096]{1,0:T(8,128)(2,1)S(1)}, u32[]{:S(2)}, u32[]{:S(2)}) collective-permute-start(bf16[32,4096]{1,0:T(8,128)(2,1)S(1)} %get-tuple-element.37), channel_id=1, source_target_pairs={{0,6},{1,7},{2,4},{3,5},{4,2},{5,3},{6,0},{7,1},{8,14},{9,15},{10,... | collective-permute-start | bytes 786440 | tf_op jit(solution)/shard_map/ppermute | solution.py:326
  34.5 20.6 %collective-permute-start.8 = (bf16[32,4096]{1,0:T(8,128)(2,1)S(1)}, bf16[32,4096]{1,0:T(8,128)(2,1)S(1)}, u32[]{:S(2)}, u32[]{:S(2)}) collective-permute-start(bf16[32,4096]{1,0:T(8,128)(2,1)S(1)} %get-tuple-element.38), channel_id=1, source_target_pairs={{0,7},{1,6},{2,5},{3,4},{4,3},{5,2},{6,1},{7,0},{8,15},{9,14},{10,... | collective-permute-start | bytes 786440 | tf_op jit(solution)/shard_map/ppermute | solution.py:326
  38.2 27.3 %collective-permute-start.9 = (bf16[32,2048]{1,0:T(8,128)(2,1)S(1)}, bf16[32,2048]{1,0:T(8,128)(2,1)S(1)}, u32[]{:S(2)}, u32[]{:S(2)}) collective-permute-start(bf16[32,2048]{1,0:T(8,128)(2,1)S(1)} %get-tuple-element.40), channel_id=1, source_target_pairs={{0,4},{1,5},{2,6},{3,7},{4,0},{5,1},{6,2},{7,3},{8,12},{9,13},{10,... | collective-permute-start | bytes 393224 | tf_op jit(solution)/shard_map/ppermute | solution.py:326
  40.4 26.3 %collective-permute-start.10 = (bf16[32,2048]{1,0:T(8,128)(2,1)S(1)}, bf16[32,2048]{1,0:T(8,128)(2,1)S(1)}, u32[]{:S(2)}, u32[]{:S(2)}) collective-permute-start(bf16[32,2048]{1,0:T(8,128)(2,1)S(1)} %get-tuple-element.41), channel_id=1, source_target_pairs={{0,5},{1,4},{2,7},{3,6},{4,1},{5,0},{6,3},{7,2},{8,13},{9,12},{10,... | collective-permute-start | bytes 393224 | tf_op jit(solution)/shard_map/ppermute | solution.py:326

commit v6 on v5

--- a/solution.py
+++ b/solution.py
@@ -16,7 +16,7 @@
 PAD = 8
 EDGE = 16
 MARK = 2.0**120
-BATCH = 8
+BATCH = (8, 4)
 MIB = 1024 * 1024
 F32 = jnp.float32
 BF16 = jnp.bfloat16
@@ -118,8 +118,9 @@
             row = iota((EDGE, 128), 0)
             u_ref[toks:, at : at + 128] = jnp.where(row == 0, corr * gain, 0.0).astype(BF16)
             r, o = at // part, at % part
-            fold_ref[r : r + 1, o : o + 128] = short[0:1]
-            fold_ref[8 + r : 9 + r, o : o + 128] = corr
+            fold_ref[8 + r : 9 + r, o : o + 128] = short[0:1]
+            if slot < KCONV - 1:
+                fold_ref[2 + r : 3 + r, o : o + 128] = corr
 
     def project(first, count):
         for group in weights[first : first + count]:
@@ -136,21 +137,28 @@
         conv(slot)
     acc_ref[...] += project(middle, SHORTEN - middle)
     rs = lax.rsqrt(jnp.sum(squares[0], axis=1, keepdims=True) * (1.0 / width) + 1e-06)
-    out_ref[0:toks, :] = (acc_ref[0:toks, 0 : 2 * kv] * rs).astype(BF16)
+    scale = jnp.where(iota((toks, 1), 0) == 0, 1.0, rs)
+    out_ref[0:toks, :] = (acc_ref[0:toks, 0 : 2 * kv] * scale).astype(BF16)
     lat_ref[...] = (acc_ref[0:toks, 2 * kv :] * rs).astype(BF16)
     edge_ref[...] = acc_ref[0:8, :]
-    row = iota((EDGE, 2 * kv), 0)
-    low = jnp.concatenate(
+    fold_ref[0:1, :] = acc_ref[toks : toks + 1, 0 : 2 * kv]
+    fold_ref[1:2, :] = jnp.concatenate(
         [acc_ref[toks : toks + 1, 2 * kv :], jnp.zeros((1, 2 * kv - rank), F32)], axis=1
     )
-    sums = jnp.where(row == 0, acc_ref[0:1, 0 : 2 * kv], 0.0)
-    sums = jnp.where(row == 1, acc_ref[toks : toks + 1, 0 : 2 * kv], sums)
-    out_ref[toks : toks + EDGE, :] = jnp.where(row == 2, low, sums).astype(BF16)
-    out_ref[toks + EDGE : toks + 2 * EDGE, 0:part] = fold_ref[...].astype(BF16)
-
-
-def plan_kernel(n_seq, rows, lens_ref, dest_ref, bias_ref, pick_ref):
-    toks, keys = bias_ref.shape
+    out_ref[toks:, :] = fold_ref[...].astype(BF16)
+
+
+def scaled_query(latent, weights):
+    factor = math.log2(math.e) / math.sqrt(weights.shape[0])
+    return (jnp.dot(latent, weights, preferred_element_type=F32) * factor).astype(BF16)
+
+
+def plan_kernel(n_seq, rows, lens_ref, dest_ref, lat_ref, wq_ref, limit_ref, pick_ref, query_ref):
+    step = min(512, wq_ref.shape[1])
+    for at in range(0, wq_ref.shape[1], step):
+        cols = slice(at, at + step)
+        query_ref[:, cols] = scaled_query(lat_ref[...], wq_ref[:, cols])
+    toks, keys = limit_ref.shape
     me = lax.axis_index("seq")
     pos = me * toks + iota((toks, 128), 0)
 
@@ -163,7 +171,7 @@
     )
     for at in range(0, keys, 128):
         key = (me - BACK) * toks + at + iota((toks, 128), 1)
-        bias_ref[:, at : at + 128] = jnp.where((key >= begin) & (key <= pos), 0.0, -1e30)
+        limit_ref[:, at : at + 128] = jnp.where((key >= begin) & (key <= pos), jnp.inf, -jnp.inf)
     lane = iota((8, toks), 1)
     panel = lane // PANEL
     dest = jnp.full((8, toks), -1, jnp.int32)
@@ -185,37 +193,35 @@
         ref[...] = placed[k * rows : (k + 1) * rows]
 
 
-def attend_kernel(half, batch, n_cross, lat_ref, edge_ref, own_ref, one_ref, two_ref, bias_ref, pick_ref, wq_ref, short_ref, *refs):
-    refs, (k_ref, v_ref, query_ref, corr_ref, layer_ref) = refs[:-5], refs[-5:]
+def attend_kernel(half, batch, n_cross, query_ref, edge_ref, own_ref, one_ref, two_ref, limit_ref, pick_ref, wq_ref, short_ref, *refs):
+    refs, (k_ref, v_ref, corr_ref, layer_ref) = refs[:-4], refs[-4:]
     if half == 0:
         cross_refs, out_layer_ref = refs[:-1], refs[-1]
     else:
         past_ref, refs = refs[0], refs[1:]
         cross_refs, far_refs, near_refs = refs[:n_cross], refs[n_cross : 2 * n_cross], refs[2 * n_cross :]
-    toks, hd = lat_ref.shape
+    toks, hd = query_ref.shape[0], k_ref.shape[1]
     wide = layer_ref.shape[1]
     heads = wide // hd
     kv = own_ref.shape[1] // 2
     part = own_ref.shape[1]
     width = 8 * part
-    keys = bias_ref.shape[1]
+    keys = limit_ref.shape[1]
 
     def root(first):
         total = jnp.sum(jnp.sum(first * first, axis=1, keepdims=True), axis=0, keepdims=True)
         return lax.rsqrt(total * (1.0 / width) + 1e-06)
 
-    fold = slice(toks + EDGE, toks + 2 * EDGE)
-    sums = slice(toks, toks + EDGE)
-    own_fold = own_ref[fold, :].astype(F32)
-    one_fold = one_ref[fold, :].astype(F32)
-    two_fold = two_ref[fold, :].astype(F32)
-    one_sums = one_ref[sums, :].astype(F32)
-    two_sums = two_ref[sums, :].astype(F32)
-    scale = root((own_fold[0:8] + one_fold[8:16]).astype(BF16).astype(F32))
-    own_kv = scale * (edge_ref[0:1, 0 : 2 * kv] + one_sums[1:2])
-    own_lat = scale * (edge_ref[0:1, 2 * kv :] + one_sums[2:3, 0:hd])
-    scale = root((one_fold[0:8] + two_fold[8:16]).astype(BF16).astype(F32))
-    one_kv = scale * (one_sums[0:1] + two_sums[1:2])
+    def tail(fold):
+        return jnp.concatenate([fold[2:8], jnp.zeros((2, part), F32)], axis=0)
+
+    own_fold, one_fold, two_fold = (ref[toks:, :].astype(F32) for ref in (own_ref, one_ref, two_ref))
+    one_tail = tail(one_fold)
+    scale = root((own_fold[8:16] + one_tail).astype(BF16).astype(F32))
+    own_kv = scale * (edge_ref[0:1, 0 : 2 * kv] + one_fold[0:1])
+    own_lat = scale * (edge_ref[0:1, 2 * kv :] + one_fold[1:2, 0:hd])
+    scale = root((one_fold[8:16] + tail(two_fold)).astype(BF16).astype(F32))
+    one_kv = scale * (one_ref[0:EDGE, :].astype(F32)[0:1] + two_fold[0:1])
     row = iota((EDGE, 2 * kv), 0)
     tops = [
         two_ref[0:EDGE, :],
@@ -231,23 +237,21 @@
         v_ref[at : at + EDGE, 0:hd] = tops[b][:, v_cols]
         v_ref[at + EDGE : at + toks, 0:hd] = ref[EDGE:toks, v_cols]
         v_ref[at : at + toks, hd:] = jnp.ones((toks, hd), BF16)
-    row = iota((EDGE, hd), 0)
-    query_ref[0:EDGE, :] = jnp.where(row == 0, own_lat, lat_ref[0:EDGE, :].astype(F32)).astype(BF16)
-    query_ref[EDGE:, :] = lat_ref[EDGE:, :]
     for c in range(wide // part):
         at = half * (wide // part) + c
-        corr_ref[:, c * part : (c + 1) * part] = one_fold[8 + at : 9 + at]
-
-    log_scale = math.log2(math.e) / math.sqrt(hd)
-    wq = wq_ref[:, half * wide : (half + 1) * wide]
-    query = (jnp.dot(query_ref[...], wq, preferred_element_type=F32) * log_scale).astype(BF16)
+        corr_ref[:, c * part : (c + 1) * part] = one_tail[at : at + 1]
+    first_lat = jnp.broadcast_to(own_lat, (EDGE, hd)).astype(BF16)
+    first_query = scaled_query(first_lat, wq_ref[:, half * wide : (half + 1) * wide])
+    query = query_ref[:, half * wide : (half + 1) * wide]
+    top = jnp.where(iota((EDGE, wide), 0) == 0, first_query.astype(F32), query[0:EDGE].astype(F32)).astype(BF16)
+    query = jnp.concatenate([top, query[EDGE:]], axis=0)
     key_all, value_all = k_ref[...], v_ref[...]
     for at in range(0, heads, batch):
         part_q = [query[:, h * hd : (h + 1) * hd] for h in range(at, at + batch)]
         scores = lax.dot_general(
             jnp.concatenate(part_q, axis=0), key_all, (((1,), (1,)), ((), ())), preferred_element_type=F32
         )
-        scores = scores.reshape(batch, toks, keys) + bias_ref[...][None]
+        scores = jnp.minimum(scores.reshape(batch, toks, keys), limit_ref[...][None])
         top = jnp.max(scores, axis=2, keepdims=True)
         probs = jnp.exp2(scores - top).astype(BF16).reshape(batch * toks, keys)
         mixed = jnp.dot(probs, value_all, preferred_element_type=F32)
@@ -370,7 +374,7 @@
     rows = slots * PANEL
     merged = rows % 16 != 0
     keys = (BACK + 1) * toks
-    held_rows = toks + 2 * EDGE
+    held_rows = toks + EDGE
 
     held, short, latent, edge = pl.pallas_call(
         project_kernel,
@@ -412,17 +416,18 @@
         for by in range(1, BACK + 1)
     ]
 
-    bias, pick = pl.pallas_call(
+    limit, pick, query = pl.pallas_call(
         functools.partial(plan_kernel, n_seq, rows),
         out_shape=[
             pltpu.VMEM((toks, keys), F32),
             pltpu.VMEM((n_seq * rows, toks), BF16),
+            pltpu.VMEM((toks, width), BF16),
         ],
-        in_specs=[smem()] * 2,
-        out_specs=[vmem()] * 2,
+        in_specs=[smem()] * 2 + [vmem()] * 2,
+        out_specs=[vmem()] * 3,
         compiler_params=params(),
         name="plan",
-    )(doc_lengths, panel_dest)
+    )(doc_lengths, panel_dest, latent, w_qup)
 
     middle = n_seq // 2
     span = width // kvh
@@ -437,16 +442,15 @@
         return [arrays[0][i * height : (i + 1) * height] for i in range(count)]
 
     def attend(half, outs, n_cross, more):
-        operands = [latent, edge, held, *behind, bias, pick, w_qup, short, *more]
+        operands = [query, edge, held, *behind, limit, pick, w_qup, short, *more]
         return pl.pallas_call(
-            functools.partial(attend_kernel, half, BATCH, n_cross),
+            functools.partial(attend_kernel, half, BATCH[half], n_cross),
             out_shape=outs,
             in_specs=[vmem()] * len(operands),
             out_specs=[vmem()] * len(outs),
             scratch_shapes=[
                 pltpu.VMEM((keys, hd), BF16),
                 pltpu.VMEM((keys, 2 * hd), BF16),
-                pltpu.VMEM((toks, rank), BF16),
                 pltpu.VMEM((1, span), F32),
                 pltpu.VMEM((toks, span), BF16),
             ],

time: 67.9 us -> 67.5 us (level)
    ppermute x2, waiting for transfers between devices: 2.32 us -> 1.54 us  [per_device(): lax.ppermute(held, 'seq', [(i, i + by) for i in range(n_seq - by)])]
  transfers between devices with their start and end apart: 11 -> 11, of which waited for: 7 -> 8; matrix products, arithmetic and copies ran while one was open for 0% -> 0% of each run, Pallas kernels for 7% -> 8%
where the time goes in v6:
time: 67.5 us; the launch traced here: 67.3 us
  waiting for transfers between devices  32.1 us (48%)
  starting transfers between devices  23 us (34%)
  Pallas kernels  12.2 us (18%)
    ppermute x9, waiting for transfers between devices, swap(): return lax.ppermute(array, 'seq', [(i, i ^ by) for i in range(size)])  30.5 us
    ppermute x9, starting transfers between devices, swap(): return lax.ppermute(array, 'seq', [(i, i ^ by) for i in range(size)])  14.6 us
    ppermute x2, starting transfers between devices, per_device(): lax.ppermute(held, 'seq', [(i, i + by) for i in range(n_seq - by)])  8.38 us
    pallas_call x2, Pallas kernels, attend(): pl.pallas_call(functools.partial(attend_kernel, half, BATCH[half], n_cros...  4.54 us
    pallas_call x1, Pallas kernels, per_device(): pl.pallas_call(project_kernel, out_shape=[pltpu.VMEM((held_rows, 2 * kv),...  4.04 us
    ppermute x2, waiting for transfers between devices, per_device(): lax.ppermute(held, 'seq', [(i, i + by) for i in range(n_seq - by)])  1.54 us
  transfers between devices with their start and end apart: 11, of which 8 were waited for; matrix products, arithmetic and copies ran while one was open for 0% of the time, Pallas kernels for 8%

profile of v6, /device:TPU:0, one launch (start us, length us, event | category | flops | bytes accessed | tf_op | source)
XLA Modules:
  0.0 67.3 jit_solution(5683192568193895429)
XLA Ops:
  0.0 0.0 copy-start
  0.0 0.0 copy-start.1
  0.0 0.0 copy-start.2
  0.0 4.0 %project.1 = (bf16[144,512]{1,0:T(8,128)(2,1)S(1)}, bf16[128,4096]{1,0:T(8,128)(2,1)S(1)}, bf16[128,128]{1,0:T(8,128)(2,1)S(1)}, f32[8,640]{1,0:T(8,128)S(1)}) custom-call(s32[16]{0:T(128)} %lens_ref.1, bf16[512,1024]{1,0:T(8,128)(2,1)} %x_hbm.1, f32[4,1024]{1,0:T(4,128)} %taps_hbm.1, f32[1,4096]{1,0:T(1,128)} %bitcast.1, bf16[4096,256]{1,0:T(8,128)(2,1)} %wk_hbm.1, ...), custom_call_target="tpu_custom_call" | custom-call | tf_op jit(solution)/shard_map/project/pallas_call | solution.py:379
  4.1 4.9 %collective-permute-start.1 = (bf16[144,512]{1,0:T(8,128)(2,1)S(1)}, bf16[144,512]{1,0:T(8,128)(2,1)S(1)}, u32[]{:S(2)}, u32[]{:S(2)}) collective-permute-start(bf16[144,512]{1,0:T(8,128)(2,1)S(1)} %get-tuple-element.28.own_ref), channel_id=1, source_target_pairs={{0,2},{1,3},{2,4},{3,5},{4,6},{5,7},{8,10},{9,11},{10,12},{11,13},... | collective-permute-start | bytes 442376 | tf_op jit(solution)/shard_map/ppermute | solution.py:415
  9.0 3.4 %collective-permute-start = (bf16[144,512]{1,0:T(8,128)(2,1)S(1)}, bf16[144,512]{1,0:T(8,128)(2,1)S(1)}, u32[]{:S(2)}, u32[]{:S(2)}) collective-permute-start(bf16[144,512]{1,0:T(8,128)(2,1)S(1)} %get-tuple-element.28.own_ref), channel_id=1, source_target_pairs={{0,1},{1,2},{2,3},{3,4},{4,5},{5,6},{6,7},{8,9},{9,10},{10,11},{11... | collective-permute-start | bytes 442376 | tf_op jit(solution)/shard_map/ppermute | solution.py:415
  12.4 0.0 copy-done
  12.5 0.0 copy-done.1
  12.5 0.0 copy-done.2
  12.5 1.2 %plan.1 = (f32[128,384]{1,0:T(8,128)S(1)}, bf16[256,128]{1,0:T(8,128)(2,1)S(1)}, bf16[128,4096]{1,0:T(8,128)(2,1)S(1)}) custom-call(s32[16]{0:T(128)S(1)} %copy-done.1, s32[32]{0:T(128)S(1)} %copy-done.2, bf16[128,128]{1,0:T(8,128)(2,1)S(1)} %get-tuple-element.25.lat_ref, bf16[128,4096]{1,0:T(8,128)(2,1)S(1)} %copy-done), custom_call_target="tpu_custom_call" | custom-call | tf_op jit(solution)/shard_map/plan/pallas_call | solution.py:419
  13.7 0.0 collective-permute-done.1.two_ref
  13.7 1.5 %collective-permute-done.one_ref = bf16[144,512]{1,0:T(8,128)(2,1)S(1)} collective-permute-done((bf16[144,512]{1,0:T(8,128)(2,1)S(1)}, bf16[144,512]{1,0:T(8,128)(2,1)S(1)}, u32[]{:S(2)}, u32[]{:S(2)}) %collective-permute-start) | collective-permute-done | bytes 147488 | tf_op jit(solution)/shard_map/ppermute | solution.py:415
  15.2 2.0 %attend_half_0.1 = (bf16[32,2048]{1,0:T(8,128)(2,1)S(1)}, bf16[32,2048]{1,0:T(8,128)(2,1)S(1)}, bf16[128,2048]{1,0:T(8,128)(2,1)S(1)}) custom-call(bf16[128,4096]{1,0:T(8,128)(2,1)S(1)} %get-tuple-element.26.query_ref, f32[8,640]{1,0:T(8,128)S(1)} %get-tuple-element.27.edge_ref, bf16[144,512]{1,0:T(8,128)(2,1)S(1)} %get-tuple-element.28.own_ref, ...), custom_call_target="tpu_custom_call" | custom-call | tf_op jit(solution)/shard_map/attend_half_0/pallas_call | solution.py:446
  17.2 4.5 %collective-permute-start.5 = (bf16[32,2048]{1,0:T(8,128)(2,1)S(1)}, bf16[32,2048]{1,0:T(8,128)(2,1)S(1)}, u32[]{:S(2)}, u32[]{:S(2)}) collective-permute-start(bf16[32,2048]{1,0:T(8,128)(2,1)S(1)} %get-tuple-element.37), channel_id=1, source_target_pairs={{0,4},{1,5},{2,6},{3,7},{4,0},{5,1},{6,2},{7,3},{8,12},{9,13},{10,... | collective-permute-start | bytes 393224 | tf_op jit(solution)/shard_map/ppermute | solution.py:330
  21.8 0.4 collective-permute-start.6
  22.1 2.5 %attend_half_1.1 = (bf16[32,2048]{1,0:T(8,128)(2,1)S(1)}, bf16[32,2048]{1,0:T(8,128)(2,1)S(1)}, bf16[32,4096]{1,0:T(8,128)(2,1)S(1)}, bf16[32,4096]{1,0:T(8,128)...) custom-call(bf16[128,4096]{1,0:T(8,128)(2,1)S(1)} %get-tuple-element, ...), custom_call_target="tpu_custom_call" | custom-call | tf_op jit(solution)/shard_map/attend_half_1/pallas_call | solution.py:446
  24.7 1.2 %collective-permute-start.2 = (bf16[32,4096]{1,0:T(8,128)(2,1)S(1)}, bf16[32,4096]{1,0:T(8,128)(2,1)S(1)}, u32[]{:S(2)}, u32[]{:S(2)}) collective-permute-start(bf16[32,4096]{1,0:T(8,128)(2,1)S(1)} %get-tuple-element.34), channel_id=1, source_target_pairs={{0,1},{1,0},{2,3},{3,2},{4,5},{5,4},{6,7},{7,6},{8,9},{9,8},{10,11... | collective-permute-start | bytes 786440 | tf_op jit(solution)/shard_map/ppermute | solution.py:330
  25.9 1.8 %collective-permute-start.3 = (bf16[32,4096]{1,0:T(8,128)(2,1)S(1)}, bf16[32,4096]{1,0:T(8,128)(2,1)S(1)}, u32[]{:S(2)}, u32[]{:S(2)}) collective-permute-start(bf16[32,4096]{1,0:T(8,128)(2,1)S(1)} %get-tuple-element.35), channel_id=1, source_target_pairs={{0,2},{1,3},{2,0},{3,1},{4,6},{5,7},{6,4},{7,5},{8,10},{9,11},{10,... | collective-permute-start | bytes 786440 | tf_op jit(solution)/shard_map/ppermute | solution.py:330
  27.7 0.5 collective-permute-start.4
  28.2 2.9 %collective-permute-done.5.refs_4_.refs_5_ = bf16[32,2048]{1,0:T(8,128)(2,1)S(1)} collective-permute-done((bf16[32,2048]{1,0:T(8,128)(2,1)S(1)}, bf16[32,2048]{1,0:T(8,128)(2,1)S(1)}, u32[]{:S(2)}, u32[]{:S(2)}) %collective-permute-start.5) | collective-permute-done | bytes 131104 | tf_op jit(solution)/shard_map/ppermute | solution.py:330
  31.1 2.3 %collective-permute-start.7 = (bf16[32,4096]{1,0:T(8,128)(2,1)S(1)}, bf16[32,4096]{1,0:T(8,128)(2,1)S(1)}, u32[]{:S(2)}, u32[]{:S(2)}) collective-permute-start(bf16[32,4096]{1,0:T(8,128)(2,1)S(1)} %get-tuple-element.39), channel_id=1, source_target_pairs={{0,6},{1,7},{2,4},{3,5},{4,2},{5,3},{6,0},{7,1},{8,14},{9,15},{10,... | collective-permute-start | bytes 786440 | tf_op jit(solution)/shard_map/ppermute | solution.py:330
  33.4 0.3 collective-permute-done.6.refs_5_.refs_6_
  33.7 3.5 %collective-permute-start.8 = (bf16[32,4096]{1,0:T(8,128)(2,1)S(1)}, bf16[32,4096]{1,0:T(8,128)(2,1)S(1)}, u32[]{:S(2)}, u32[]{:S(2)}) collective-permute-start(bf16[32,4096]{1,0:T(8,128)(2,1)S(1)} %get-tuple-element.40), channel_id=1, source_target_pairs={{0,7},{1,6},{2,5},{3,4},{4,3},{5,2},{6,1},{7,0},{8,15},{9,14},{10,... | collective-permute-start | bytes 786440 | tf_op jit(solution)/shard_map/ppermute | solution.py:330
  37.1 0.0 collective-permute-done.2.refs_1_.refs_2_
  37.1 0.0 collective-permute-start.9
  37.1 2.4 %collective-permute-done.3.refs_2_.refs_3_ = bf16[32,4096]{1,0:T(8,128)(2,1)S(1)} collective-permute-done((bf16[32,4096]{1,0:T(8,128)(2,1)S(1)}, bf16[32,4096]{1,0:T(8,128)(2,1)S(1)}, u32[]{:S(2)}, u32[]{:S(2)}) %collective-permute-start.3) | collective-permute-done | bytes 262176 | tf_op jit(solution)/shard_map/ppermute | solution.py:330
  39.5 0.4 collective-permute-start.10
  39.9 11.1 %collective-permute-done.4.refs_3_.refs_4_ = bf16[32,4096]{1,0:T(8,128)(2,1)S(1)} collective-permute-done((bf16[32,4096]{1,0:T(8,128)(2,1)S(1)}, bf16[32,4096]{1,0:T(8,128)(2,1)S(1)}, u32[]{:S(2)}, u32[]{:S(2)}) %collective-permute-start.4) | collective-permute-done | bytes 262176 | tf_op jit(solution)/shard_map/ppermute | solution.py:330
  51.0 0.1 count.1.refs_0_
  51.1 0.0 collective-permute-done.7.refs_7_
  51.1 3.3 %collective-permute-done.8.refs_8_ = bf16[32,4096]{1,0:T(8,128)(2,1)S(1)} collective-permute-done((bf16[32,4096]{1,0:T(8,128)(2,1)S(1)}, bf16[32,4096]{1,0:T(8,128)(2,1)S(1)}, u32[]{:S(2)}, u32[]{:S(2)}) %collective-permute-start.8) | collective-permute-done | bytes 262176 | tf_op jit(solution)/shard_map/ppermute | solution.py:330
  54.5 1.2 %place_first.1 = (bf16[128,4096]{1,0:T(8,128)(2,1)}, bf16[128,256]{1,0:T(8,128)(2,1)S(1)}) custom-call(f32[16,128]{1,0:T(8,128)S(1)} %count.1.refs_0_, bf16[32,4096]{1,0:T(8,128)(2,1)S(1)} %get-tuple-element.33.refs_0_.refs_1_, bf16[32,4096]{1,0:T(8,128)(2,1)S(1)} %collective-permute-done.2.refs_1_.refs_2_, ...), custom_call_target="tpu_custom_call" | custom-call | tf_op jit(solution)/shard_map/place_first/pallas_call | solution.py:502
  55.7 8.7 %collective-permute-done.9.refs_5_ = bf16[32,2048]{1,0:T(8,128)(2,1)S(1)} collective-permute-done((bf16[32,2048]{1,0:T(8,128)(2,1)S(1)}, bf16[32,2048]{1,0:T(8,128)(2,1)S(1)}, u32[]{:S(2)}, u32[]{:S(2)}) %collective-permute-start.9) | collective-permute-done | bytes 131104 | tf_op jit(solution)/shard_map/ppermute | solution.py:330
  64.4 1.9 %collective-permute-done.10.refs_6_ = bf16[32,2048]{1,0:T(8,128)(2,1)S(1)} collective-permute-done((bf16[32,2048]{1,0:T(8,128)(2,1)S(1)}, bf16[32,2048]{1,0:T(8,128)(2,1)S(1)}, u32[]{:S(2)}, u32[]{:S(2)}) %collective-permute-start.10) | collective-permute-done | bytes 131104 | tf_op jit(solution)/shard_map/ppermute | solution.py:330
  66.3 1.0 %place_second.1 = bf16[128,4096]{1,0:T(8,128)(2,1)} custom-call(bf16[128,256]{1,0:T(8,128)(2,1)S(1)} %get-tuple-element.41.refs_0_, bf16[32,4096]{1,0:T(8,128)(2,1)S(1)} %get-tuple-element.33.refs_0_.refs_1_, bf16[32,4096]{1,0:T(8,128)(2,1)S(1)} %collective-permute-done.2.refs_1_.refs_2_, ...), custom_call_target="tpu_custom_call", output_to_operand_aliasing={{}: (9, {})} | custom-call | tf_op jit(solution)/shard_map/place_second/pallas_call | solution.py:512
Async XLA Ops:
  0.0 12.4 %copy-start = (bf16[128,4096]{1,0:T(8,128)(2,1)S(1)}, bf16[128,4096]{1,0:T(8,128)(2,1)}, u32[]{:S(2)}) copy-start(bf16[128,4096]{1,0:T(8,128)(2,1)} %wq_ref.5) | copy-start | bytes 3145732
  0.0 12.5 %copy-start.1 = (s32[16]{0:T(128)S(1)}, s32[16]{0:T(128)}, u32[]{:S(2)}) copy-start(s32[16]{0:T(128)} %lens_ref.1) | copy-start | bytes 196
  0.0 12.5 %copy-start.2 = (s32[32]{0:T(128)S(1)}, s32[32]{0:T(128)}, u32[]{:S(2)}) copy-start(s32[32]{0:T(128)} %dest_ref.1) | copy-start | bytes 388
  4.1 9.6 %collective-permute-start.1 = (bf16[144,512]{1,0:T(8,128)(2,1)S(1)}, bf16[144,512]{1,0:T(8,128)(2,1)S(1)}, u32[]{:S(2)}, u32[]{:S(2)}) collective-permute-start(bf16[144,512]{1,0:T(8,128)(2,1)S(1)} %get-tuple-element.28.own_ref), channel_id=1, source_target_pairs={{0,2},{1,3},{2,4},{3,5},{4,6},{5,7},{8,10},{9,11},{10,12},{11,13},... | collective-permute-start | bytes 442376 | tf_op jit(solution)/shard_map/ppermute | solution.py:415
  9.0 6.2 %collective-permute-start = (bf16[144,512]{1,0:T(8,128)(2,1)S(1)}, bf16[144,512]{1,0:T(8,128)(2,1)S(1)}, u32[]{:S(2)}, u32[]{:S(2)}) collective-permute-start(bf16[144,512]{1,0:T(8,128)(2,1)S(1)} %get-tuple-element.28.own_ref), channel_id=1, source_target_pairs={{0,1},{1,2},{2,3},{3,4},{4,5},{5,6},{6,7},{8,9},{9,10},{10,11},{11... | collective-permute-start | bytes 442376 | tf_op jit(solution)/shard_map/ppermute | solution.py:415
  17.2 13.8 %collective-permute-start.5 = (bf16[32,2048]{1,0:T(8,128)(2,1)S(1)}, bf16[32,2048]{1,0:T(8,128)(2,1)S(1)}, u32[]{:S(2)}, u32[]{:S(2)}) collective-permute-start(bf16[32,2048]{1,0:T(8,128)(2,1)S(1)} %get-tuple-element.37), channel_id=1, source_target_pairs={{0,4},{1,5},{2,6},{3,7},{4,0},{5,1},{6,2},{7,3},{8,12},{9,13},{10,... | collective-permute-start | bytes 393224 | tf_op jit(solution)/shard_map/ppermute | solution.py:330
  21.8 11.9 %collective-permute-start.6 = (bf16[32,2048]{1,0:T(8,128)(2,1)S(1)}, bf16[32,2048]{1,0:T(8,128)(2,1)S(1)}, u32[]{:S(2)}, u32[]{:S(2)}) collective-permute-start(bf16[32,2048]{1,0:T(8,128)(2,1)S(1)} %get-tuple-element.38), channel_id=1, source_target_pairs={{0,5},{1,4},{2,7},{3,6},{4,1},{5,0},{6,3},{7,2},{8,13},{9,12},{10,... | collective-permute-start | bytes 393224 | tf_op jit(solution)/shard_map/ppermute | solution.py:330
  24.7 12.4 %collective-permute-start.2 = (bf16[32,4096]{1,0:T(8,128)(2,1)S(1)}, bf16[32,4096]{1,0:T(8,128)(2,1)S(1)}, u32[]{:S(2)}, u32[]{:S(2)}) collective-permute-start(bf16[32,4096]{1,0:T(8,128)(2,1)S(1)} %get-tuple-element.34), channel_id=1, source_target_pairs={{0,1},{1,0},{2,3},{3,2},{4,5},{5,4},{6,7},{7,6},{8,9},{9,8},{10,11... | collective-permute-start | bytes 786440 | tf_op jit(solution)/shard_map/ppermute | solution.py:330
  25.9 13.6 %collective-permute-start.3 = (bf16[32,4096]{1,0:T(8,128)(2,1)S(1)}, bf16[32,4096]{1,0:T(8,128)(2,1)S(1)}, u32[]{:S(2)}, u32[]{:S(2)}) collective-permute-start(bf16[32,4096]{1,0:T(8,128)(2,1)S(1)} %get-tuple-element.35), channel_id=1, source_target_pairs={{0,2},{1,3},{2,0},{3,1},{4,6},{5,7},{6,4},{7,5},{8,10},{9,11},{10,... | collective-permute-start | bytes 786440 | tf_op jit(solution)/shard_map/ppermute | solution.py:330
  27.7 23.2 %collective-permute-start.4 = (bf16[32,4096]{1,0:T(8,128)(2,1)S(1)}, bf16[32,4096]{1,0:T(8,128)(2,1)S(1)}, u32[]{:S(2)}, u32[]{:S(2)}) collective-permute-start(bf16[32,4096]{1,0:T(8,128)(2,1)S(1)} %get-tuple-element.36), channel_id=1, source_target_pairs={{0,3},{1,2},{2,1},{3,0},{4,7},{5,6},{6,5},{7,4},{8,11},{9,10},{10,... | collective-permute-start | bytes 786440 | tf_op jit(solution)/shard_map/ppermute | solution.py:330
  31.1 20.0 %collective-permute-start.7 = (bf16[32,4096]{1,0:T(8,128)(2,1)S(1)}, bf16[32,4096]{1,0:T(8,128)(2,1)S(1)}, u32[]{:S(2)}, u32[]{:S(2)}) collective-permute-start(bf16[32,4096]{1,0:T(8,128)(2,1)S(1)} %get-tuple-element.39), channel_id=1, source_target_pairs={{0,6},{1,7},{2,4},{3,5},{4,2},{5,3},{6,0},{7,1},{8,14},{9,15},{10,... | collective-permute-start | bytes 786440 | tf_op jit(solution)/shard_map/ppermute | solution.py:330
  33.7 20.8 %collective-permute-start.8 = (bf16[32,4096]{1,0:T(8,128)(2,1)S(1)}, bf16[32,4096]{1,0:T(8,128)(2,1)S(1)}, u32[]{:S(2)}, u32[]{:S(2)}) collective-permute-start(bf16[32,4096]{1,0:T(8,128)(2,1)S(1)} %get-tuple-element.40), channel_id=1, source_target_pairs={{0,7},{1,6},{2,5},{3,4},{4,3},{5,2},{6,1},{7,0},{8,15},{9,14},{10,... | collective-permute-start | bytes 786440 | tf_op jit(solution)/shard_map/ppermute | solution.py:330
  37.1 27.3 %collective-permute-start.9 = (bf16[32,2048]{1,0:T(8,128)(2,1)S(1)}, bf16[32,2048]{1,0:T(8,128)(2,1)S(1)}, u32[]{:S(2)}, u32[]{:S(2)}) collective-permute-start(bf16[32,2048]{1,0:T(8,128)(2,1)S(1)} %get-tuple-element.42), channel_id=1, source_target_pairs={{0,4},{1,5},{2,6},{3,7},{4,0},{5,1},{6,2},{7,3},{8,12},{9,13},{10,... | collective-permute-start | bytes 393224 | tf_op jit(solution)/shard_map/ppermute | solution.py:330
  39.5 26.8 %collective-permute-start.10 = (bf16[32,2048]{1,0:T(8,128)(2,1)S(1)}, bf16[32,2048]{1,0:T(8,128)(2,1)S(1)}, u32[]{:S(2)}, u32[]{:S(2)}) collective-permute-start(bf16[32,2048]{1,0:T(8,128)(2,1)S(1)} %get-tuple-element.43), channel_id=1, source_target_pairs={{0,5},{1,4},{2,7},{3,6},{4,1},{5,0},{6,3},{7,2},{8,13},{9,12},{10,... | collective-permute-start | bytes 393224 | tf_op jit(solution)/shard_map/ppermute | solution.py:330

commit v7 on v6

--- a/solution.py
+++ b/solution.py
@@ -265,12 +265,12 @@
             layer_ref[:, cols] = (mixed[h * toks : (h + 1) * toks] + short).astype(BF16)
     middle = pick_ref.shape[0] // 2
     far = middle + middle // 2
-    put_blocks(pick_ref[middle:far, :], layer_ref[...], cross_refs)
+    put_blocks(pick_ref[far:, :], layer_ref[...], cross_refs)
     if half == 0:
         out_layer_ref[...] = layer_ref[...]
     else:
         layer = jnp.concatenate([past_ref[...], layer_ref[...]], axis=1)
-        put_blocks(pick_ref[far:, :], layer, far_refs)
+        put_blocks(pick_ref[middle:far, :], layer, far_refs)
         put_blocks(pick_ref[0:middle, :], layer, near_refs)
 
 
@@ -462,14 +462,14 @@
     cross = shapes(half_cross, rows, span)
     *first, layer = attend(0, cross + [pltpu.VMEM((toks, span), BF16)], len(cross), [])
     first = split(first, half_cross)
-    got_first = [swap(first[k], middle + k, n_seq) for k in range(half_cross)]
+    got_first = [swap(first[k], middle + half_cross + k, n_seq) for k in range(half_cross)]
     far, near = shapes(half_cross, rows, width), shapes(middle, rows, width)
     outs = attend(1, cross + far + near, len(cross), [layer])
     second, outs = split(outs[: len(cross)], half_cross), outs[len(cross) :]
     far, near = split(outs[: len(far)], half_cross), split(outs[len(far) :], middle)
-    got_far = [swap(far[k], middle + half_cross + k, n_seq) for k in range(half_cross)]
+    got_far = [swap(far[k], middle + k, n_seq) for k in range(half_cross)]
     got_near = [near[0]] + [swap(near[k], k, n_seq) for k in range(1, middle)]
-    got_second = [swap(second[k], middle + k, n_seq) for k in range(half_cross)]
+    got_second = [swap(second[k], middle + half_cross + k, n_seq) for k in range(half_cross)]
 
     def parts(found):
         if merged:
@@ -479,7 +479,7 @@
 
     near_parts = [[(a, 0, half * span) for a in got_near] for half in range(kvh)]
     cross_parts = [
-        [(a, 0, 0) for a in got] + [(a, 0, half * span) for a in got_far]
+        [(a, 0, half * span) for a in got_far] + [(a, 0, 0) for a in got]
         for half, got in enumerate((got_first, got_second))
     ]
     arrays, where = parts(near_parts[0])

time: 67.5 us -> 65.2 us (0.966)
  waiting for transfers between devices: 32.1 us -> 24.4 us
  starting transfers between devices: 23 us -> 28 us
    ppermute x9, waiting for transfers between devices: 30.5 us -> 22.9 us  [swap(): return lax.ppermute(array, 'seq', [(i, i ^ by) for i in range(size)])]
    ppermute x9, starting transfers between devices: 14.6 us -> 19.6 us  [swap(): return lax.ppermute(array, 'seq', [(i, i ^ by) for i in range(size)])]
  transfers between devices with their start and end apart: 11 -> 11, of which waited for: 8 -> 4; matrix products, arithmetic and copies ran while one was open for 0% -> 0% of each run, Pallas kernels for 8% -> 8%
where the time goes in v7:
time: 65.2 us; the launch traced here: 64.8 us
  starting transfers between devices  28 us (43%)
  waiting for transfers between devices  24.4 us (37%)
  Pallas kernels  12.2 us (19%)
    ppermute x9, waiting for transfers between devices, swap(): return lax.ppermute(array, 'seq', [(i, i ^ by) for i in range(size)])  22.9 us
    ppermute x9, starting transfers between devices, swap(): return lax.ppermute(array, 'seq', [(i, i ^ by) for i in range(size)])  19.6 us
    ppermute x2, starting transfers between devices, per_device(): lax.ppermute(held, 'seq', [(i, i + by) for i in range(n_seq - by)])  8.38 us
    pallas_call x2, Pallas kernels, attend(): pl.pallas_call(functools.partial(attend_kernel, half, BATCH[half], n_cros...  4.54 us
    pallas_call x1, Pallas kernels, per_device(): pl.pallas_call(project_kernel, out_shape=[pltpu.VMEM((held_rows, 2 * kv),...  4.04 us
    ppermute x2, waiting for transfers between devices, per_device(): lax.ppermute(held, 'seq', [(i, i + by) for i in range(n_seq - by)])  1.54 us
  transfers between devices with their start and end apart: 11, of which 4 were waited for; matrix products, arithmetic and copies ran while one was open for 0% of the time, Pallas kernels for 8%

profile of v7, /device:TPU:0, one launch (start us, length us, event | category | flops | bytes accessed | tf_op | source)
XLA Modules:
  0.0 64.8 jit_solution(12840001857626749678)
XLA Ops:
  0.0 0.0 copy-start
  0.0 0.0 copy-start.1
  0.0 0.0 copy-start.2
  0.0 4.0 %project.1 = (bf16[144,512]{1,0:T(8,128)(2,1)S(1)}, bf16[128,4096]{1,0:T(8,128)(2,1)S(1)}, bf16[128,128]{1,0:T(8,128)(2,1)S(1)}, f32[8,640]{1,0:T(8,128)S(1)}) custom-call(s32[16]{0:T(128)} %lens_ref.1, bf16[512,1024]{1,0:T(8,128)(2,1)} %x_hbm.1, f32[4,1024]{1,0:T(4,128)} %taps_hbm.1, f32[1,4096]{1,0:T(1,128)} %bitcast.1, bf16[4096,256]{1,0:T(8,128)(2,1)} %wk_hbm.1, ...), custom_call_target="tpu_custom_call" | custom-call | tf_op jit(solution)/shard_map/project/pallas_call | solution.py:379
  4.1 4.9 %collective-permute-start.1 = (bf16[144,512]{1,0:T(8,128)(2,1)S(1)}, bf16[144,512]{1,0:T(8,128)(2,1)S(1)}, u32[]{:S(2)}, u32[]{:S(2)}) collective-permute-start(bf16[144,512]{1,0:T(8,128)(2,1)S(1)} %get-tuple-element.28.own_ref), channel_id=1, source_target_pairs={{0,2},{1,3},{2,4},{3,5},{4,6},{5,7},{8,10},{9,11},{10,12},{11,13},... | collective-permute-start | bytes 442376 | tf_op jit(solution)/shard_map/ppermute | solution.py:415
  9.0 3.4 %collective-permute-start = (bf16[144,512]{1,0:T(8,128)(2,1)S(1)}, bf16[144,512]{1,0:T(8,128)(2,1)S(1)}, u32[]{:S(2)}, u32[]{:S(2)}) collective-permute-start(bf16[144,512]{1,0:T(8,128)(2,1)S(1)} %get-tuple-element.28.own_ref), channel_id=1, source_target_pairs={{0,1},{1,2},{2,3},{3,4},{4,5},{5,6},{6,7},{8,9},{9,10},{10,11},{11... | collective-permute-start | bytes 442376 | tf_op jit(solution)/shard_map/ppermute | solution.py:415
  12.4 0.0 copy-done
  12.5 0.0 copy-done.1
  12.5 0.0 copy-done.2
  12.5 1.2 %plan.1 = (f32[128,384]{1,0:T(8,128)S(1)}, bf16[256,128]{1,0:T(8,128)(2,1)S(1)}, bf16[128,4096]{1,0:T(8,128)(2,1)S(1)}) custom-call(s32[16]{0:T(128)S(1)} %copy-done.1, s32[32]{0:T(128)S(1)} %copy-done.2, bf16[128,128]{1,0:T(8,128)(2,1)S(1)} %get-tuple-element.25.lat_ref, bf16[128,4096]{1,0:T(8,128)(2,1)S(1)} %copy-done), custom_call_target="tpu_custom_call" | custom-call | tf_op jit(solution)/shard_map/plan/pallas_call | solution.py:419
  13.7 0.0 collective-permute-done.1.two_ref
  13.7 1.5 %collective-permute-done.one_ref = bf16[144,512]{1,0:T(8,128)(2,1)S(1)} collective-permute-done((bf16[144,512]{1,0:T(8,128)(2,1)S(1)}, bf16[144,512]{1,0:T(8,128)(2,1)S(1)}, u32[]{:S(2)}, u32[]{:S(2)}) %collective-permute-start) | collective-permute-done | bytes 147488 | tf_op jit(solution)/shard_map/ppermute | solution.py:415
  15.2 2.0 %attend_half_0.1 = (bf16[32,2048]{1,0:T(8,128)(2,1)S(1)}, bf16[32,2048]{1,0:T(8,128)(2,1)S(1)}, bf16[128,2048]{1,0:T(8,128)(2,1)S(1)}) custom-call(bf16[128,4096]{1,0:T(8,128)(2,1)S(1)} %get-tuple-element.26.query_ref, f32[8,640]{1,0:T(8,128)S(1)} %get-tuple-element.27.edge_ref, bf16[144,512]{1,0:T(8,128)(2,1)S(1)} %get-tuple-element.28.own_ref, ...), custom_call_target="tpu_custom_call" | custom-call | tf_op jit(solution)/shard_map/attend_half_0/pallas_call | solution.py:446
  17.2 5.5 %collective-permute-start.5 = (bf16[32,2048]{1,0:T(8,128)(2,1)S(1)}, bf16[32,2048]{1,0:T(8,128)(2,1)S(1)}, u32[]{:S(2)}, u32[]{:S(2)}) collective-permute-start(bf16[32,2048]{1,0:T(8,128)(2,1)S(1)} %get-tuple-element.37), channel_id=1, source_target_pairs={{0,6},{1,7},{2,4},{3,5},{4,2},{5,3},{6,0},{7,1},{8,14},{9,15},{10,... | collective-permute-start | bytes 393224 | tf_op jit(solution)/shard_map/ppermute | solution.py:330
  22.8 0.3 collective-permute-start.6
  23.0 2.5 %attend_half_1.1 = (bf16[32,2048]{1,0:T(8,128)(2,1)S(1)}, bf16[32,2048]{1,0:T(8,128)(2,1)S(1)}, bf16[32,4096]{1,0:T(8,128)(2,1)S(1)}, bf16[32,4096]{1,0:T(8,128)...) custom-call(bf16[128,4096]{1,0:T(8,128)(2,1)S(1)} %get-tuple-element, ...), custom_call_target="tpu_custom_call" | custom-call | tf_op jit(solution)/shard_map/attend_half_1/pallas_call | solution.py:446
  25.6 1.3 %collective-permute-start.2 = (bf16[32,4096]{1,0:T(8,128)(2,1)S(1)}, bf16[32,4096]{1,0:T(8,128)(2,1)S(1)}, u32[]{:S(2)}, u32[]{:S(2)}) collective-permute-start(bf16[32,4096]{1,0:T(8,128)(2,1)S(1)} %get-tuple-element.34), channel_id=1, source_target_pairs={{0,1},{1,0},{2,3},{3,2},{4,5},{5,4},{6,7},{7,6},{8,9},{9,8},{10,11... | collective-permute-start | bytes 786440 | tf_op jit(solution)/shard_map/ppermute | solution.py:330
  26.9 0.0 collective-permute-start.3
  26.9 2.2 %collective-permute-start.4 = (bf16[32,4096]{1,0:T(8,128)(2,1)S(1)}, bf16[32,4096]{1,0:T(8,128)(2,1)S(1)}, u32[]{:S(2)}, u32[]{:S(2)}) collective-permute-start(bf16[32,4096]{1,0:T(8,128)(2,1)S(1)} %get-tuple-element.36), channel_id=1, source_target_pairs={{0,3},{1,2},{2,1},{3,0},{4,7},{5,6},{6,5},{7,4},{8,11},{9,10},{10,... | collective-permute-start | bytes 786440 | tf_op jit(solution)/shard_map/ppermute | solution.py:330
  29.1 0.0 collective-permute-done.5.refs_4_.refs_7_
  29.1 3.8 %collective-permute-start.7 = (bf16[32,4096]{1,0:T(8,128)(2,1)S(1)}, bf16[32,4096]{1,0:T(8,128)(2,1)S(1)}, u32[]{:S(2)}, u32[]{:S(2)}) collective-permute-start(bf16[32,4096]{1,0:T(8,128)(2,1)S(1)} %get-tuple-element.39), channel_id=1, source_target_pairs={{0,4},{1,5},{2,6},{3,7},{4,0},{5,1},{6,2},{7,3},{8,12},{9,13},{10,... | collective-permute-start | bytes 786440 | tf_op jit(solution)/shard_map/ppermute | solution.py:330
  32.9 0.0 collective-permute-done.6.refs_5_.refs_8_
  32.9 3.8 %collective-permute-start.8 = (bf16[32,4096]{1,0:T(8,128)(2,1)S(1)}, bf16[32,4096]{1,0:T(8,128)(2,1)S(1)}, u32[]{:S(2)}, u32[]{:S(2)}) collective-permute-start(bf16[32,4096]{1,0:T(8,128)(2,1)S(1)} %get-tuple-element.40), channel_id=1, source_target_pairs={{0,5},{1,4},{2,7},{3,6},{4,1},{5,0},{6,3},{7,2},{8,13},{9,12},{10,... | collective-permute-start | bytes 786440 | tf_op jit(solution)/shard_map/ppermute | solution.py:330
  36.7 0.0 collective-permute-done.2.refs_1_.refs_2_
  36.7 1.2 %collective-permute-start.9 = (bf16[32,2048]{1,0:T(8,128)(2,1)S(1)}, bf16[32,2048]{1,0:T(8,128)(2,1)S(1)}, u32[]{:S(2)}, u32[]{:S(2)}) collective-permute-start(bf16[32,2048]{1,0:T(8,128)(2,1)S(1)} %get-tuple-element.42), channel_id=1, source_target_pairs={{0,6},{1,7},{2,4},{3,5},{4,2},{5,3},{6,0},{7,1},{8,14},{9,15},{10,... | collective-permute-start | bytes 393224 | tf_op jit(solution)/shard_map/ppermute | solution.py:330
  37.9 6.6 %collective-permute-done.3.refs_2_.refs_3_ = bf16[32,4096]{1,0:T(8,128)(2,1)S(1)} collective-permute-done((bf16[32,4096]{1,0:T(8,128)(2,1)S(1)}, bf16[32,4096]{1,0:T(8,128)(2,1)S(1)}, u32[]{:S(2)}, u32[]{:S(2)}) %collective-permute-start.3) | collective-permute-done | bytes 262176 | tf_op jit(solution)/shard_map/ppermute | solution.py:330
  44.5 1.6 %collective-permute-start.10 = (bf16[32,2048]{1,0:T(8,128)(2,1)S(1)}, bf16[32,2048]{1,0:T(8,128)(2,1)S(1)}, u32[]{:S(2)}, u32[]{:S(2)}) collective-permute-start(bf16[32,2048]{1,0:T(8,128)(2,1)S(1)} %get-tuple-element.43), channel_id=1, source_target_pairs={{0,7},{1,6},{2,5},{3,4},{4,3},{5,2},{6,1},{7,0},{8,15},{9,14},{10,... | collective-permute-start | bytes 393224 | tf_op jit(solution)/shard_map/ppermute | solution.py:330
  46.0 3.9 %collective-permute-done.4.refs_3_.refs_4_ = bf16[32,4096]{1,0:T(8,128)(2,1)S(1)} collective-permute-done((bf16[32,4096]{1,0:T(8,128)(2,1)S(1)}, bf16[32,4096]{1,0:T(8,128)(2,1)S(1)}, u32[]{:S(2)}, u32[]{:S(2)}) %collective-permute-start.4) | collective-permute-done | bytes 262176 | tf_op jit(solution)/shard_map/ppermute | solution.py:330
  50.0 0.1 count.1.refs_0_
  50.1 0.0 collective-permute-done.7.refs_5_
  50.1 12.4 %collective-permute-done.8.refs_6_ = bf16[32,4096]{1,0:T(8,128)(2,1)S(1)} collective-permute-done((bf16[32,4096]{1,0:T(8,128)(2,1)S(1)}, bf16[32,4096]{1,0:T(8,128)(2,1)S(1)}, u32[]{:S(2)}, u32[]{:S(2)}) %collective-permute-start.8) | collective-permute-done | bytes 262176 | tf_op jit(solution)/shard_map/ppermute | solution.py:330
  62.5 1.2 %place_first.1 = (bf16[128,4096]{1,0:T(8,128)(2,1)}, bf16[128,256]{1,0:T(8,128)(2,1)S(1)}) custom-call(f32[16,128]{1,0:T(8,128)S(1)} %count.1.refs_0_, bf16[32,4096]{1,0:T(8,128)(2,1)S(1)} %get-tuple-element.33.refs_0_.refs_1_, bf16[32,4096]{1,0:T(8,128)(2,1)S(1)} %collective-permute-done.2.refs_1_.refs_2_, ...), custom_call_target="tpu_custom_call" | custom-call | tf_op jit(solution)/shard_map/place_first/pallas_call | solution.py:502
  63.7 0.0 collective-permute-done.9.refs_7_
  63.7 0.0 collective-permute-done.10.refs_8_
  63.7 1.0 %place_second.1 = bf16[128,4096]{1,0:T(8,128)(2,1)} custom-call(bf16[128,256]{1,0:T(8,128)(2,1)S(1)} %get-tuple-element.41.refs_0_, bf16[32,4096]{1,0:T(8,128)(2,1)S(1)} %get-tuple-element.33.refs_0_.refs_1_, bf16[32,4096]{1,0:T(8,128)(2,1)S(1)} %collective-permute-done.2.refs_1_.refs_2_, ...), custom_call_target="tpu_custom_call", output_to_operand_aliasing={{}: (9, {})} | custom-call | tf_op jit(solution)/shard_map/place_second/pallas_call | solution.py:512
Async XLA Ops:
  0.0 12.4 %copy-start = (bf16[128,4096]{1,0:T(8,128)(2,1)S(1)}, bf16[128,4096]{1,0:T(8,128)(2,1)}, u32[]{:S(2)}) copy-start(bf16[128,4096]{1,0:T(8,128)(2,1)} %wq_ref.5) | copy-start | bytes 3145732
  0.0 12.5 %copy-start.1 = (s32[16]{0:T(128)S(1)}, s32[16]{0:T(128)}, u32[]{:S(2)}) copy-start(s32[16]{0:T(128)} %lens_ref.1) | copy-start | bytes 196
  0.0 12.5 %copy-start.2 = (s32[32]{0:T(128)S(1)}, s32[32]{0:T(128)}, u32[]{:S(2)}) copy-start(s32[32]{0:T(128)} %dest_ref.1) | copy-start | bytes 388
  4.1 9.6 %collective-permute-start.1 = (bf16[144,512]{1,0:T(8,128)(2,1)S(1)}, bf16[144,512]{1,0:T(8,128)(2,1)S(1)}, u32[]{:S(2)}, u32[]{:S(2)}) collective-permute-start(bf16[144,512]{1,0:T(8,128)(2,1)S(1)} %get-tuple-element.28.own_ref), channel_id=1, source_target_pairs={{0,2},{1,3},{2,4},{3,5},{4,6},{5,7},{8,10},{9,11},{10,12},{11,13},... | collective-permute-start | bytes 442376 | tf_op jit(solution)/shard_map/ppermute | solution.py:415
  9.0 6.2 %collective-permute-start = (bf16[144,512]{1,0:T(8,128)(2,1)S(1)}, bf16[144,512]{1,0:T(8,128)(2,1)S(1)}, u32[]{:S(2)}, u32[]{:S(2)}) collective-permute-start(bf16[144,512]{1,0:T(8,128)(2,1)S(1)} %get-tuple-element.28.own_ref), channel_id=1, source_target_pairs={{0,1},{1,2},{2,3},{3,4},{4,5},{5,6},{6,7},{8,9},{9,10},{10,11},{11... | collective-permute-start | bytes 442376 | tf_op jit(solution)/shard_map/ppermute | solution.py:415
  17.2 11.9 %collective-permute-start.5 = (bf16[32,2048]{1,0:T(8,128)(2,1)S(1)}, bf16[32,2048]{1,0:T(8,128)(2,1)S(1)}, u32[]{:S(2)}, u32[]{:S(2)}) collective-permute-start(bf16[32,2048]{1,0:T(8,128)(2,1)S(1)} %get-tuple-element.37), channel_id=1, source_target_pairs={{0,6},{1,7},{2,4},{3,5},{4,2},{5,3},{6,0},{7,1},{8,14},{9,15},{10,... | collective-permute-start | bytes 393224 | tf_op jit(solution)/shard_map/ppermute | solution.py:330
  22.8 10.1 %collective-permute-start.6 = (bf16[32,2048]{1,0:T(8,128)(2,1)S(1)}, bf16[32,2048]{1,0:T(8,128)(2,1)S(1)}, u32[]{:S(2)}, u32[]{:S(2)}) collective-permute-start(bf16[32,2048]{1,0:T(8,128)(2,1)S(1)} %get-tuple-element.38), channel_id=1, source_target_pairs={{0,7},{1,6},{2,5},{3,4},{4,3},{5,2},{6,1},{7,0},{8,15},{9,14},{10,... | collective-permute-start | bytes 393224 | tf_op jit(solution)/shard_map/ppermute | solution.py:330
  25.6 11.1 %collective-permute-start.2 = (bf16[32,4096]{1,0:T(8,128)(2,1)S(1)}, bf16[32,4096]{1,0:T(8,128)(2,1)S(1)}, u32[]{:S(2)}, u32[]{:S(2)}) collective-permute-start(bf16[32,4096]{1,0:T(8,128)(2,1)S(1)} %get-tuple-element.34), channel_id=1, source_target_pairs={{0,1},{1,0},{2,3},{3,2},{4,5},{5,4},{6,7},{7,6},{8,9},{9,8},{10,11... | collective-permute-start | bytes 786440 | tf_op jit(solution)/shard_map/ppermute | solution.py:330
  26.9 17.5 %collective-permute-start.3 = (bf16[32,4096]{1,0:T(8,128)(2,1)S(1)}, bf16[32,4096]{1,0:T(8,128)(2,1)S(1)}, u32[]{:S(2)}, u32[]{:S(2)}) collective-permute-start(bf16[32,4096]{1,0:T(8,128)(2,1)S(1)} %get-tuple-element.35), channel_id=1, source_target_pairs={{0,2},{1,3},{2,0},{3,1},{4,6},{5,7},{6,4},{7,5},{8,10},{9,11},{10,... | collective-permute-start | bytes 786440 | tf_op jit(solution)/shard_map/ppermute | solution.py:330
  26.9 23.0 %collective-permute-start.4 = (bf16[32,4096]{1,0:T(8,128)(2,1)S(1)}, bf16[32,4096]{1,0:T(8,128)(2,1)S(1)}, u32[]{:S(2)}, u32[]{:S(2)}) collective-permute-start(bf16[32,4096]{1,0:T(8,128)(2,1)S(1)} %get-tuple-element.36), channel_id=1, source_target_pairs={{0,3},{1,2},{2,1},{3,0},{4,7},{5,6},{6,5},{7,4},{8,11},{9,10},{10,... | collective-permute-start | bytes 786440 | tf_op jit(solution)/shard_map/ppermute | solution.py:330
  29.1 21.0 %collective-permute-start.7 = (bf16[32,4096]{1,0:T(8,128)(2,1)S(1)}, bf16[32,4096]{1,0:T(8,128)(2,1)S(1)}, u32[]{:S(2)}, u32[]{:S(2)}) collective-permute-start(bf16[32,4096]{1,0:T(8,128)(2,1)S(1)} %get-tuple-element.39), channel_id=1, source_target_pairs={{0,4},{1,5},{2,6},{3,7},{4,0},{5,1},{6,2},{7,3},{8,12},{9,13},{10,... | collective-permute-start | bytes 786440 | tf_op jit(solution)/shard_map/ppermute | solution.py:330
  32.9 29.6 %collective-permute-start.8 = (bf16[32,4096]{1,0:T(8,128)(2,1)S(1)}, bf16[32,4096]{1,0:T(8,128)(2,1)S(1)}, u32[]{:S(2)}, u32[]{:S(2)}) collective-permute-start(bf16[32,4096]{1,0:T(8,128)(2,1)S(1)} %get-tuple-element.40), channel_id=1, source_target_pairs={{0,5},{1,4},{2,7},{3,6},{4,1},{5,0},{6,3},{7,2},{8,13},{9,12},{10,... | collective-permute-start | bytes 786440 | tf_op jit(solution)/shard_map/ppermute | solution.py:330
  36.7 27.0 %collective-permute-start.9 = (bf16[32,2048]{1,0:T(8,128)(2,1)S(1)}, bf16[32,2048]{1,0:T(8,128)(2,1)S(1)}, u32[]{:S(2)}, u32[]{:S(2)}) collective-permute-start(bf16[32,2048]{1,0:T(8,128)(2,1)S(1)} %get-tuple-element.42), channel_id=1, source_target_pairs={{0,6},{1,7},{2,4},{3,5},{4,2},{5,3},{6,0},{7,1},{8,14},{9,15},{10,... | collective-permute-start | bytes 393224 | tf_op jit(solution)/shard_map/ppermute | solution.py:330
  44.5 19.2 %collective-permute-start.10 = (bf16[32,2048]{1,0:T(8,128)(2,1)S(1)}, bf16[32,2048]{1,0:T(8,128)(2,1)S(1)}, u32[]{:S(2)}, u32[]{:S(2)}) collective-permute-start(bf16[32,2048]{1,0:T(8,128)(2,1)S(1)} %get-tuple-element.43), channel_id=1, source_target_pairs={{0,7},{1,6},{2,5},{3,4},{4,3},{5,2},{6,1},{7,0},{8,15},{9,14},{10,... | collective-permute-start | bytes 393224 | tf_op jit(solution)/shard_map/ppermute | solution.py:330

commit v8 on v7

--- a/solution.py
+++ b/solution.py
@@ -193,7 +193,7 @@
         ref[...] = placed[k * rows : (k + 1) * rows]
 
 
-def attend_kernel(half, batch, n_cross, query_ref, edge_ref, own_ref, one_ref, two_ref, limit_ref, pick_ref, wq_ref, short_ref, *refs):
+def attend_kernel(half, batch, n_cross, query_ref, edge_ref, own_ref, two_ref, one_ref, limit_ref, pick_ref, wq_ref, short_ref, *refs):
     refs, (k_ref, v_ref, corr_ref, layer_ref) = refs[:-4], refs[-4:]
     if half == 0:
         cross_refs, out_layer_ref = refs[:-1], refs[-1]
@@ -442,7 +442,7 @@
         return [arrays[0][i * height : (i + 1) * height] for i in range(count)]
 
     def attend(half, outs, n_cross, more):
-        operands = [query, edge, held, *behind, limit, pick, w_qup, short, *more]
+        operands = [query, edge, held, *behind[::-1], limit, pick, w_qup, short, *more]
         return pl.pallas_call(
             functools.partial(attend_kernel, half, BATCH[half], n_cross),
             out_shape=outs,

time: 65.2 us -> 65.2 us (level)
  no operation moved by 1% of the time
where the time goes in v8:
time: 65.2 us; the launch traced here: 65 us
  starting transfers between devices  28.4 us (44%)
  waiting for transfers between devices  24.4 us (37%)
  Pallas kernels  12.2 us (19%)
    ppermute x9, waiting for transfers between devices, swap(): return lax.ppermute(array, 'seq', [(i, i ^ by) for i in range(size)])  22.8 us
    ppermute x9, starting transfers between devices, swap(): return lax.ppermute(array, 'seq', [(i, i ^ by) for i in range(size)])  20 us
    ppermute x2, starting transfers between devices, per_device(): lax.ppermute(held, 'seq', [(i, i + by) for i in range(n_seq - by)])  8.37 us
    pallas_call x2, Pallas kernels, attend(): pl.pallas_call(functools.partial(attend_kernel, half, BATCH[half], n_cros...  4.52 us
    pallas_call x1, Pallas kernels, per_device(): pl.pallas_call(project_kernel, out_shape=[pltpu.VMEM((held_rows, 2 * kv),...  4.04 us
    ppermute x2, waiting for transfers between devices, per_device(): lax.ppermute(held, 'seq', [(i, i + by) for i in range(n_seq - by)])  1.54 us
  transfers between devices with their start and end apart: 11, of which 4 were waited for; matrix products, arithmetic and copies ran while one was open for 0% of the time, Pallas kernels for 8%

profile of v8, /device:TPU:0, one launch (start us, length us, event | category | flops | bytes accessed | tf_op | source)
XLA Modules:
  0.0 65.0 jit_solution(8731180541180372386)
XLA Ops:
  0.0 0.0 copy-start
  0.0 0.0 copy-start.1
  0.0 0.0 copy-start.2
  0.0 4.0 %project.1 = (bf16[144,512]{1,0:T(8,128)(2,1)S(1)}, bf16[128,4096]{1,0:T(8,128)(2,1)S(1)}, bf16[128,128]{1,0:T(8,128)(2,1)S(1)}, f32[8,640]{1,0:T(8,128)S(1)}) custom-call(s32[16]{0:T(128)} %lens_ref.1, bf16[512,1024]{1,0:T(8,128)(2,1)} %x_hbm.1, f32[4,1024]{1,0:T(4,128)} %taps_hbm.1, f32[1,4096]{1,0:T(1,128)} %bitcast.1, bf16[4096,256]{1,0:T(8,128)(2,1)} %wk_hbm.1, ...), custom_call_target="tpu_custom_call" | custom-call | tf_op jit(solution)/shard_map/project/pallas_call | solution.py:379
  4.1 4.9 %collective-permute-start.1 = (bf16[144,512]{1,0:T(8,128)(2,1)S(1)}, bf16[144,512]{1,0:T(8,128)(2,1)S(1)}, u32[]{:S(2)}, u32[]{:S(2)}) collective-permute-start(bf16[144,512]{1,0:T(8,128)(2,1)S(1)} %get-tuple-element.28.own_ref), channel_id=1, source_target_pairs={{0,1},{1,2},{2,3},{3,4},{4,5},{5,6},{6,7},{8,9},{9,10},{10,11},{11... | collective-permute-start | bytes 442376 | tf_op jit(solution)/shard_map/ppermute | solution.py:415
  8.9 3.5 %collective-permute-start = (bf16[144,512]{1,0:T(8,128)(2,1)S(1)}, bf16[144,512]{1,0:T(8,128)(2,1)S(1)}, u32[]{:S(2)}, u32[]{:S(2)}) collective-permute-start(bf16[144,512]{1,0:T(8,128)(2,1)S(1)} %get-tuple-element.28.own_ref), channel_id=1, source_target_pairs={{0,2},{1,3},{2,4},{3,5},{4,6},{5,7},{8,10},{9,11},{10,12},{11,13},... | collective-permute-start | bytes 442376 | tf_op jit(solution)/shard_map/ppermute | solution.py:415
  12.4 0.0 copy-done
  12.5 0.0 copy-done.1
  12.5 0.0 copy-done.2
  12.5 1.2 %plan.1 = (f32[128,384]{1,0:T(8,128)S(1)}, bf16[256,128]{1,0:T(8,128)(2,1)S(1)}, bf16[128,4096]{1,0:T(8,128)(2,1)S(1)}) custom-call(s32[16]{0:T(128)S(1)} %copy-done.1, s32[32]{0:T(128)S(1)} %copy-done.2, bf16[128,128]{1,0:T(8,128)(2,1)S(1)} %get-tuple-element.25.lat_ref, bf16[128,4096]{1,0:T(8,128)(2,1)S(1)} %copy-done), custom_call_target="tpu_custom_call" | custom-call | tf_op jit(solution)/shard_map/plan/pallas_call | solution.py:419
  13.7 0.0 collective-permute-done.1.one_ref
  13.7 1.5 %collective-permute-done.two_ref = bf16[144,512]{1,0:T(8,128)(2,1)S(1)} collective-permute-done((bf16[144,512]{1,0:T(8,128)(2,1)S(1)}, bf16[144,512]{1,0:T(8,128)(2,1)S(1)}, u32[]{:S(2)}, u32[]{:S(2)}) %collective-permute-start) | collective-permute-done | bytes 147488 | tf_op jit(solution)/shard_map/ppermute | solution.py:415
  15.2 2.0 %attend_half_0.1 = (bf16[32,2048]{1,0:T(8,128)(2,1)S(1)}, bf16[32,2048]{1,0:T(8,128)(2,1)S(1)}, bf16[128,2048]{1,0:T(8,128)(2,1)S(1)}) custom-call(bf16[128,4096]{1,0:T(8,128)(2,1)S(1)} %get-tuple-element.26.query_ref, f32[8,640]{1,0:T(8,128)S(1)} %get-tuple-element.27.edge_ref, bf16[144,512]{1,0:T(8,128)(2,1)S(1)} %get-tuple-element.28.own_ref, ...), custom_call_target="tpu_custom_call" | custom-call | tf_op jit(solution)/shard_map/attend_half_0/pallas_call | solution.py:446
  17.2 4.6 %collective-permute-start.5 = (bf16[32,2048]{1,0:T(8,128)(2,1)S(1)}, bf16[32,2048]{1,0:T(8,128)(2,1)S(1)}, u32[]{:S(2)}, u32[]{:S(2)}) collective-permute-start(bf16[32,2048]{1,0:T(8,128)(2,1)S(1)} %get-tuple-element.37), channel_id=1, source_target_pairs={{0,6},{1,7},{2,4},{3,5},{4,2},{5,3},{6,0},{7,1},{8,14},{9,15},{10,... | collective-permute-start | bytes 393224 | tf_op jit(solution)/shard_map/ppermute | solution.py:330
  21.8 1.0 %collective-permute-start.6 = (bf16[32,2048]{1,0:T(8,128)(2,1)S(1)}, bf16[32,2048]{1,0:T(8,128)(2,1)S(1)}, u32[]{:S(2)}, u32[]{:S(2)}) collective-permute-start(bf16[32,2048]{1,0:T(8,128)(2,1)S(1)} %get-tuple-element.38), channel_id=1, source_target_pairs={{0,7},{1,6},{2,5},{3,4},{4,3},{5,2},{6,1},{7,0},{8,15},{9,14},{10,... | collective-permute-start | bytes 393224 | tf_op jit(solution)/shard_map/ppermute | solution.py:330
  22.8 2.5 %attend_half_1.1 = (bf16[32,2048]{1,0:T(8,128)(2,1)S(1)}, bf16[32,2048]{1,0:T(8,128)(2,1)S(1)}, bf16[32,4096]{1,0:T(8,128)(2,1)S(1)}, bf16[32,4096]{1,0:T(8,128)...) custom-call(bf16[128,4096]{1,0:T(8,128)(2,1)S(1)} %get-tuple-element, ...), custom_call_target="tpu_custom_call" | custom-call | tf_op jit(solution)/shard_map/attend_half_1/pallas_call | solution.py:446
  25.3 0.6 collective-permute-start.2
  26.0 0.0 collective-permute-start.3
  26.0 2.9 %collective-permute-start.4 = (bf16[32,4096]{1,0:T(8,128)(2,1)S(1)}, bf16[32,4096]{1,0:T(8,128)(2,1)S(1)}, u32[]{:S(2)}, u32[]{:S(2)}) collective-permute-start(bf16[32,4096]{1,0:T(8,128)(2,1)S(1)} %get-tuple-element.36), channel_id=1, source_target_pairs={{0,3},{1,2},{2,1},{3,0},{4,7},{5,6},{6,5},{7,4},{8,11},{9,10},{10,... | collective-permute-start | bytes 786440 | tf_op jit(solution)/shard_map/ppermute | solution.py:330
  28.9 0.0 collective-permute-done.5.refs_4_.refs_7_
  28.9 3.0 %collective-permute-start.7 = (bf16[32,4096]{1,0:T(8,128)(2,1)S(1)}, bf16[32,4096]{1,0:T(8,128)(2,1)S(1)}, u32[]{:S(2)}, u32[]{:S(2)}) collective-permute-start(bf16[32,4096]{1,0:T(8,128)(2,1)S(1)} %get-tuple-element.39), channel_id=1, source_target_pairs={{0,4},{1,5},{2,6},{3,7},{4,0},{5,1},{6,2},{7,3},{8,12},{9,13},{10,... | collective-permute-start | bytes 786440 | tf_op jit(solution)/shard_map/ppermute | solution.py:330
  31.9 0.0 collective-permute-done.6.refs_5_.refs_8_
  31.9 2.7 %collective-permute-start.8 = (bf16[32,4096]{1,0:T(8,128)(2,1)S(1)}, bf16[32,4096]{1,0:T(8,128)(2,1)S(1)}, u32[]{:S(2)}, u32[]{:S(2)}) collective-permute-start(bf16[32,4096]{1,0:T(8,128)(2,1)S(1)} %get-tuple-element.40), channel_id=1, source_target_pairs={{0,5},{1,4},{2,7},{3,6},{4,1},{5,0},{6,3},{7,2},{8,13},{9,12},{10,... | collective-permute-start | bytes 786440 | tf_op jit(solution)/shard_map/ppermute | solution.py:330
  34.6 0.0 collective-permute-done.2.refs_1_.refs_2_
  34.6 2.6 %collective-permute-start.9 = (bf16[32,2048]{1,0:T(8,128)(2,1)S(1)}, bf16[32,2048]{1,0:T(8,128)(2,1)S(1)}, u32[]{:S(2)}, u32[]{:S(2)}) collective-permute-start(bf16[32,2048]{1,0:T(8,128)(2,1)S(1)} %get-tuple-element.42), channel_id=1, source_target_pairs={{0,6},{1,7},{2,4},{3,5},{4,2},{5,3},{6,0},{7,1},{8,14},{9,15},{10,... | collective-permute-start | bytes 393224 | tf_op jit(solution)/shard_map/ppermute | solution.py:330
  37.2 7.7 %collective-permute-done.3.refs_2_.refs_3_ = bf16[32,4096]{1,0:T(8,128)(2,1)S(1)} collective-permute-done((bf16[32,4096]{1,0:T(8,128)(2,1)S(1)}, bf16[32,4096]{1,0:T(8,128)(2,1)S(1)}, u32[]{:S(2)}, u32[]{:S(2)}) %collective-permute-start.3) | collective-permute-done | bytes 262176 | tf_op jit(solution)/shard_map/ppermute | solution.py:330
  44.9 2.6 %collective-permute-start.10 = (bf16[32,2048]{1,0:T(8,128)(2,1)S(1)}, bf16[32,2048]{1,0:T(8,128)(2,1)S(1)}, u32[]{:S(2)}, u32[]{:S(2)}) collective-permute-start(bf16[32,2048]{1,0:T(8,128)(2,1)S(1)} %get-tuple-element.43), channel_id=1, source_target_pairs={{0,7},{1,6},{2,5},{3,4},{4,3},{5,2},{6,1},{7,0},{8,15},{9,14},{10,... | collective-permute-start | bytes 393224 | tf_op jit(solution)/shard_map/ppermute | solution.py:330
  47.5 1.3 %collective-permute-done.4.refs_3_.refs_4_ = bf16[32,4096]{1,0:T(8,128)(2,1)S(1)} collective-permute-done((bf16[32,4096]{1,0:T(8,128)(2,1)S(1)}, bf16[32,4096]{1,0:T(8,128)(2,1)S(1)}, u32[]{:S(2)}, u32[]{:S(2)}) %collective-permute-start.4) | collective-permute-done | bytes 262176 | tf_op jit(solution)/shard_map/ppermute | solution.py:330
  48.7 0.1 count.1.refs_0_
  48.9 0.0 collective-permute-done.7.refs_5_
  48.9 13.8 %collective-permute-done.8.refs_6_ = bf16[32,4096]{1,0:T(8,128)(2,1)S(1)} collective-permute-done((bf16[32,4096]{1,0:T(8,128)(2,1)S(1)}, bf16[32,4096]{1,0:T(8,128)(2,1)S(1)}, u32[]{:S(2)}, u32[]{:S(2)}) %collective-permute-start.8) | collective-permute-done | bytes 262176 | tf_op jit(solution)/shard_map/ppermute | solution.py:330
  62.7 1.2 %place_first.1 = (bf16[128,4096]{1,0:T(8,128)(2,1)}, bf16[128,256]{1,0:T(8,128)(2,1)S(1)}) custom-call(f32[16,128]{1,0:T(8,128)S(1)} %count.1.refs_0_, bf16[32,4096]{1,0:T(8,128)(2,1)S(1)} %get-tuple-element.33.refs_0_.refs_1_, bf16[32,4096]{1,0:T(8,128)(2,1)S(1)} %collective-permute-done.2.refs_1_.refs_2_, ...), custom_call_target="tpu_custom_call" | custom-call | tf_op jit(solution)/shard_map/place_first/pallas_call | solution.py:502
  64.0 0.0 collective-permute-done.9.refs_7_
  64.0 0.0 collective-permute-done.10.refs_8_
  64.0 1.0 %place_second.1 = bf16[128,4096]{1,0:T(8,128)(2,1)} custom-call(bf16[128,256]{1,0:T(8,128)(2,1)S(1)} %get-tuple-element.41.refs_0_, bf16[32,4096]{1,0:T(8,128)(2,1)S(1)} %get-tuple-element.33.refs_0_.refs_1_, bf16[32,4096]{1,0:T(8,128)(2,1)S(1)} %collective-permute-done.2.refs_1_.refs_2_, ...), custom_call_target="tpu_custom_call", output_to_operand_aliasing={{}: (9, {})} | custom-call | tf_op jit(solution)/shard_map/place_second/pallas_call | solution.py:512
Async XLA Ops:
  0.0 12.4 %copy-start = (bf16[128,4096]{1,0:T(8,128)(2,1)S(1)}, bf16[128,4096]{1,0:T(8,128)(2,1)}, u32[]{:S(2)}) copy-start(bf16[128,4096]{1,0:T(8,128)(2,1)} %wq_ref.5) | copy-start | bytes 3145732
  0.0 12.5 %copy-start.1 = (s32[16]{0:T(128)S(1)}, s32[16]{0:T(128)}, u32[]{:S(2)}) copy-start(s32[16]{0:T(128)} %lens_ref.1) | copy-start | bytes 196
  0.0 12.5 %copy-start.2 = (s32[32]{0:T(128)S(1)}, s32[32]{0:T(128)}, u32[]{:S(2)}) copy-start(s32[32]{0:T(128)} %dest_ref.1) | copy-start | bytes 388
  4.1 9.6 %collective-permute-start.1 = (bf16[144,512]{1,0:T(8,128)(2,1)S(1)}, bf16[144,512]{1,0:T(8,128)(2,1)S(1)}, u32[]{:S(2)}, u32[]{:S(2)}) collective-permute-start(bf16[144,512]{1,0:T(8,128)(2,1)S(1)} %get-tuple-element.28.own_ref), channel_id=1, source_target_pairs={{0,1},{1,2},{2,3},{3,4},{4,5},{5,6},{6,7},{8,9},{9,10},{10,11},{11... | collective-permute-start | bytes 442376 | tf_op jit(solution)/shard_map/ppermute | solution.py:415
  8.9 6.3 %collective-permute-start = (bf16[144,512]{1,0:T(8,128)(2,1)S(1)}, bf16[144,512]{1,0:T(8,128)(2,1)S(1)}, u32[]{:S(2)}, u32[]{:S(2)}) collective-permute-start(bf16[144,512]{1,0:T(8,128)(2,1)S(1)} %get-tuple-element.28.own_ref), channel_id=1, source_target_pairs={{0,2},{1,3},{2,4},{3,5},{4,6},{5,7},{8,10},{9,11},{10,12},{11,13},... | collective-permute-start | bytes 442376 | tf_op jit(solution)/shard_map/ppermute | solution.py:415
  17.2 11.7 %collective-permute-start.5 = (bf16[32,2048]{1,0:T(8,128)(2,1)S(1)}, bf16[32,2048]{1,0:T(8,128)(2,1)S(1)}, u32[]{:S(2)}, u32[]{:S(2)}) collective-permute-start(bf16[32,2048]{1,0:T(8,128)(2,1)S(1)} %get-tuple-element.37), channel_id=1, source_target_pairs={{0,6},{1,7},{2,4},{3,5},{4,2},{5,3},{6,0},{7,1},{8,14},{9,15},{10,... | collective-permute-start | bytes 393224 | tf_op jit(solution)/shard_map/ppermute | solution.py:330
  21.8 10.0 %collective-permute-start.6 = (bf16[32,2048]{1,0:T(8,128)(2,1)S(1)}, bf16[32,2048]{1,0:T(8,128)(2,1)S(1)}, u32[]{:S(2)}, u32[]{:S(2)}) collective-permute-start(bf16[32,2048]{1,0:T(8,128)(2,1)S(1)} %get-tuple-element.38), channel_id=1, source_target_pairs={{0,7},{1,6},{2,5},{3,4},{4,3},{5,2},{6,1},{7,0},{8,15},{9,14},{10,... | collective-permute-start | bytes 393224 | tf_op jit(solution)/shard_map/ppermute | solution.py:330
  25.3 9.3 %collective-permute-start.2 = (bf16[32,4096]{1,0:T(8,128)(2,1)S(1)}, bf16[32,4096]{1,0:T(8,128)(2,1)S(1)}, u32[]{:S(2)}, u32[]{:S(2)}) collective-permute-start(bf16[32,4096]{1,0:T(8,128)(2,1)S(1)} %get-tuple-element.34), channel_id=1, source_target_pairs={{0,1},{1,0},{2,3},{3,2},{4,5},{5,4},{6,7},{7,6},{8,9},{9,8},{10,11... | collective-permute-start | bytes 786440 | tf_op jit(solution)/shard_map/ppermute | solution.py:330
  26.0 18.9 %collective-permute-start.3 = (bf16[32,4096]{1,0:T(8,128)(2,1)S(1)}, bf16[32,4096]{1,0:T(8,128)(2,1)S(1)}, u32[]{:S(2)}, u32[]{:S(2)}) collective-permute-start(bf16[32,4096]{1,0:T(8,128)(2,1)S(1)} %get-tuple-element.35), channel_id=1, source_target_pairs={{0,2},{1,3},{2,0},{3,1},{4,6},{5,7},{6,4},{7,5},{8,10},{9,11},{10,... | collective-permute-start | bytes 786440 | tf_op jit(solution)/shard_map/ppermute | solution.py:330
  26.0 22.8 %collective-permute-start.4 = (bf16[32,4096]{1,0:T(8,128)(2,1)S(1)}, bf16[32,4096]{1,0:T(8,128)(2,1)S(1)}, u32[]{:S(2)}, u32[]{:S(2)}) collective-permute-start(bf16[32,4096]{1,0:T(8,128)(2,1)S(1)} %get-tuple-element.36), channel_id=1, source_target_pairs={{0,3},{1,2},{2,1},{3,0},{4,7},{5,6},{6,5},{7,4},{8,11},{9,10},{10,... | collective-permute-start | bytes 786440 | tf_op jit(solution)/shard_map/ppermute | solution.py:330
  28.9 20.0 %collective-permute-start.7 = (bf16[32,4096]{1,0:T(8,128)(2,1)S(1)}, bf16[32,4096]{1,0:T(8,128)(2,1)S(1)}, u32[]{:S(2)}, u32[]{:S(2)}) collective-permute-start(bf16[32,4096]{1,0:T(8,128)(2,1)S(1)} %get-tuple-element.39), channel_id=1, source_target_pairs={{0,4},{1,5},{2,6},{3,7},{4,0},{5,1},{6,2},{7,3},{8,12},{9,13},{10,... | collective-permute-start | bytes 786440 | tf_op jit(solution)/shard_map/ppermute | solution.py:330
  31.9 30.9 %collective-permute-start.8 = (bf16[32,4096]{1,0:T(8,128)(2,1)S(1)}, bf16[32,4096]{1,0:T(8,128)(2,1)S(1)}, u32[]{:S(2)}, u32[]{:S(2)}) collective-permute-start(bf16[32,4096]{1,0:T(8,128)(2,1)S(1)} %get-tuple-element.40), channel_id=1, source_target_pairs={{0,5},{1,4},{2,7},{3,6},{4,1},{5,0},{6,3},{7,2},{8,13},{9,12},{10,... | collective-permute-start | bytes 786440 | tf_op jit(solution)/shard_map/ppermute | solution.py:330
  34.6 29.4 %collective-permute-start.9 = (bf16[32,2048]{1,0:T(8,128)(2,1)S(1)}, bf16[32,2048]{1,0:T(8,128)(2,1)S(1)}, u32[]{:S(2)}, u32[]{:S(2)}) collective-permute-start(bf16[32,2048]{1,0:T(8,128)(2,1)S(1)} %get-tuple-element.42), channel_id=1, source_target_pairs={{0,6},{1,7},{2,4},{3,5},{4,2},{5,3},{6,0},{7,1},{8,14},{9,15},{10,... | collective-permute-start | bytes 393224 | tf_op jit(solution)/shard_map/ppermute | solution.py:330
  44.9 19.1 %collective-permute-start.10 = (bf16[32,2048]{1,0:T(8,128)(2,1)S(1)}, bf16[32,2048]{1,0:T(8,128)(2,1)S(1)}, u32[]{:S(2)}, u32[]{:S(2)}) collective-permute-start(bf16[32,2048]{1,0:T(8,128)(2,1)S(1)} %get-tuple-element.43), channel_id=1, source_target_pairs={{0,7},{1,6},{2,5},{3,4},{4,3},{5,2},{6,1},{7,0},{8,15},{9,14},{10,... | collective-permute-start | bytes 393224 | tf_op jit(solution)/shard_map/ppermute | solution.py:330
